TPU v7x, 32 devices: a whole 2x2x4 slice. The times are simulated.
32 devices in a mesh: img: 8 (over z, y), seq: 4 (over x, core).
Axes of the slice: x: 2, y: 2, z: 4, core: 2. Of those that a mesh axis runs over, the one named last changes fastest.
Arguments:
- tokens: bfloat16 [24, 1056, 768], P('img', 'seq'), may hold values from -6 to 6
- cotangent: bfloat16 [24, 1056, 768], P('img', 'seq'), may hold values from -6 to 6
- images_held: int32 [8], P('img'), may hold values from 2 to 3, as said below
- piece_rows: int32 [4], replicated, may hold values from 260 to 264, as said below
- norm_gain: bfloat16 [768], P('img'), may hold values from 0.5 to 1.5
- norm_shift: bfloat16 [768], P('img'), may hold values from -4 to 4
- qkv_weight: bfloat16 [768, 2304], P('img'), may hold values from -0.21875 to 0.21875
- qkv_bias: bfloat16 [1536], P('img'), may hold values from -0.75 to 0.75
- out_weight: bfloat16 [768, 768], P('img'), may hold values from -6 to 6
- out_bias: bfloat16 [768], P('img'), may hold values from -4 to 4
- mlp_gain: bfloat16 [768], P('img'), may hold values from 0.5 to 1.5
- mlp_shift: bfloat16 [768], P('img'), may hold values from -4 to 4
- up_weight: bfloat16 [768, 3072], P('img'), may hold values from -0.21875 to 0.21875
- up_bias: bfloat16 [3072], P('img'), may hold values from -4 to 4
- down_weight: bfloat16 [3072, 768], P('img'), may hold values from -0.109375 to 0.109375
- down_bias: bfloat16 [768], P('img'), may hold values from -4 to 4
Outputs:
- layer_out: bfloat16 [24, 1056, 768], P('img', 'seq')
- tokens_grad: float32 [24, 1056, 768], P('img', 'seq')
- grad_norm_gain: float32 [768], P('img')
- grad_norm_shift: float32 [768], P('img')
- grad_qkv_weight: float32 [768, 2304], P('img')
- grad_qkv_bias: float32 [1536], P('img')
- grad_out_weight: float32 [768, 768], P('img')
- grad_out_bias: float32 [768], P('img')
- grad_mlp_gain: float32 [768], P('img')
- grad_mlp_shift: float32 [768], P('img')
- grad_up_weight: float32 [768, 3072], P('img')
- grad_up_bias: float32 [3072], P('img')
- grad_down_weight: float32 [3072, 768], P('img')
- grad_down_bias: float32 [768], P('img')
Inputs may be any that keep to these rules, and one draw needn't show every extreme that they name: `images_held`: every group holds 2 or 3 images; some group holds 3 and some group holds 2. `piece_rows`: one piece is full.
All inputs are finite; a program needn't handle non-finite values.
Results may differ from a plain program's by a relative error of at most 0.013.
Values may be sent and summed in bfloat16 or wider, within the bound.
No kernel may reach another device: no remote copies, remote signals or barrier semaphores. Data moves between devices by JAX's collectives and lax.ppermute only.
A program may use at most 192 MiB of HBM per device.

v0:
```python
from functools import partial

import jax
import jax.numpy as jnp
from jax import lax
from jax.sharding import PartitionSpec as P

D = 768
HEADS = 12
HEAD_DIM = 64


EPS = 1e-06
NEG = -1e30


def layer_norm(features, gain_vec, shift_vec):
    row_mean = jnp.mean(features, axis=-1, keepdims=True)
    centred = features - row_mean
    spread = jnp.mean(centred * centred, axis=-1, keepdims=True)
    return centred * lax.rsqrt(spread + EPS) * gain_vec + shift_vec


def full_bias(pair_bias):
    paired = pair_bias.astype(jnp.float32).reshape(HEADS, 2, HEAD_DIM)
    zero_keys = jnp.zeros((HEADS, 1, HEAD_DIM), jnp.float32)
    return jnp.concatenate([paired[:, :1], zero_keys, paired[:, 1:]], axis=1).reshape(3 * D)


def slot_scores(slot_block, key_valid, score_scale):
    queries = slot_block[:, :, 0]
    key_rows = slot_block[:, :, 1]
    scores = (
        jnp.einsum("qhd,khd->hqk", queries, key_rows, preferred_element_type=jnp.float32)
        * score_scale
    )
    return jnp.where(key_valid[None, None, :], scores, NEG)


def attend_forward(slot_block, key_valid, score_scale):
    values = slot_block[:, :, 2]
    scores = slot_scores(slot_block, key_valid, score_scale)
    row_peak = jnp.max(scores, axis=-1, keepdims=True)
    exp_terms = jnp.exp(scores - row_peak)
    row_total = jnp.sum(exp_terms, axis=-1, keepdims=True)
    attn_probs = (exp_terms / row_total).astype(jnp.bfloat16)
    attended = jnp.einsum("hqk,khd->qhd", attn_probs, values, preferred_element_type=jnp.float32)
    return (attended.astype(jnp.bfloat16), (row_peak + jnp.log(row_total))[..., 0])


def attend_backward(slot_items, key_valid, score_scale):
    slot_block, log_total, grad_attended = slot_items
    queries = slot_block[:, :, 0]
    key_rows = slot_block[:, :, 1]
    values = slot_block[:, :, 2]
    scores = slot_scores(slot_block, key_valid, score_scale)
    attn_probs = jnp.exp(scores - log_total[..., None])
    grad_probs = jnp.einsum(
        "qhd,khd->hqk", grad_attended, values, preferred_element_type=jnp.float32
    )
    inner_sum = jnp.sum(attn_probs * grad_probs, axis=-1, keepdims=True)
    grad_scores = (attn_probs * (grad_probs - inner_sum)).astype(jnp.bfloat16)
    grad_queries = (
        jnp.einsum("hqk,khd->qhd", grad_scores, key_rows, preferred_element_type=jnp.float32)
        * score_scale
    )
    grad_keys = (
        jnp.einsum("hqk,qhd->khd", grad_scores, queries, preferred_element_type=jnp.float32)
        * score_scale
    )
    grad_values = jnp.einsum(
        "hqk,qhd->khd",
        attn_probs.astype(jnp.bfloat16),
        grad_attended,
        preferred_element_type=jnp.float32,
    )
    return jnp.stack([grad_queries, grad_keys, grad_values], axis=2).astype(jnp.bfloat16)


def local(
    tokens,
    cotangent,
    images_held,
    piece_rows,
    norm_gain,
    norm_shift,
    qkv_weight,
    qkv_bias,
    out_weight,
    out_bias,
    mlp_gain,
    mlp_shift,
    up_weight,
    up_bias,
    down_weight,
    down_bias,
):
    slot_count, piece_size, model_width = tokens.shape
    seq_count = lax.axis_size("seq")
    seq_rows = seq_count * piece_size
    row_count = slot_count * piece_size
    heads_here = HEADS // seq_count
    score_scale = HEAD_DIM ** (-0.5)
    key_valid = (jnp.arange(piece_size)[None, :] < piece_rows[:, None]).reshape(seq_rows)
    own_valid = lax.dynamic_slice_in_dim(key_valid, lax.axis_index("seq") * piece_size, piece_size)
    live_slots = jnp.arange(slot_count) < images_held[0]
    valid_rows = (live_slots[:, None] & own_valid[None, :]).reshape(row_count)
    inputs = tokens.reshape(row_count, model_width).astype(jnp.float32)
    first_set = (
        lax.all_gather(norm_gain, "img", axis=0, tiled=True),
        lax.all_gather(norm_shift, "img", axis=0, tiled=True),
        lax.all_gather(qkv_weight, "img", axis=0, tiled=True),
        lax.all_gather(qkv_bias, "img", axis=0, tiled=True),
        lax.all_gather(out_weight, "img", axis=0, tiled=True),
        lax.all_gather(out_bias, "img", axis=0, tiled=True),
    )
    gain_first = first_set[0].astype(jnp.float32)
    shift_first = first_set[1].astype(jnp.float32)
    normed = layer_norm(inputs, gain_first, shift_first).astype(jnp.bfloat16)
    qkv_rows = (
        jnp.dot(normed, first_set[2], preferred_element_type=jnp.float32) + full_bias(first_set[3])
    ).astype(jnp.bfloat16)
    qkv_heads = lax.all_to_all(
        qkv_rows.reshape(slot_count, piece_size, seq_count, -1),
        "seq",
        split_axis=2,
        concat_axis=1,
        tiled=True,
    )
    qkv_heads = qkv_heads.reshape(slot_count, seq_rows, heads_here, 3, HEAD_DIM)
    attended, log_total = lax.map(
        partial(attend_forward, key_valid=key_valid, score_scale=score_scale), qkv_heads
    )
    attended_tokens = lax.all_to_all(
        attended.reshape(slot_count, seq_rows, 1, heads_here * HEAD_DIM),
        "seq",
        split_axis=1,
        concat_axis=2,
        tiled=True,
    )
    attended_tokens = attended_tokens.reshape(row_count, model_width)
    residual = (
        inputs
        + jnp.dot(attended_tokens, first_set[4], preferred_element_type=jnp.float32)
        + first_set[5].astype(jnp.float32)
    )
    second_set = (
        lax.all_gather(mlp_gain, "img", axis=0, tiled=True),
        lax.all_gather(mlp_shift, "img", axis=0, tiled=True),
        lax.all_gather(up_weight, "img", axis=0, tiled=True),
        lax.all_gather(up_bias, "img", axis=0, tiled=True),
        lax.all_gather(down_weight, "img", axis=0, tiled=True),
        lax.all_gather(down_bias, "img", axis=0, tiled=True),
    )
    gain_second = second_set[0].astype(jnp.float32)
    shift_second = second_set[1].astype(jnp.float32)
    normed_mlp = layer_norm(residual, gain_second, shift_second).astype(jnp.bfloat16)
    hidden_pre = jnp.dot(
        normed_mlp, second_set[2], preferred_element_type=jnp.float32
    ) + second_set[3].astype(jnp.float32)
    gelu_out, gelu_back = jax.vjp(partial(jax.nn.gelu, approximate=False), hidden_pre)
    activated = gelu_out.astype(jnp.bfloat16)
    output = (
        residual
        + jnp.dot(activated, second_set[4], preferred_element_type=jnp.float32)
        + second_set[5].astype(jnp.float32)
    )
    layer_out = (
        jnp.where(valid_rows[:, None], output, 0.0)
        .astype(jnp.bfloat16)
        .reshape(slot_count, piece_size, model_width)
    )
    mlp_back = (
        lax.all_gather(mlp_gain, "img", axis=0, tiled=True),
        lax.all_gather(mlp_shift, "img", axis=0, tiled=True),
        lax.all_gather(up_weight, "img", axis=0, tiled=True),
        lax.all_gather(down_weight, "img", axis=0, tiled=True),
    )
    grad_out = jnp.where(
        valid_rows[:, None], cotangent.reshape(row_count, model_width), jnp.zeros((), jnp.bfloat16)
    )
    grad_down_weight = jnp.einsum(
        "rf,rd->fd", activated, grad_out, preferred_element_type=jnp.float32
    )
    grad_down_bias = jnp.sum(grad_out.astype(jnp.float32), axis=0)
    grad_act = jnp.einsum("rd,fd->rf", grad_out, mlp_back[3], preferred_element_type=jnp.float32)
    grad_hidden = gelu_back(grad_act)[0].astype(jnp.bfloat16)
    grad_up_weight = jnp.einsum(
        "rd,rf->df", normed_mlp, grad_hidden, preferred_element_type=jnp.float32
    )
    grad_up_bias = jnp.sum(grad_hidden.astype(jnp.float32), axis=0)
    grad_norm_in = jnp.einsum(
        "rf,df->rd", grad_hidden, mlp_back[2], preferred_element_type=jnp.float32
    )
    second_norm, second_back = jax.vjp(
        layer_norm, residual, mlp_back[0].astype(jnp.float32), mlp_back[1].astype(jnp.float32)
    )
    grad_resid_norm, grad_mlp_gain, grad_mlp_shift = second_back(grad_norm_in)
    grad_residual = grad_out.astype(jnp.float32) + grad_resid_norm
    mlp_shares = (
        lax.psum_scatter(grad_mlp_gain, "img", scatter_dimension=0, tiled=True),
        lax.psum_scatter(grad_mlp_shift, "img", scatter_dimension=0, tiled=True),
        lax.psum_scatter(grad_up_weight, "img", scatter_dimension=0, tiled=True),
        lax.psum_scatter(grad_up_bias, "img", scatter_dimension=0, tiled=True),
        lax.psum_scatter(grad_down_weight, "img", scatter_dimension=0, tiled=True),
        lax.psum_scatter(grad_down_bias, "img", scatter_dimension=0, tiled=True),
    )
    attn_back = (
        lax.all_gather(norm_gain, "img", axis=0, tiled=True),
        lax.all_gather(norm_shift, "img", axis=0, tiled=True),
        lax.all_gather(qkv_weight, "img", axis=0, tiled=True),
        lax.all_gather(out_weight, "img", axis=0, tiled=True),
    )
    grad_branch = grad_residual.astype(jnp.bfloat16)
    grad_out_weight = jnp.einsum(
        "rd,re->de", attended_tokens, grad_branch, preferred_element_type=jnp.float32
    )
    grad_out_bias = jnp.sum(grad_branch.astype(jnp.float32), axis=0)
    grad_attended = jnp.einsum(
        "re,de->rd", grad_branch, attn_back[3], preferred_element_type=jnp.float32
    ).astype(jnp.bfloat16)
    grad_heads = lax.all_to_all(
        grad_attended.reshape(slot_count, piece_size, seq_count, -1),
        "seq",
        split_axis=2,
        concat_axis=1,
        tiled=True,
    )
    grad_heads = grad_heads.reshape(slot_count, seq_rows, heads_here, HEAD_DIM)
    grad_qkv_heads = lax.map(
        partial(attend_backward, key_valid=key_valid, score_scale=score_scale),
        (qkv_heads, log_total, grad_heads),
    )
    grad_qkv = lax.all_to_all(
        grad_qkv_heads.reshape(slot_count, seq_rows, 1, -1),
        "seq",
        split_axis=1,
        concat_axis=2,
        tiled=True,
    )
    grad_qkv = grad_qkv.reshape(row_count, 3 * model_width)
    grad_qkv_weight = jnp.einsum("rd,re->de", normed, grad_qkv, preferred_element_type=jnp.float32)
    bias_sums = jnp.sum(grad_qkv.astype(jnp.float32), axis=0).reshape(HEADS, 3, HEAD_DIM)
    grad_qkv_bias = jnp.concatenate([bias_sums[:, :1], bias_sums[:, 2:]], axis=1).reshape(
        2 * model_width
    )
    grad_norm_first = jnp.einsum(
        "re,de->rd", grad_qkv, attn_back[2], preferred_element_type=jnp.float32
    )
    first_norm, first_back = jax.vjp(
        layer_norm, inputs, attn_back[0].astype(jnp.float32), attn_back[1].astype(jnp.float32)
    )
    grad_inputs_norm, grad_norm_gain, grad_norm_shift = first_back(grad_norm_first)
    tokens_grad = (grad_residual + grad_inputs_norm).reshape(slot_count, piece_size, model_width)
    attn_shares = (
        lax.psum_scatter(grad_norm_gain, "img", scatter_dimension=0, tiled=True),
        lax.psum_scatter(grad_norm_shift, "img", scatter_dimension=0, tiled=True),
        lax.psum_scatter(grad_qkv_weight, "img", scatter_dimension=0, tiled=True),
        lax.psum_scatter(grad_qkv_bias, "img", scatter_dimension=0, tiled=True),
        lax.psum_scatter(grad_out_weight, "img", scatter_dimension=0, tiled=True),
        lax.psum_scatter(grad_out_bias, "img", scatter_dimension=0, tiled=True),
    )
    summed = (
        lax.psum(attn_shares[0].astype(jnp.bfloat16), "seq").astype(jnp.float32),
        lax.psum(attn_shares[1].astype(jnp.bfloat16), "seq").astype(jnp.float32),
        lax.psum(attn_shares[2].astype(jnp.bfloat16), "seq").astype(jnp.float32),
        lax.psum(attn_shares[3].astype(jnp.bfloat16), "seq").astype(jnp.float32),
        lax.psum(attn_shares[4].astype(jnp.bfloat16), "seq").astype(jnp.float32),
        lax.psum(attn_shares[5].astype(jnp.bfloat16), "seq").astype(jnp.float32),
        lax.psum(mlp_shares[0].astype(jnp.bfloat16), "seq").astype(jnp.float32),
        lax.psum(mlp_shares[1].astype(jnp.bfloat16), "seq").astype(jnp.float32),
        lax.psum(mlp_shares[2].astype(jnp.bfloat16), "seq").astype(jnp.float32),
        lax.psum(mlp_shares[3].astype(jnp.bfloat16), "seq").astype(jnp.float32),
        lax.psum(mlp_shares[4].astype(jnp.bfloat16), "seq").astype(jnp.float32),
        lax.psum(mlp_shares[5].astype(jnp.bfloat16), "seq").astype(jnp.float32),
    )
    return (
        layer_out,
        tokens_grad,
        summed[0],
        summed[1],
        summed[2],
        summed[3],
        summed[4],
        summed[5],
        summed[6],
        summed[7],
        summed[8],
        summed[9],
        summed[10],
        summed[11],
    )


def solution(mesh):
    placed = (
        P("img", "seq", None),
        P("img", "seq", None),
        P("img"),
        P(),
        P("img"),
        P("img"),
        P("img", None),
        P("img"),
        P("img", None),
        P("img"),
        P("img"),
        P("img"),
        P("img", None),
        P("img"),
        P("img", None),
        P("img"),
    )
    return jax.shard_map(
        local,
        mesh=mesh,
        in_specs=placed,
        out_specs=(
            P("img", "seq", None),
            P("img", "seq", None),
            P("img"),
            P("img"),
            P("img", None),
            P("img"),
            P("img", None),
            P("img"),
            P("img"),
            P("img"),
            P("img", None),
            P("img"),
            P("img", None),
            P("img"),
        ),
        check_vma=False,
    )
```

profile of v0, /device:TPU:0, one launch (start us, length us, event | category | flops | bytes accessed | tf_op | source)
XLA Modules:
  0.0 1106.6 jit_solution(14994718269147157189)
XLA Ops:
  17.9 40.3 %all-reduce.16 = (bf16[1536]{0:T(1024)(128)(2,1)S(1)}, bf16[768]{0:T(1024)(128)(2,1)S(1)}, bf16[768]{0:T(1024)(128)(2,1)S(1)}, bf16[768]{0:T(1024)(128)(2,1)}, b...) all-reduce(bf16[1536]{0:T(1024)(128)(2,1)S(1)} %dynamic-update-slic, ...), channel_id=1, replica_groups=mesh['img'=8,'seq'=4] {'img'}, use_global_device_ids=true, to_apply=%add.2 | all-reduce | flops 6144 | bytes 24576
  63.8 14.7 %all-gather.6.cloned.1.call-done = bf16[768,2304]{1,0:T(8,128)(2,1)} async-done(((bf16[96,2304]{1,0:T(8,128)(2,1)}), bf16[768,2304]{1,0:T(8,128)(2,1)}) %all-gather.6.cloned.1.call-update) | async-done | bytes 3538960 | tf_op jit(solution)/shard_map/all_gather | solution.py:112
  86.3 9.3 reshape.297
  105.6 46.1 %all-to-all-done = bf16[3,264,4,576]{3,1,0,2:T(8,128)(2,1)} async-done(((bf16[3,264,4,576]{3,1,0,2:T(8,128)(2,1)}), bf16[3,264,4,576]{3,1,0,2:T(8,128)(2,1)}, u32[]{:S(2)}, u32[]{:S(2)}) %all-to-all-start) | async-done | bytes 3649568 | tf_op jit(solution)/shard_map/all_to_all | solution.py:123
  151.7 11.3 %copy.66 = bf16[3,4,264,1,576]{2,1,4,0,3:T(4,128)(2,1)} copy(bf16[3,4,264,1,576]{4,2,0,1,3:T(8,128)(2,1)} %bitcast.5) | data formatting | bytes 7299072 | tf_op jit(solution)/shard_map/all_to_all | solution.py:123
  163.0 9.3 reshape.298
  176.7 75.5 %while.24 = (s32[]{:T(128)}, bf16[3,1056,3,64]{1,3,2,0:T(8,128)(2,1)S(1)}, f32[3,3,1056]{2,1,0:T(4,128)}, bf16[3,1056,3,3,64]{1,4,2,3,0:T(8,128)(2,1)}, s32[4]{0:T(128)S(1)}, /*index=5*/s32[]{:T(128)}) while((s32[]{:T(128)}, bf16[3,1056,3,64]{1,3,2,0:T(8,128)(2,1)S(1)}, f32[3,3,1056]{2,1,0:T(4,128)}, ...), condition=%wide.region_5.6_spmd.clone, body=%wide.region_2.5_spmd.clone.sunk | while | flops 883388416 | bytes 44471368 | solution.py:131
  203.2 8.0 fusion.98
  260.9 26.1 %all-gather = bf16[8,1,384]{2,1,0:T(2,128)(2,1)S(1)} all-gather(bf16[1,1,384]{2,1,0:T(2,128)(2,1)S(1)} %reshape.334), channel_id=1, replica_groups=mesh['img'=8,'seq'=4] {'img'}, dimensions={0}, use_global_device_ids=true | all-gather | bytes 6912 | tf_op jit(solution)/shard_map/all_gather | solution.py:151
  296.3 9.0 fusion.51
  305.5 32.1 %convert_reduce_fusion = (f32[3072]{0:T(1024)}, bf16[792,3072]{1,0:T(8,128)(2,1)S(1)}, f32[792,3072]{1,0:T(8,128)}) fusion(f32[792,3072]{1,0:T(8,128)} %fusion.51, f32[3072]{0:T(1024)S(1)} %bitcast.175, bf16[792,768]{1,0:T(8,128)(2,1)} %bitcast_select_fusion, bf16[3072,768]{1,0:T(8,128)(2,1)} %all-gather.12.cloned.1.call-done), kind=kOutput, calls=%fused_computation.50 | convolution fusion | flops 3919598592 | bytes 30289920 | tf_op jit(solution)/shard_map/rd,fd->rf/dot_general | solution.py:186
  358.1 16.4 %all-to-all-done.2 = bf16[3,264,4,192]{3,1,0,2:T(8,128)(2,1)S(1)} async-done(((bf16[3,264,4,192]{3,1,0,2:T(8,128)(2,1)}), bf16[3,264,4,192]{3,1,0,2:T(8,128)(2,1)S(1)}, u32[]{:S(2)}, u32[]{:S(2)}) %all-to-all-start.2) | async-done | bytes 1216544 | tf_op jit(solution)/shard_map/all_to_all | solution.py:222
  380.9 95.5 %while.25 = (s32[]{:T(128)}, bf16[3,1056,3,3,64]{1,4,3,2,0:T(8,128)(2,1)}, bf16[3,1056,3,3,64]{1,4,2,3,0:T(8,128)(2,1)}, f32[3,3,1056]{2,1,0:T(4,128)}, bf16[3,1...) while((s32[]{:T(128)}, bf16[3,1056,3,3,64]{1,4,3,2,0:T(8,128)(2,1)}, ...), condition=%wide.region_12.13_spmd.clone, body=%wide.region_10.12_spmd.clone.sunk | while | flops 2173398016 | bytes 123108104 | solution.py:230
  385.4 8.0 multiply_reduce_fusion.7
  476.5 11.2 %copy.75 = bf16[3,1056,1,576]{3,0,2,1:T(4,128)(2,1)} copy(bf16[3,1056,1,576]{1,3,0,2:T(8,128)(2,1)} %bitcast.172) | data formatting | bytes 7299072 | tf_op jit(solution)/shard_map/reshape | solution.py:235
  493.7 60.4 %all-to-all-done.3 = bf16[3,1056,1,576]{3,0,2,1:T(4,128)(2,1)} async-done(((bf16[3,1056,1,576]{3,0,2,1:T(4,128)(2,1)}), bf16[3,1056,1,576]{3,0,2,1:T(4,128)(2,1)}, u32[]{:S(2)}, u32[]{:S(2)}) %all-to-all-start.3) | async-done | bytes 3649568 | tf_op jit(solution)/shard_map/all_to_all | solution.py:234
  580.2 10.3 fusion.50
  591.2 11.3 %multiply_convert_fusion.1 = bf16[792,3072]{1,0:T(8,128)(2,1)} fusion(f32[792,3072]{1,0:T(8,128)} %get-tuple-element.195, f32[792,3072]{1,0:T(8,128)} %fusion.51, f32[3072]{0:T(1024)S(1)} %bitcast.176), kind=kLoop, calls=%fused_computation.52 | loop fusion | flops 9732096 | bytes 24342528 | tf_op jit(solution)/shard_map/convert_element_type | solution.py:162
  602.5 9.6 fusion.62
  616.1 9.0 select_convert_fusion
  637.5 66.8 %reduce-scatter.5.cloned.1.call-done = f32[96,2304]{1,0:T(8,128)} async-done(((f32[768,2304]{1,0:T(8,128)}), f32[96,2304]{1,0:T(8,128)}) %reduce-scatter.5.cloned.1.call-update) | async-done | bytes 884752 | tf_op jit(solution)/shard_map/reduce_scatter | solution.py:258
  706.3 164.6 %reduce-scatter.9.cloned.1.call-done = f32[96,3072]{1,0:T(8,128)} async-done(((f32[768,3072]{1,0:T(8,128)}), f32[96,3072]{1,0:T(8,128)}) %reduce-scatter.9.cloned.1.call-update) | async-done | bytes 1179664 | tf_op jit(solution)/shard_map/reduce_scatter | solution.py:203
  873.1 164.3 %reduce-scatter.11.cloned.1.call-done = f32[384,768]{1,0:T(8,128)} async-done(((f32[3072,768]{1,0:T(8,128)}), f32[384,768]{1,0:T(8,128)}) %reduce-scatter.11.cloned.1.call-update) | async-done | bytes 1179664 | tf_op jit(solution)/shard_map/reduce_scatter | solution.py:205
  1041.8 35.6 %all-reduce.15 = (bf16[768]{0:T(1024)(128)(2,1)S(1)}, bf16[768]{0:T(1024)(128)(2,1)S(1)}, bf16[1536]{0:T(1024)(128)(2,1)S(1)}, bf16[768]{0:T(1024)(128)(2,1)S(1)...) all-reduce(f32[768]{0:T(1024)S(1)} %get-tuple-element.143, ...), channel_id=2, replica_groups=mesh['img'=8,'seq'=4] {'img'}, use_global_device_ids=true, to_apply=%region_16.17.clone | all-reduce | flops 9216 | bytes 55296
  (339 shorter events, 313.4 us)
Async XLA Ops:
  7.2 52.7 %copy-start.5 = (bf16[3,264,768]{2,1,0:T(8,128)(2,1)S(1)}, bf16[3,264,768]{2,1,0:T(8,128)(2,1)}, u32[]{:S(2)}) copy-start(bf16[3,264,768]{2,1,0:T(8,128)(2,1)} %param.20) | copy-start | bytes 3649540
  7.2 71.4 %all-gather.6.cloned.1.call-start = ((), (), s32[]{:S(2)}) async-start(), calls=%async_computation.8 | async-start | bytes 3981312 | tf_op jit(solution)/shard_map/all_gather | solution.py:112
  7.9 283.8 %all-gather.8.cloned.1.call-start = ((), (), s32[]{:S(2)}) async-start(), calls=%async_computation.9 | async-start | bytes 1327104 | tf_op jit(solution)/shard_map/all_gather | solution.py:114
  8.7 287.0 %all-gather.10.cloned.1.call-start = ((), (), s32[]{:S(2)}) async-start(), calls=%async_computation.10 | async-start | bytes 5308416 | tf_op jit(solution)/shard_map/all_gather | solution.py:150
  100.2 51.5 %all-to-all-start = ((bf16[3,264,4,576]{3,1,0,2:T(8,128)(2,1)}), bf16[3,264,4,576]{3,1,0,2:T(8,128)(2,1)}, u32[]{:S(2)}, u32[]{:S(2)}) async-start(bf16[3,264,4,576]{3,1,0,2:T(8,128)(2,1)} %copy.65), calls=%async_computation | async-start | bytes 8110080 | tf_op jit(solution)/shard_map/all_to_all | solution.py:123
  105.0 200.4 %all-gather.12.cloned.1.call-start = ((), (), s32[]{:S(2)}) async-start(), calls=%async_computation.11 | async-start | bytes 5308416 | tf_op jit(solution)/shard_map/all_gather | solution.py:152
  255.4 32.9 %all-to-all-start.1 = ((bf16[3,1056,1,192]{3,0,2,1:T(4,128)(2,1)}), bf16[3,1056,1,192]{3,0,2,1:T(4,128)(2,1)S(1)}, u32[]{:S(2)}, u32[]{:S(2)}) async-start(bf16[3,1056,1,192]{3,0,2,1:T(4,128)(2,1)} %copy.68), calls=%async_computation.1 | async-start | bytes 4325376 | tf_op jit(solution)/shard_map/all_to_all | solution.py:134
  260.8 34.9 %copy-start.19 = (f32[768]{0:T(1024)}, f32[768]{0:T(1024)S(1)}, u32[]{:S(2)}) copy-start(f32[768]{0:T(1024)S(1)} %convert_element_type.183) | copy-start | bytes 9220
  260.8 34.9 %copy-start.25 = (f32[768]{0:T(1024)}, f32[768]{0:T(1024)S(1)}, u32[]{:S(2)}) copy-start(f32[768]{0:T(1024)S(1)} %convert_element_type.184) | copy-start | bytes 9220
  260.9 34.9 %copy-start.31 = (f32[768]{0:T(1024)}, f32[768]{0:T(1024)S(1)}, u32[]{:S(2)}) copy-start(f32[768]{0:T(1024)S(1)} %convert_element_type.185) | copy-start | bytes 9220
  305.4 32.1 %copy-start.1 = (f32[792,768]{1,0:T(8,128)S(1)}, f32[792,768]{1,0:T(8,128)}, u32[]{:S(2)}) copy-start(f32[792,768]{1,0:T(8,128)} %copy-done) | copy-start | bytes 7299076
  305.4 32.1 %copy-start.20 = (f32[768]{0:T(1024)S(1)}, f32[768]{0:T(1024)}, u32[]{:S(2)}) copy-start(f32[768]{0:T(1024)} %copy-done.19) | copy-start | bytes 9220
  305.4 32.1 %copy-start.23 = (f32[792]{0:T(1024)S(1)}, f32[792]{0:T(1024)}, u32[]{:S(2)}) copy-start(f32[792]{0:T(1024)} %copy-done.22) | copy-start | bytes 9508
  305.4 32.1 %copy-start.26 = (f32[768]{0:T(1024)S(1)}, f32[768]{0:T(1024)}, u32[]{:S(2)}) copy-start(f32[768]{0:T(1024)} %copy-done.25) | copy-start | bytes 9220
  305.4 32.1 %copy-start.29 = (f32[792]{0:T(1024)S(1)}, f32[792]{0:T(1024)}, u32[]{:S(2)}) copy-start(f32[792]{0:T(1024)} %copy-done.28) | copy-start | bytes 9508
  350.2 24.3 %all-to-all-start.2 = ((bf16[3,264,4,192]{3,1,0,2:T(8,128)(2,1)}), bf16[3,264,4,192]{3,1,0,2:T(8,128)(2,1)S(1)}, u32[]{:S(2)}, u32[]{:S(2)}) async-start(bf16[3,264,4,192]{3,1,0,2:T(8,128)(2,1)} %copy.71), calls=%async_computation.2 | async-start | bytes 3244032 | tf_op jit(solution)/shard_map/all_to_all | solution.py:222
  353.9 282.0 %reduce-scatter.7.cloned.1.call-start = ((), (), s32[]{:S(2)}) async-start(), calls=%async_computation.13 | async-start | bytes 2654208 | tf_op jit(solution)/shard_map/reduce_scatter | solution.py:260
  487.7 66.4 %all-to-all-start.3 = ((bf16[3,1056,1,576]{3,0,2,1:T(4,128)(2,1)}), bf16[3,1056,1,576]{3,0,2,1:T(4,128)(2,1)}, u32[]{:S(2)}, u32[]{:S(2)}) async-start(bf16[3,1056,1,576]{3,0,2,1:T(4,128)(2,1)} %copy.75), calls=%async_computation.3 | async-start | bytes 10813440 | tf_op jit(solution)/shard_map/all_to_all | solution.py:234
  492.9 211.5 %reduce-scatter.5.cloned.1.call-start = ((), (), s32[]{:S(2)}) async-start(), calls=%async_computation.12 | async-start | bytes 7962624 | tf_op jit(solution)/shard_map/reduce_scatter | solution.py:258
  578.5 292.4 %reduce-scatter.9.cloned.1.call-start = ((), (), s32[]{:S(2)}) async-start(), calls=%async_computation.14 | async-start | bytes 10616832 | tf_op jit(solution)/shard_map/reduce_scatter | solution.py:203
  590.5 446.9 %reduce-scatter.11.cloned.1.call-start = ((), (), s32[]{:S(2)}) async-start(), calls=%async_computation.15 | async-start | bytes 10616832 | tf_op jit(solution)/shard_map/reduce_scatter | solution.py:205
  612.1 480.5 %all-reduce.21.cloned.1.call-start = ((), (), s32[]{:S(2)}) async-start(), calls=%async_computation.16 | async-start | bytes 3538944 | tf_op jit(solution)/shard_map/psum | solution.py:266
  1039.5 49.1 %copy-start.11 = (f32[792,768]{1,0:T(8,128)S(1)}, f32[792,768]{1,0:T(8,128)}, u32[]{:S(2)}) copy-start(f32[792,768]{1,0:T(8,128)} %copy-done.10) | copy-start | bytes 7299076
  1039.5 49.1 %copy-start.48 = (f32[792]{0:T(1024)S(1)}, f32[792]{0:T(1024)}, u32[]{:S(2)}) copy-start(f32[792]{0:T(1024)} %copy-done.47) | copy-start | bytes 9508
  (63 other events, 372.5 us)
Sparse Core Ops, SparseCore 0:
  10.2 68.3 all-gather.5
  80.8 39.6 all-gather.7
  122.6 78.6 all-gather.9
  203.4 78.0 all-gather.11
  358.2 67.0 reduce-scatter.6
  578.6 125.6 reduce-scatter.4
  708.4 162.4 reduce-scatter.8
  874.9 162.3 reduce-scatter.10
  1041.3 45.9 all-reduce.20
where the time goes:
time: 1120 us; the launch traced here: 1110 us
  waiting for transfers between devices  536 us (48%)
  matrix products  217 us (19%)
  local copies, waits for them, and re-layouts  110 us (10%)
  blocking collectives  108 us (10%)
  other arithmetic  97.5 us (9%)
  between operations  19 us (2%)
  starting transfers between devices  18.5 us (2%)
    reduce_scatter x1, waiting for transfers between devices, local(): lax.psum_scatter(grad_up_weight, 'img', scatter_dimension=0, tiled=True)  165 us
    reduce_scatter x1, waiting for transfers between devices, local(): lax.psum_scatter(grad_down_weight, 'img', scatter_dimension=0, tiled=True)  164 us
    unnamed x2, blocking collectives  75.9 us
    reduce_scatter x1, waiting for transfers between devices, local(): lax.psum_scatter(grad_qkv_weight, 'img', scatter_dimension=0, tiled=True)  66.8 us
    all_to_all x1, waiting for transfers between devices, local(): lax.all_to_all(grad_qkv_heads.reshape(slot_count, seq_rows, 1, -1), 'seq'...  60.4 us
    dot_general x6, matrix products, slot_scores(): jnp.einsum('qhd,khd->hqk', queries, key_rows, preferred_element_type=jnp....  47.7 us
    all_to_all x1, waiting for transfers between devices, local(): lax.all_to_all(qkv_rows.reshape(slot_count, piece_size, seq_count, -1), '...  46.1 us
    dot_general x1, matrix products, local(): jnp.einsum('rd,fd->rf', grad_out, mlp_back[3], preferred_element_type=jnp...  32.1 us
  transfers between devices with their start and end apart: 13, of which 7 were waited for; matrix products, arithmetic and copies ran while one was open for 33% of the time, Pallas kernels for 0%

commit v1 on v0

v1 whole, which is shorter than its diff:
```python
from functools import partial

import jax
import jax.numpy as jnp
from jax import lax
from jax.sharding import PartitionSpec as P

D = 768
HEADS = 12
HEAD_DIM = 64


EPS = 1e-06
NEG = -1e30


def layer_norm(features, gain_vec, shift_vec):
    row_mean = jnp.mean(features, axis=-1, keepdims=True)
    centred = features - row_mean
    spread = jnp.mean(centred * centred, axis=-1, keepdims=True)
    return centred * lax.rsqrt(spread + EPS) * gain_vec + shift_vec

def xor_send(block, axis, bits):
    n = lax.axis_size(axis)
    return lax.ppermute(block, axis, [(i, i ^ bits) for i in range(n)])


def img_shape():
    n = lax.axis_size("img")
    return n // 2, 2


def ring_perm():
    outer, inner = img_shape()
    return [
        (z * inner + y, ((z + 1) % outer) * inner + y) for z in range(outer) for y in range(inner)
    ]


def small_axis():
    return lax.axis_size("img") <= 16


def pair_up(block, bits):
    other = xor_send(block, "img", bits)
    first = (lax.axis_index("img") & bits) == 0
    return jnp.where(first, jnp.stack([block, other]), jnp.stack([other, block]))


def ring_gather(block):
    outer, inner = img_shape()
    z = lax.axis_index("img") // inner
    gathered = jnp.zeros((outer,) + block.shape, block.dtype)
    moving = block
    for step in range(outer):
        owner = (z + outer - step) % outer
        gathered = lax.dynamic_update_slice_in_dim(gathered, moving[None], owner, 0)
        if step < outer - 1:
            moving = lax.ppermute(moving, "img", ring_perm())
    return gathered


def gather_img(block, inner_first=True):
    n = lax.axis_size("img")
    if not small_axis():
        return lax.all_gather(block, "img", axis=0)
    if inner_first:
        return ring_gather(pair_up(block, 1)).reshape((n,) + block.shape)
    both = pair_up(ring_gather(block), 1)
    return jnp.swapaxes(both, 0, 1).reshape((n,) + block.shape)


def ring_reduce(parts):
    outer, inner = img_shape()
    z = lax.axis_index("img") // inner

    def part(step):
        return lax.dynamic_index_in_dim(parts, (z + 2 * outer - step) % outer, 0, keepdims=False)

    total = part(1)
    for step in range(1, outer):
        arrived = lax.ppermute(total.astype(jnp.bfloat16), "img", ring_perm())
        total = arrived.astype(jnp.float32) + part(step + 1).astype(jnp.float32)
    return total


def pair_reduce(parts):
    me = lax.axis_index("img") & 1
    keep = lax.dynamic_index_in_dim(parts, me, 0, keepdims=False)
    send = lax.dynamic_index_in_dim(parts, 1 - me, 0, keepdims=False)
    arrived = xor_send(send.astype(jnp.bfloat16), "img", 1)
    return keep.astype(jnp.float32) + arrived.astype(jnp.float32)


def reduce_img(parts, inner_first=True):
    if not small_axis():
        return lax.psum_scatter(
            parts.astype(jnp.bfloat16), "img", scatter_dimension=0, tiled=False
        ).astype(jnp.float32)
    outer, inner = img_shape()
    split = parts.reshape((outer, inner) + parts.shape[1:])
    if inner_first:
        return ring_reduce(pair_reduce(jnp.swapaxes(split, 0, 1)))
    return pair_reduce(ring_reduce(split))


def all_sum(vector):
    axes = (("seq", 1), ("seq", 2)) + tuple(
        ("img", 1 << k) for k in range(lax.axis_size("img").bit_length() - 1)
    )
    for axis, bits in axes:
        vector = vector + xor_send(vector, axis, bits)
    return vector


def halves(mine, axis):
    first = (lax.axis_index("seq") & 1) == 0
    other = xor_send(mine, "seq", 1)
    return jnp.where(
        first,
        jnp.concatenate([mine, other], axis),
        jnp.concatenate([other, mine], axis),
    )


def half_of(block, axis, which):
    size = block.shape[axis] // 2
    return lax.dynamic_slice_in_dim(block, which * size, size, axis)


def finish_halves(total, axis):
    low = total.astype(jnp.bfloat16)
    low = (low.astype(jnp.float32) + xor_send(low, "seq", 2).astype(jnp.float32)).astype(
        jnp.bfloat16
    )
    return halves(low, axis).astype(jnp.float32)


def half_reduce(grad, axis):
    me = lax.axis_index("seq") & 1
    arrived = xor_send(half_of(grad, axis, 1 - me).astype(jnp.bfloat16), "seq", 1)
    return half_of(grad, axis, me).astype(jnp.float32) + arrived.astype(jnp.float32)


def attend_forward(qkv_rows, key_valid, score_scale):
    heads_here = qkv_rows.shape[1] // (3 * HEAD_DIM)
    cols = qkv_rows.reshape(-1, heads_here, 3, HEAD_DIM)
    scores = (
        jnp.einsum("qhd,khd->hqk", cols[:, :, 0], cols[:, :, 1], preferred_element_type=jnp.float32)
        * score_scale
    )
    scores = jnp.where(key_valid[None, None, :], scores, NEG)
    probs = jax.nn.softmax(scores, axis=-1).astype(jnp.bfloat16)
    attended = jnp.einsum("hqk,khd->qhd", probs, cols[:, :, 2], preferred_element_type=jnp.float32)
    return attended.astype(jnp.bfloat16).reshape(qkv_rows.shape[0], -1)


def attend_backward(qkv_rows, grad_attended, key_valid, score_scale):
    heads_here = qkv_rows.shape[1] // (3 * HEAD_DIM)
    cols = qkv_rows.reshape(-1, heads_here, 3, HEAD_DIM)
    grads = grad_attended.reshape(-1, heads_here, HEAD_DIM)
    scores = (
        jnp.einsum("qhd,khd->hqk", cols[:, :, 0], cols[:, :, 1], preferred_element_type=jnp.float32)
        * score_scale
    )
    scores = jnp.where(key_valid[None, None, :], scores, NEG)
    probs = jax.nn.softmax(scores, axis=-1)
    grad_probs = jnp.einsum("qhd,khd->hqk", grads, cols[:, :, 2], preferred_element_type=jnp.float32)
    inner = jnp.sum(probs * grad_probs, axis=-1, keepdims=True)
    grad_scores = (probs * (grad_probs - inner)).astype(jnp.bfloat16)
    grad_q = score_scale * jnp.einsum(
        "hqk,khd->qhd", grad_scores, cols[:, :, 1], preferred_element_type=jnp.float32
    )
    grad_k = score_scale * jnp.einsum(
        "hqk,qhd->khd", grad_scores, cols[:, :, 0], preferred_element_type=jnp.float32
    )
    grad_v = jnp.einsum(
        "hqk,qhd->khd", probs.astype(jnp.bfloat16), grads, preferred_element_type=jnp.float32
    )
    return jnp.stack([grad_q, grad_k, grad_v], axis=2).astype(jnp.bfloat16).reshape(qkv_rows.shape)


def local(
    tokens,
    cotangent,
    images_held,
    piece_rows,
    norm_gain,
    norm_shift,
    qkv_weight,
    qkv_bias,
    out_weight,
    out_bias,
    mlp_gain,
    mlp_shift,
    up_weight,
    up_bias,
    down_weight,
    down_bias,
):
    slot_count, piece_size, model_width = tokens.shape
    n_seq = lax.axis_size("seq")
    n_img = lax.axis_size("img")
    me = lax.axis_index("seq")
    own_img = lax.axis_index("img")
    row_count = slot_count * piece_size
    heads_here = HEADS // n_seq
    group = 3 * D // n_seq
    shard = D // n_img
    score_scale = HEAD_DIM ** (-0.5)

    pieces = me ^ jnp.arange(n_seq)
    rows_of = piece_rows[pieces]
    key_valid = (jnp.arange(piece_size)[None, :] < rows_of[:, None]).reshape(n_seq * piece_size)
    own_valid = key_valid[:piece_size]
    live_slots = jnp.arange(slot_count) < images_held[0]
    valid_rows = (live_slots[:, None] & own_valid[None, :]).reshape(row_count)

    slot_tokens = []
    for slot in range(slot_count):
        own = tokens[slot]
        pair = xor_send(own, "seq", 1)
        across = xor_send(own, "seq", 2)
        slot_tokens.append([own, pair, across, xor_send(across, "seq", 1)])
    small = jnp.concatenate(
        [norm_gain, norm_shift, out_bias, mlp_gain, mlp_shift, down_bias, qkv_bias, up_bias]
    )
    small_rows = -(-small.shape[0] // group)
    small_rows = -(-small_rows // 16) * 16
    small = jnp.pad(small, (0, small_rows * group - small.shape[0])).reshape(small_rows, group)
    my_columns = lax.dynamic_slice_in_dim(qkv_weight, me * group, group, 1)
    first_set = gather_img(jnp.concatenate([my_columns, small], axis=0))
    qkv_cols = first_set[:, :shard].reshape(model_width, group)
    params = first_set[:, shard:].reshape(n_img, -1).astype(jnp.float32)

    def param(start, width):
        return params[:, start * shard : (start + width) * shard].reshape(-1)

    gain_first, shift_first, bias_out = param(0, 1), param(1, 1), param(2, 1)
    gain_second, shift_second, bias_down = param(3, 1), param(4, 1), param(5, 1)
    pair_bias, bias_up = param(6, 2), param(8, 4)
    paired = lax.dynamic_slice_in_dim(
        pair_bias.reshape(HEADS, 2, HEAD_DIM), me * heads_here, heads_here, 0
    )
    bias_qkv = jnp.concatenate(
        [paired[:, :1], jnp.zeros((heads_here, 1, HEAD_DIM), jnp.float32), paired[:, 1:]], axis=1
    ).reshape(group)

    pair_me = me & 1
    half_up = gather_img(
        jnp.concatenate([half_of(up_weight, 1, pair_me), half_of(out_weight, 1, pair_me)], axis=1),
        inner_first=False,
    ).reshape(model_width, -1)
    half_down = gather_img(half_of(down_weight, 1, pair_me)).reshape(-1, model_width // 2)
    ff = up_weight.shape[1]
    up_full = halves(half_up[:, : ff // 2], 1)
    out_full = halves(half_up[:, ff // 2 :], 1)
    down_full = halves(half_down, 1)

    inputs = tokens.reshape(row_count, model_width).astype(jnp.float32)
    slot_normed, slot_qkv, slot_attended = [], [], []
    for slot in range(slot_count):
        rows = jnp.concatenate(slot_tokens[slot], axis=0).astype(jnp.float32)
        normed = layer_norm(rows, gain_first, shift_first).astype(jnp.bfloat16)
        qkv_rows = (
            jnp.dot(normed, qkv_cols, preferred_element_type=jnp.float32) + bias_qkv
        ).astype(jnp.bfloat16)
        attended = attend_forward(qkv_rows, key_valid, score_scale).reshape(
            n_seq, piece_size, -1
        )
        slot_normed.append(normed)
        slot_qkv.append(qkv_rows)
        slot_attended.append(
            [attended[0]] + [xor_send(attended[r], "seq", r) for r in range(1, n_seq)]
        )

    group_width = heads_here * HEAD_DIM
    out_rel = [
        lax.dynamic_slice_in_dim(out_full, (me ^ r) * group_width, group_width, 0)
        for r in range(n_seq)
    ]
    out_rel = jnp.concatenate(out_rel, axis=0)
    attended_tokens = jnp.concatenate(
        [jnp.concatenate(parts, axis=1) for parts in slot_attended], axis=0
    )
    residual = (
        inputs + jnp.dot(attended_tokens, out_rel, preferred_element_type=jnp.float32) + bias_out
    )

    normed_mlp = layer_norm(residual, gain_second, shift_second).astype(jnp.bfloat16)
    hidden_pre = jnp.dot(normed_mlp, up_full, preferred_element_type=jnp.float32) + bias_up
    gelu_out, gelu_back = jax.vjp(partial(jax.nn.gelu, approximate=False), hidden_pre)
    activated = gelu_out.astype(jnp.bfloat16)
    output = residual + jnp.dot(activated, down_full, preferred_element_type=jnp.float32) + bias_down
    layer_out = (
        jnp.where(valid_rows[:, None], output, 0.0)
        .astype(jnp.bfloat16)
        .reshape(slot_count, piece_size, model_width)
    )
    grad_out = jnp.where(
        valid_rows[:, None], cotangent.reshape(row_count, model_width), jnp.zeros((), jnp.bfloat16)
    )
    grad_act = jnp.einsum("rd,fd->rf", grad_out, down_full, preferred_element_type=jnp.float32)
    grad_hidden = gelu_back(grad_act)[0].astype(jnp.bfloat16)
    grad_norm_in = jnp.einsum("rf,df->rd", grad_hidden, up_full, preferred_element_type=jnp.float32)
    second_norm, second_back = jax.vjp(layer_norm, residual, gain_second, shift_second)
    grad_resid_norm, grad_mlp_gain, grad_mlp_shift = second_back(grad_norm_in)
    grad_residual = grad_out.astype(jnp.float32) + grad_resid_norm
    grad_branch = grad_residual.astype(jnp.bfloat16)
    grad_attended = jnp.einsum(
        "re,de->rd", grad_branch, out_rel, preferred_element_type=jnp.float32
    ).astype(jnp.bfloat16)
    grad_attended = grad_attended.reshape(slot_count, piece_size, n_seq, group_width)
    slot_grads = []
    for slot in range(slot_count):
        slot_grads.append(
            jnp.concatenate(
                [grad_attended[slot, :, 0]]
                + [xor_send(grad_attended[slot, :, r], "seq", r) for r in range(1, n_seq)],
                axis=0,
            )
        )

    grad_down_weight = jnp.einsum(
        "rf,rd->fd", activated, grad_out, preferred_element_type=jnp.float32
    )
    grad_up_weight = jnp.einsum(
        "rd,rf->df", normed_mlp, grad_hidden, preferred_element_type=jnp.float32
    )
    grad_out_rel = jnp.einsum(
        "rd,re->de", attended_tokens, grad_branch, preferred_element_type=jnp.float32
    ).reshape(n_seq, group_width, model_width)
    grad_out_weight = jnp.concatenate(
        [lax.dynamic_index_in_dim(grad_out_rel, me ^ r, 0, keepdims=False) for r in range(n_seq)],
        axis=0,
    )
    part_up = half_reduce(grad_up_weight, 1)
    part_out = half_reduce(grad_out_weight, 1)
    part_down = half_reduce(grad_down_weight, 1)
    own_up = reduce_img(
        jnp.concatenate([part_up, part_out], axis=1).reshape(n_img, shard, -1), inner_first=False
    )
    own_down = reduce_img(part_down.reshape(n_img, ff // n_img, -1))
    share_up = finish_halves(own_up[:, : ff // 2], 1)
    share_out = finish_halves(own_up[:, ff // 2 :], 1)
    share_down = finish_halves(own_down, 1)

    grad_down_bias = jnp.sum(grad_out.astype(jnp.float32), axis=0)
    grad_up_bias = jnp.sum(grad_hidden.astype(jnp.float32), axis=0)
    grad_out_bias = jnp.sum(grad_branch.astype(jnp.float32), axis=0)

    grad_columns = jnp.zeros((model_width, group), jnp.float32)
    bias_sums = jnp.zeros((group,), jnp.float32)
    own_sums = []
    for slot in range(slot_count):
        grad_qkv = attend_backward(slot_qkv[slot], slot_grads[slot], key_valid, score_scale)
        partial_in = jnp.einsum(
            "re,de->rd", grad_qkv, qkv_cols, preferred_element_type=jnp.float32
        ).reshape(n_seq, piece_size, model_width)
        low = partial_in.astype(jnp.bfloat16)
        pair = xor_send(low[1], "seq", 1).astype(jnp.float32)
        across = xor_send(low[3], "seq", 1).astype(jnp.float32)
        across = xor_send((partial_in[2] + across).astype(jnp.bfloat16), "seq", 2)
        own_sums.append(partial_in[0] + pair + across.astype(jnp.float32))
        grad_columns += jnp.einsum(
            "rd,re->de", slot_normed[slot], grad_qkv, preferred_element_type=jnp.float32
        )
        bias_sums += jnp.sum(grad_qkv.astype(jnp.float32), axis=0)
    grad_norm_first = jnp.concatenate(own_sums, axis=0)
    first_norm, first_back = jax.vjp(layer_norm, inputs, gain_first, shift_first)
    grad_inputs_norm, grad_norm_gain, grad_norm_shift = first_back(grad_norm_first)
    tokens_grad = (grad_residual + grad_inputs_norm).reshape(slot_count, piece_size, model_width)

    own_columns = reduce_img(grad_columns.reshape(n_img, shard, group)).astype(jnp.bfloat16)
    by_sender = [own_columns] + [xor_send(own_columns, "seq", r) for r in range(1, n_seq)]
    by_sender = jnp.stack(by_sender)
    share_qkv = jnp.concatenate(
        [lax.dynamic_index_in_dim(by_sender, me ^ g, 0, keepdims=False) for g in range(n_seq)],
        axis=1,
    ).astype(jnp.float32)

    bias_sums = bias_sums.reshape(heads_here, 3, HEAD_DIM)
    grad_pairs = jnp.concatenate([bias_sums[:, :1], bias_sums[:, 2:]], axis=1).reshape(-1)
    grad_pairs = lax.dynamic_update_slice_in_dim(
        jnp.zeros((2 * D,), jnp.float32), grad_pairs, me * grad_pairs.shape[0], 0
    )
    vectors = [
        grad_norm_gain,
        grad_norm_shift,
        grad_pairs,
        grad_out_bias,
        grad_mlp_gain,
        grad_mlp_shift,
        grad_up_bias,
        grad_down_bias,
    ]
    totals = all_sum(jnp.concatenate([v.reshape(n_img, -1) for v in vectors], axis=1))
    mine = lax.dynamic_index_in_dim(totals, own_img, 0, keepdims=False)
    shares, at = [], 0
    for v in vectors:
        size = v.shape[0] // n_img
        shares.append(mine[at : at + size])
        at += size
    return (
        layer_out,
        tokens_grad,
        shares[0],
        shares[1],
        share_qkv,
        shares[2],
        share_out,
        shares[3],
        shares[4],
        shares[5],
        share_up,
        shares[6],
        share_down,
        shares[7],
    )


def solution(mesh):
    placed = (
        P("img", "seq", None),
        P("img", "seq", None),
        P("img"),
        P(),
        P("img"),
        P("img"),
        P("img", None),
        P("img"),
        P("img", None),
        P("img"),
        P("img"),
        P("img"),
        P("img", None),
        P("img"),
        P("img", None),
        P("img"),
    )
    return jax.shard_map(
        local,
        mesh=mesh,
        in_specs=placed,
        out_specs=(
            P("img", "seq", None),
            P("img", "seq", None),
            P("img"),
            P("img"),
            P("img", None),
            P("img"),
            P("img", None),
            P("img"),
            P("img"),
            P("img"),
            P("img", None),
            P("img"),
            P("img", None),
            P("img"),
        ),
        check_vma=False,
    )
```

time: 1120 us -> 674 us (0.60)
  waiting for transfers between devices: 536 us -> 178 us
  blocking collectives: 108 us -> 0 us
  matrix products: 217 us -> 251 us
  starting transfers between devices: 18.5 us -> 47.6 us
  between operations: 19 us -> 4.32 us
  local copies, waits for them, and re-layouts: 110 us -> 97.8 us
    reduce_scatter x4 -> x0, waiting for transfers between devices: 396 us -> none  [the longest x1 165 us: local(): lax.psum_scatter(grad_up_weight, 'img', scatter_dimension=0, tiled=True)]
    ppermute x0 -> x80, waiting for transfers between devices: none -> 178 us  [the longest x62 84 us: xor_send(): return lax.ppermute(block, axis, [(i, i ^ bits) for i in range(n)])]
    all_to_all x4 -> x0, waiting for transfers between devices: 123 us -> none  [the longest x1 60.4 us: local(): lax.all_to_all(grad_qkv_heads.reshape(slot_count, seq_rows, 1, -1), 'seq'...]
    unnamed x2 -> x0, blocking collectives: 75.9 us -> none
    ppermute x0 -> x80, starting transfers between devices: none -> 47.6 us  [the longest x62 37.4 us: xor_send(): return lax.ppermute(block, axis, [(i, i ^ bits) for i in range(n)])]
    reshape x13 -> x10, local copies, waits for them, and re-layouts: 52.1 us -> 8.18 us  [the longest x1 4.6 us: local(): grad_attended.reshape(slot_count, piece_size, n_seq, group_width)]
    sub x0 -> x3, matrix products: none -> 33.2 us  [attend_forward(): probs = jax.nn.softmax(scores, axis=-1).astype(jnp.bfloat16)]
    all_gather x1 -> x0, blocking collectives: 26.1 us -> none  [local(): lax.all_gather(up_bias, 'img', axis=0, tiled=True)]
  transfers between devices with their start and end apart: 13 -> 80, of which waited for: 7 -> 30; matrix products, arithmetic and copies ran while one was open for 33% -> 55% of each run, Pallas kernels for 0% -> 0%
where the time goes in v1:
time: 674 us; the launch traced here: 666 us
  matrix products  251 us (37%)
  waiting for transfers between devices  178 us (26%)
  local copies, waits for them, and re-layouts  97.8 us (15%)
  other arithmetic  87.4 us (13%)
  starting transfers between devices  47.6 us (7%)
    ppermute x62, waiting for transfers between devices, xor_send(): return lax.ppermute(block, axis, [(i, i ^ bits) for i in range(n)])  84 us
    ppermute x9, waiting for transfers between devices, ring_reduce(): arrived = lax.ppermute(total.astype(jnp.bfloat16), 'img', ring_perm())  62.4 us
    dot_general x3, matrix products, attend_backward(): jnp.einsum('qhd,khd->hqk', grads, cols[:, :, 2], preferred_element_type=j...  41.6 us
    ppermute x62, starting transfers between devices, xor_send(): return lax.ppermute(block, axis, [(i, i ^ bits) for i in range(n)])  37.4 us
    sub x3, matrix products, attend_forward(): probs = jax.nn.softmax(scores, axis=-1).astype(jnp.bfloat16)  33.2 us
    ppermute x9, waiting for transfers between devices, ring_gather(): moving = lax.ppermute(moving, 'img', ring_perm())  31.7 us
    dot_general x1, matrix products, local(): jnp.dot(normed_mlp, up_full, preferred_element_type=jnp.float32) + bias_up  31.3 us
    dot_general x3, matrix products, attend_backward(): jnp.einsum('hqk,qhd->khd', probs.astype(jnp.bfloat16), grads, preferred_e...  24.7 us
  transfers between devices with their start and end apart: 80, of which 30 were waited for; matrix products, arithmetic and copies ran while one was open for 55% of the time, Pallas kernels for 0%

profile of v1, /device:TPU:0, one launch (start us, length us, event | category | flops | bytes accessed | tf_op | source)
XLA Modules:
  0.0 666.1 jit_solution(11639381765579995693)
XLA Ops:
  40.6 12.7 %collective-permute-done.5 = bf16[2,112,576]{2,1,0:T(8,128)(2,1)S(1)} collective-permute-done((bf16[2,112,576]{2,1,0:T(8,128)(2,1)S(1)}, bf16[2,112,576]{2,1,0:T(8,128)(2,1)S(1)}, u32[]{:S(2)}, u32[]{:S(2)}) %collective-permute-start.5) | collective-permute-done | bytes 258080 | tf_op jit(solution)/shard_map/ppermute | solution.py:59
  56.4 8.8 %collective-permute-done.17 = bf16[264,768]{1,0:T(8,128)(2,1)S(1)} collective-permute-done((bf16[264,768]{1,0:T(8,128)(2,1)S(1)}, bf16[264,768]{1,0:T(8,128)(2,1)S(1)}, u32[]{:S(2)}, u32[]{:S(2)}) %collective-permute-start.17) | collective-permute-done | bytes 405536 | tf_op jit(solution)/shard_map/ppermute | solution.py:25
  72.8 10.5 %collective-permute-done.29 = bf16[2,384,384]{2,1,0:T(8,128)(2,1)} collective-permute-done((bf16[2,384,384]{2,1,0:T(8,128)(2,1)S(1)}, bf16[2,384,384]{2,1,0:T(8,128)(2,1)}, u32[]{:S(2)}, u32[]{:S(2)}) %collective-permute-start.29) | collective-permute-done | bytes 589856 | tf_op jit(solution)/shard_map/ppermute | solution.py:59
  99.0 11.0 %fusion.181 = (f32[3,1056]{1,0:T(4,128)S(1)}, f32[3,1056,1056]{1,2,0:T(8,128)}) fusion(pred[1056]{0:T(1024)(128)(4,1)S(1)} %lt.232, bf16[1056,3,3,64]{0,3,2,1:T(8,128)(2,1)} %bitcast.485), kind=kOutput, calls=%fused_computation.357 | convolution fusion | flops 441594912 | bytes 14280096 | tf_op jit(solution)/shard_map/sub | solution.py:153
  110.0 8.4 %fusion.93 = bf16[1056,3,64]{0,2,1:T(8,128)(2,1)} fusion(bf16[1056,3,3,64]{0,3,2,1:T(8,128)(2,1)} %bitcast.486, f32[3,1056]{1,0:T(4,128)S(1)} %get-tuple-element.112, pred[1056]{0:T(1024)(128)(4,1)S(1)} %lt.232), kind=kOutput, calls=%fused_computation.147 | convolution fusion | flops 873358464 | bytes 1635744 | tf_op jit(solution)/shard_map/hqk,khd->qhd/dot_general | solution.py:154
  122.4 11.1 %fusion.180 = (f32[3,1056]{1,0:T(4,128)S(1)}, f32[3,1056,1056]{1,2,0:T(8,128)}) fusion(pred[1056]{0:T(1024)(128)(4,1)S(1)} %lt.232, bf16[1056,3,3,64]{0,3,2,1:T(8,128)(2,1)} %bitcast.491), kind=kOutput, calls=%fused_computation.356 | convolution fusion | flops 441594912 | bytes 14280096 | tf_op jit(solution)/shard_map/sub | solution.py:153
  140.0 7.8 %fusion.90 = bf16[1056,3,64]{0,2,1:T(8,128)(2,1)S(1)} fusion(bf16[1056,3,3,64]{0,3,2,1:T(8,128)(2,1)} %bitcast.492, f32[3,1056]{1,0:T(4,128)S(1)} %get-tuple-element.110, pred[1056]{0:T(1024)(128)(4,1)S(1)} %lt.232), kind=kOutput, calls=%fused_computation.146 | convolution fusion | flops 873358464 | bytes 1635744 | tf_op jit(solution)/shard_map/hqk,khd->qhd/dot_general | solution.py:154
  147.9 11.0 %fusion.179 = (f32[3,1056]{1,0:T(4,128)S(1)}, f32[3,1056,1056]{1,2,0:T(8,128)}) fusion(pred[1056]{0:T(1024)(128)(4,1)S(1)} %lt.232, bf16[1056,3,3,64]{0,3,2,1:T(8,128)(2,1)} %bitcast.497), kind=kOutput, calls=%fused_computation.355 | convolution fusion | flops 441594912 | bytes 14280096 | tf_op jit(solution)/shard_map/sub | solution.py:153
  160.9 8.3 %fusion.87 = bf16[1056,3,64]{0,2,1:T(8,128)(2,1)} fusion(bf16[1056,3,3,64]{0,3,2,1:T(8,128)(2,1)} %bitcast.498, f32[3,1056]{1,0:T(4,128)S(1)} %get-tuple-element.108, pred[1056]{0:T(1024)(128)(4,1)S(1)} %lt.232), kind=kOutput, calls=%fused_computation.145 | convolution fusion | flops 873358464 | bytes 1635744 | tf_op jit(solution)/shard_map/hqk,khd->qhd/dot_general | solution.py:154
  203.6 31.3 %multiply_convert_fusion.3 = (bf16[792,3072]{1,0:T(8,128)(2,1)}, f32[792,3072]{1,0:T(8,128)}, f32[792,3072]{1,0:T(8,128)}) fusion(f32[3072]{0:T(1024)S(1)} %copy-done.113, bf16[768,1536]{1,0:T(8,128)(2,1)S(1)} %collective-permute-done.27, bf16[768,1536]{1,0:T(8,128)(2,1)S(1)} %slice.407, pred[]{:T(512)S(6)} %eq.39, f32[792,768]{1,0:T(8,128)S(1)} %bitcast_add_fusion, ...), kind=kOutput, calls=%fused_computation.26 | convolution fusion | flops 3922587648 | bytes 31509696 | tf_op jit(solution)/shard_map/dot_general | solution.py:291
  236.3 14.0 %convert_reduce_fusion = (f32[3072]{0:T(1024)S(1)}, bf16[792,3072]{1,0:T(8,128)(2,1)}) fusion(f32[792,3072]{1,0:T(8,128)} %get-tuple-element.38, bf16[792,768]{1,0:T(8,128)(2,1)} %bitcast_select_fusion, bf16[3072,384]{1,0:T(8,128)(2,1)} %copy-done.125, bf16[3072,384]{1,0:T(8,128)(2,1)S(1)} %bitcast.470, pred[]{:T(512)S(6)} %eq.39, ...), kind=kOutput, calls=%fused_computation.24 | convolution fusion | flops 3799716864 | bytes 30289920 | tf_op jit(solution)/shard_map/rd,fd->rf/dot_general | solution.py:303
  251.0 10.4 %fusion.158 = f32[768,3072]{1,0:T(8,128)} fusion(bf16[792,3072]{1,0:T(8,128)(2,1)} %get-tuple-element.129, f32[792,768]{1,0:T(8,128)S(1)} %bitcast_add_fusion, f32[768]{0:T(1024)S(1)} %add.506, f32[768]{0:T(1024)S(1)} %mul.348, f32[792]{0:T(1024)S(1)} %fusion.133, f32[792]{0:T(1024)S(1)} %broadcast_multiply_fusion.4, f32[768]{0:T(1024)S(1)} %add.502), kind=kOutput, calls=%fused_computation.339 | convolution fusion | flops 3740774400 | bytes 16751808 | tf_op jit(solution)/shard_map/rd,rf->df/dot_general | solution.py:327
  284.9 8.4 %fusion.159 = f32[768,768]{1,0:T(8,128)S(1)} fusion(bf16[792,768]{1,0:T(8,128)(2,1)} %get-tuple-element.22, bf16[264,192]{0,1:T(8,128)(2,1)} %copy-done.139, bf16[264,192]{0,1:T(8,128)(2,1)} %copy-done.140, bf16[264,192]{0,1:T(8,128)(2,1)} %copy-done.141, bf16[264,192]{0,1:T(8,128)(2,1)S(1)} %bitcast.509, bf16[264,192]{0,1:T(8,128)(2,1)S(1)} %copy-done.136, ...), kind=kOutput, calls=%fused_computation.340 | convolution fusion | flops 948879360 | bytes 4792320 | tf_op jit(solution)/shard_map/rd,re->de/dot_general | solution.py:330
  332.2 14.1 %multiply_reduce_fusion = (f32[3,1056]{1,0:T(4,128)S(1)}, f32[3,1056,1056]{1,2,0:T(8,128)}) fusion(f32[3,1056,1056]{1,2,0:T(8,128)} %get-tuple-element.109, f32[3,1056]{1,0:T(4,128)S(1)} %copy-done.104, bf16[1056,3,64]{0,2,1:T(8,128)(2,1)S(1)} %concatenate.188, bf16[1056,3,3,64]{0,3,2,1:T(8,128)(2,1)S(1)} %bitcast.501), kind=kOutput, calls=%fused_computation.17 | convolution fusion | flops 438245280 | bytes 27679104 | tf_op jit(solution)/shard_map/qhd,khd->hqk/dot_general | solution.py:168
  364.2 7.9 %fusion.54 = bf16[1056,3,1,64]{0,3,1,2:T(8,128)(2,1)} fusion(bf16[1056,3,64]{0,2,1:T(8,128)(2,1)} %concatenate.183, f32[3,1056]{1,0:T(4,128)S(1)} %copy-done.102, pred[1056]{0:T(1024)(128)(4,1)S(1)} %copy-done.124, bf16[1056,3,3,64]{0,3,2,1:T(8,128)(2,1)S(1)} %bitcast.493), kind=kOutput, calls=%fused_computation.109 | convolution fusion | flops 873155712 | bytes 1716224 | tf_op jit(solution)/shard_map/hqk,qhd->khd/dot_general | solution.py:177
  372.2 13.9 %multiply_reduce_fusion.1 = (f32[3,1056]{1,0:T(4,128)S(1)}, f32[3,1056,1056]{1,2,0:T(8,128)}) fusion(f32[3,1056,1056]{1,2,0:T(8,128)} %get-tuple-element.111, f32[3,1056]{1,0:T(4,128)S(1)} %copy-done.102, bf16[1056,3,64]{0,2,1:T(8,128)(2,1)S(1)} %copy-done.70, bf16[1056,3,3,64]{0,3,2,1:T(8,128)(2,1)S(1)} %bitcast.494), kind=kOutput, calls=%fused_computation.19 | convolution fusion | flops 438245280 | bytes 27679104 | tf_op jit(solution)/shard_map/qhd,khd->hqk/dot_general | solution.py:168
  396.5 8.1 %fusion.57 = bf16[1056,3,1,64]{0,3,1,2:T(8,128)(2,1)} fusion(bf16[1056,3,64]{0,2,1:T(8,128)(2,1)} %copy-done.69, f32[3,1056]{1,0:T(4,128)S(1)} %copy-done.104, pred[1056]{0:T(1024)(128)(4,1)S(1)} %copy-done.124, bf16[1056,3,3,64]{0,3,2,1:T(8,128)(2,1)} %bitcast.500), kind=kOutput, calls=%fused_computation.110 | convolution fusion | flops 873155712 | bytes 1746336 | tf_op jit(solution)/shard_map/hqk,qhd->khd/dot_general | solution.py:177
  408.8 8.6 %fusion.51 = bf16[1056,3,1,64]{0,3,1,2:T(8,128)(2,1)} fusion(bf16[1056,3,64]{0,2,1:T(8,128)(2,1)} %concatenate.178, f32[3,1056]{1,0:T(4,128)S(1)} %copy-done.100, pred[1056]{0:T(1024)(128)(4,1)S(1)} %copy-done.124, bf16[1056,3,3,64]{0,3,2,1:T(8,128)(2,1)} %bitcast.487), kind=kOutput, calls=%fused_computation.108 | convolution fusion | flops 873155712 | bytes 1746336 | tf_op jit(solution)/shard_map/hqk,qhd->khd/dot_general | solution.py:177
  417.5 13.5 %multiply_reduce_fusion.2 = (f32[3,1056]{1,0:T(4,128)S(1)}, f32[3,1056,1056]{1,2,0:T(8,128)}) fusion(f32[3,1056,1056]{1,2,0:T(8,128)} %get-tuple-element.113, f32[3,1056]{1,0:T(4,128)S(1)} %copy-done.100, bf16[1056,3,64]{0,2,1:T(8,128)(2,1)} %concatenate.178, bf16[1056,3,3,64]{0,3,2,1:T(8,128)(2,1)S(1)} %bitcast.488), kind=kOutput, calls=%fused_computation.21 | convolution fusion | flops 438245280 | bytes 27642240 | tf_op jit(solution)/shard_map/qhd,khd->hqk/dot_general | solution.py:168
  474.5 10.0 %collective-permute-done.56 = bf16[4,96,576]{2,1,0:T(8,128)(2,1)S(1)} collective-permute-done((bf16[4,96,576]{2,1,0:T(8,128)(2,1)S(1)}, bf16[4,96,576]{2,1,0:T(8,128)(2,1)S(1)}, u32[]{:S(2)}, u32[]{:S(2)}) %collective-permute-start.56) | collective-permute-done | bytes 442400 | tf_op jit(solution)/shard_map/ppermute | solution.py:25
  555.1 12.1 %collective-permute-done.65 = bf16[2,96,1920]{2,1,0:T(8,128)(2,1)} collective-permute-done((bf16[2,96,1920]{2,1,0:T(8,128)(2,1)}, bf16[2,96,1920]{2,1,0:T(8,128)(2,1)}, u32[]{:S(2)}, u32[]{:S(2)}) %collective-permute-start.65) | collective-permute-done | bytes 737312 | tf_op jit(solution)/shard_map/ppermute | solution.py:82
  569.9 12.8 %collective-permute-done.53 = f32[8,1152]{1,0:T(8,128)S(1)} collective-permute-done((f32[8,1152]{1,0:T(8,128)S(1)}, f32[8,1152]{1,0:T(8,128)S(1)}, u32[]{:S(2)}, u32[]{:S(2)}) %collective-permute-start.53) | collective-permute-done | bytes 36896 | tf_op jit(solution)/shard_map/ppermute | solution.py:25
  589.4 13.4 %collective-permute-done.54 = f32[8,1152]{1,0:T(8,128)S(1)} collective-permute-done((f32[8,1152]{1,0:T(8,128)S(1)}, f32[8,1152]{1,0:T(8,128)S(1)}, u32[]{:S(2)}, u32[]{:S(2)}) %collective-permute-start.54) | collective-permute-done | bytes 36896 | tf_op jit(solution)/shard_map/ppermute | solution.py:25
  618.8 18.6 %collective-permute-done.76 = bf16[384,384]{1,0:T(8,128)(2,1)} collective-permute-done((bf16[384,384]{1,0:T(8,128)(2,1)}, bf16[384,384]{1,0:T(8,128)(2,1)}, u32[]{:S(2)}, u32[]{:S(2)}) %collective-permute-start.76) | collective-permute-done | bytes 294944 | tf_op jit(solution)/shard_map/ppermute | solution.py:82
  (708 shorter events, 374.8 us)
Async XLA Ops:
  3.0 50.3 %collective-permute-start.1 = (bf16[264,768]{1,0:T(8,128)(2,1)}, bf16[264,768]{1,0:T(8,128)(2,1)}, u32[]{:S(2)}, u32[]{:S(2)}) collective-permute-start(bf16[264,768]{1,0:T(8,128)(2,1)} %get-tuple-element.61), channel_id=1, source_target_pairs={{0,2},{1,3},{2,0},{3,1},{4,6},{5,7},{6,4},{7,5},{8,10},{9,11},{10,... | collective-permute-start | bytes 1216520 | tf_op jit(solution)/shard_map/ppermute | solution.py:25
  6.0 50.1 %collective-permute-start = (bf16[264,768]{1,0:T(8,128)(2,1)}, bf16[264,768]{1,0:T(8,128)(2,1)}, u32[]{:S(2)}, u32[]{:S(2)}) collective-permute-start(bf16[264,768]{1,0:T(8,128)(2,1)} %get-tuple-element.61), channel_id=1, source_target_pairs={{0,1},{1,0},{2,3},{3,2},{4,5},{5,4},{6,7},{7,6},{8,9},{9,8},{10,11... | collective-permute-start | bytes 1216520 | tf_op jit(solution)/shard_map/ppermute | solution.py:25
  68.4 69.0 %collective-permute-start.24 = (bf16[96,1920]{1,0:T(8,128)(2,1)}, bf16[96,1920]{1,0:T(8,128)(2,1)}, u32[]{:S(2)}, u32[]{:S(2)}) collective-permute-start(bf16[96,1920]{1,0:T(8,128)(2,1)} %collective-permute-done.23), channel_id=1, source_target_pairs={{0,8},{4,12},{8,16},{12,20},{16,24},{20,28},{24,0},{28,4},{1,9},{5... | collective-permute-start | bytes 1105928 | tf_op jit(solution)/shard_map/ppermute | solution.py:59
  83.4 85.9 %collective-permute-start.30 = (bf16[2,384,384]{2,1,0:T(8,128)(2,1)}, bf16[2,384,384]{2,1,0:T(8,128)(2,1)}, u32[]{:S(2)}, u32[]{:S(2)}) collective-permute-start(bf16[2,384,384]{2,1,0:T(8,128)(2,1)} %collective-permute-done.29), channel_id=1, source_target_pairs={{0,8},{4,12},{8,16},{12,20},{16,24},{20,28},{24,0},{28,4},{1,9},{5... | collective-permute-start | bytes 1769480 | tf_op jit(solution)/shard_map/ppermute | solution.py:59
  138.4 31.9 %collective-permute-start.25 = (bf16[4,96,1920]{2,1,0:T(8,128)(2,1)S(1)}, bf16[4,96,1920]{2,1,0:T(8,128)(2,1)}, u32[]{:S(2)}, u32[]{:S(2)}) collective-permute-start(bf16[4,96,1920]{2,1,0:T(8,128)(2,1)S(1)} %bitcast_dynamic-update-slice_fusion.3), channel_id=1, source_target_pairs={{0,4},{4,0},{8,12},{12,8},{16,20},{20,16},{24,28},{28,24},{1,5},{5... | collective-permute-start | bytes 4423688 | tf_op jit(solution)/shard_map/ppermute | solution.py:25
  195.3 39.6 %collective-permute-start.32 = (bf16[3072,384]{1,0:T(8,128)(2,1)S(1)}, bf16[3072,384]{1,0:T(8,128)(2,1)S(1)}, u32[]{:S(2)}, u32[]{:S(2)}) collective-permute-start(bf16[3072,384]{1,0:T(8,128)(2,1)S(1)} %bitcast.469), channel_id=1, source_target_pairs={{0,1},{1,0},{2,3},{3,2},{4,5},{5,4},{6,7},{7,6},{8,9},{9,8},{10,11... | collective-permute-start | bytes 7077896 | tf_op jit(solution)/shard_map/ppermute | solution.py:25
  294.5 207.6 %collective-permute-start.64 = (bf16[768,384]{1,0:T(8,128)(2,1)}, bf16[768,384]{1,0:T(8,128)(2,1)}, u32[]{:S(2)}, u32[]{:S(2)}) collective-permute-start(bf16[768,384]{1,0:T(8,128)(2,1)} %dynamic-slice_convert_fusion.3), channel_id=1, source_target_pairs={{0,1},{1,0},{2,3},{3,2},{4,5},{5,4},{6,7},{7,6},{8,9},{9,8},{10,11... | collective-permute-start | bytes 1769480 | tf_op jit(solution)/shard_map/ppermute | solution.py:25
  300.9 25.7 %collective-permute-start.47 = (bf16[264,192]{1,0:T(8,128)(2,1)}, bf16[264,192]{1,0:T(8,128)(2,1)}, u32[]{:S(2)}, u32[]{:S(2)}) collective-permute-start(bf16[264,192]{1,0:T(8,128)(2,1)} %bitcast.421), channel_id=1, source_target_pairs={{0,3},{1,2},{2,1},{3,0},{4,7},{5,6},{6,5},{7,4},{8,11},{9,10},{10,... | collective-permute-start | bytes 304136 | tf_op jit(solution)/shard_map/ppermute | solution.py:25
  301.3 27.0 %collective-permute-start.45 = (bf16[264,192]{1,0:T(8,128)(2,1)}, bf16[264,192]{1,0:T(8,128)(2,1)}, u32[]{:S(2)}, u32[]{:S(2)}) collective-permute-start(bf16[264,192]{1,0:T(8,128)(2,1)} %bitcast.423), channel_id=1, source_target_pairs={{0,1},{1,0},{2,3},{3,2},{4,5},{5,4},{6,7},{7,6},{8,9},{9,8},{10,11... | collective-permute-start | bytes 304136 | tf_op jit(solution)/shard_map/ppermute | solution.py:25
  302.2 28.4 %collective-permute-start.46 = (bf16[264,192]{1,0:T(8,128)(2,1)}, bf16[264,192]{1,0:T(8,128)(2,1)}, u32[]{:S(2)}, u32[]{:S(2)}) collective-permute-start(bf16[264,192]{1,0:T(8,128)(2,1)} %bitcast.422), channel_id=1, source_target_pairs={{0,2},{1,3},{2,0},{3,1},{4,6},{5,7},{6,4},{7,5},{8,10},{9,11},{10,... | collective-permute-start | bytes 304136 | tf_op jit(solution)/shard_map/ppermute | solution.py:25
  326.0 78.6 %collective-permute-start.33 = (bf16[264,192]{1,0:T(8,128)(2,1)}, bf16[264,192]{1,0:T(8,128)(2,1)}, u32[]{:S(2)}, u32[]{:S(2)}) collective-permute-start(bf16[264,192]{1,0:T(8,128)(2,1)} %bitcast.429), channel_id=1, source_target_pairs={{0,1},{1,0},{2,3},{3,2},{4,5},{5,4},{6,7},{7,6},{8,9},{9,8},{10,11... | collective-permute-start | bytes 304136 | tf_op jit(solution)/shard_map/ppermute | solution.py:25
  326.6 31.0 %collective-permute-start.39 = (bf16[264,192]{1,0:T(8,128)(2,1)}, bf16[264,192]{1,0:T(8,128)(2,1)}, u32[]{:S(2)}, u32[]{:S(2)}) collective-permute-start(bf16[264,192]{1,0:T(8,128)(2,1)} %bitcast.426), channel_id=1, source_target_pairs={{0,1},{1,0},{2,3},{3,2},{4,5},{5,4},{6,7},{7,6},{8,9},{9,8},{10,11... | collective-permute-start | bytes 304136 | tf_op jit(solution)/shard_map/ppermute | solution.py:25
  328.3 31.7 %collective-permute-start.40 = (bf16[264,192]{1,0:T(8,128)(2,1)}, bf16[264,192]{1,0:T(8,128)(2,1)}, u32[]{:S(2)}, u32[]{:S(2)}) collective-permute-start(bf16[264,192]{1,0:T(8,128)(2,1)} %bitcast.425), channel_id=1, source_target_pairs={{0,2},{1,3},{2,0},{3,1},{4,6},{5,7},{6,4},{7,5},{8,10},{9,11},{10,... | collective-permute-start | bytes 304136 | tf_op jit(solution)/shard_map/ppermute | solution.py:25
  330.5 31.5 %collective-permute-start.41 = (bf16[264,192]{1,0:T(8,128)(2,1)}, bf16[264,192]{1,0:T(8,128)(2,1)}, u32[]{:S(2)}, u32[]{:S(2)}) collective-permute-start(bf16[264,192]{1,0:T(8,128)(2,1)} %bitcast.424), channel_id=1, source_target_pairs={{0,3},{1,2},{2,1},{3,0},{4,7},{5,6},{6,5},{7,4},{8,11},{9,10},{10,... | collective-permute-start | bytes 304136 | tf_op jit(solution)/shard_map/ppermute | solution.py:25
  357.7 48.0 %collective-permute-start.34 = (bf16[264,192]{1,0:T(8,128)(2,1)}, bf16[264,192]{1,0:T(8,128)(2,1)}, u32[]{:S(2)}, u32[]{:S(2)}) collective-permute-start(bf16[264,192]{1,0:T(8,128)(2,1)} %bitcast.428), channel_id=1, source_target_pairs={{0,2},{1,3},{2,0},{3,1},{4,6},{5,7},{6,4},{7,5},{8,10},{9,11},{10,... | collective-permute-start | bytes 304136 | tf_op jit(solution)/shard_map/ppermute | solution.py:25
  359.9 46.8 %collective-permute-start.35 = (bf16[264,192]{1,0:T(8,128)(2,1)S(1)}, bf16[264,192]{1,0:T(8,128)(2,1)}, u32[]{:S(2)}, u32[]{:S(2)}) collective-permute-start(bf16[264,192]{1,0:T(8,128)(2,1)S(1)} %bitcast.519), channel_id=1, source_target_pairs={{0,3},{1,2},{2,1},{3,0},{4,7},{5,6},{6,5},{7,4},{8,11},{9,10},{10,... | collective-permute-start | bytes 304136 | tf_op jit(solution)/shard_map/ppermute | solution.py:25
  362.1 179.4 %collective-permute-start.63 = (bf16[768,1536]{1,0:T(8,128)(2,1)}, bf16[768,1536]{1,0:T(8,128)(2,1)}, u32[]{:S(2)}, u32[]{:S(2)}) collective-permute-start(bf16[768,1536]{1,0:T(8,128)(2,1)} %dynamic-slice_convert_fusion.1), channel_id=1, source_target_pairs={{0,1},{1,0},{2,3},{3,2},{4,5},{5,4},{6,7},{7,6},{8,9},{9,8},{10,11... | collective-permute-start | bytes 7077896 | tf_op jit(solution)/shard_map/ppermute | solution.py:25
  447.3 62.8 %collective-permute-start.42 = (bf16[264,768]{1,0:T(8,128)(2,1)}, bf16[264,768]{1,0:T(8,128)(2,1)S(1)}, u32[]{:S(2)}, u32[]{:S(2)}) collective-permute-start(bf16[264,768]{1,0:T(8,128)(2,1)} %get-tuple-element.57), channel_id=1, source_target_pairs={{0,1},{1,0},{2,3},{3,2},{4,5},{5,4},{6,7},{7,6},{8,9},{9,8},{10,11... | collective-permute-start | bytes 1216520 | tf_op jit(solution)/shard_map/ppermute | solution.py:25
  514.6 32.2 %collective-permute-start.73 = (bf16[3072,384]{1,0:T(8,128)(2,1)}, bf16[3072,384]{1,0:T(8,128)(2,1)}, u32[]{:S(2)}, u32[]{:S(2)}) collective-permute-start(bf16[3072,384]{1,0:T(8,128)(2,1)} %dynamic-slice_convert_fusion), channel_id=1, source_target_pairs={{0,1},{1,0},{2,3},{3,2},{4,5},{5,4},{6,7},{7,6},{8,9},{9,8},{10,11... | collective-permute-start | bytes 7077896 | tf_op jit(solution)/shard_map/ppermute | solution.py:25
  522.0 65.6 %collective-permute-start.62 = (bf16[96,576]{1,0:T(8,128)(2,1)S(1)}, bf16[96,576]{1,0:T(8,128)(2,1)}, u32[]{:S(2)}, u32[]{:S(2)}) collective-permute-start(bf16[96,576]{1,0:T(8,128)(2,1)S(1)} %fusion.127), channel_id=1, source_target_pairs={{0,3},{1,2},{2,1},{3,0},{4,7},{5,6},{6,5},{7,4},{8,11},{9,10},{10,... | collective-permute-start | bytes 331784 | tf_op jit(solution)/shard_map/ppermute | solution.py:25
  522.2 65.5 %collective-permute-start.61 = (bf16[96,576]{1,0:T(8,128)(2,1)S(1)}, bf16[96,576]{1,0:T(8,128)(2,1)S(1)}, u32[]{:S(2)}, u32[]{:S(2)}) collective-permute-start(bf16[96,576]{1,0:T(8,128)(2,1)S(1)} %fusion.127), channel_id=1, source_target_pairs={{0,2},{1,3},{2,0},{3,1},{4,6},{5,7},{6,4},{7,5},{8,10},{9,11},{10,... | collective-permute-start | bytes 331784 | tf_op jit(solution)/shard_map/ppermute | solution.py:25
  554.0 49.4 %collective-permute-start.74 = (bf16[4,384,384]{2,1,0:T(8,128)(2,1)}, bf16[4,384,384]{2,1,0:T(8,128)(2,1)}, u32[]{:S(2)}, u32[]{:S(2)}) collective-permute-start(bf16[4,384,384]{2,1,0:T(8,128)(2,1)} %fusion.99), channel_id=1, source_target_pairs={{0,4},{4,0},{8,12},{12,8},{16,20},{20,16},{24,28},{28,24},{1,5},{5... | collective-permute-start | bytes 3538952 | tf_op jit(solution)/shard_map/ppermute | solution.py:25
  555.0 32.7 %collective-permute-start.60 = (bf16[96,576]{1,0:T(8,128)(2,1)S(1)}, bf16[96,576]{1,0:T(8,128)(2,1)S(1)}, u32[]{:S(2)}, u32[]{:S(2)}) collective-permute-start(bf16[96,576]{1,0:T(8,128)(2,1)S(1)} %fusion.127), channel_id=1, source_target_pairs={{0,1},{1,0},{2,3},{3,2},{4,5},{5,4},{6,7},{7,6},{8,9},{9,8},{10,11... | collective-permute-start | bytes 331784 | tf_op jit(solution)/shard_map/ppermute | solution.py:25
  607.4 31.1 %collective-permute-start.67 = (bf16[2,96,1920]{2,1,0:T(8,128)(2,1)}, bf16[2,96,1920]{2,1,0:T(8,128)(2,1)}, u32[]{:S(2)}, u32[]{:S(2)}) collective-permute-start(bf16[2,96,1920]{2,1,0:T(8,128)(2,1)} %fusion.97), channel_id=1, source_target_pairs={{0,8},{4,12},{8,16},{12,20},{16,24},{20,28},{24,0},{28,4},{1,9},{5... | collective-permute-start | bytes 2211848 | tf_op jit(solution)/shard_map/ppermute | solution.py:82
  (218 other events, 2783.9 us)

commit v2 on v1

v2 whole, which is shorter than its diff:
```python
from functools import partial

import jax
import jax.numpy as jnp
import numpy as np
from jax import lax
from jax.experimental import pallas as pl
from jax.experimental.pallas import tpu as pltpu
from jax.sharding import PartitionSpec as P

D = 768
HEADS = 12
HEAD_DIM = 64
EPS = 1e-06
NEG = -1e30
LANES = 128
F32 = jnp.float32
BF16 = jnp.bfloat16
VMEM_BYTES = 60 * 1024 * 1024


def mm(left, right, left_dim=1, right_dim=0):
    return lax.dot_general(
        left, right, (((left_dim,), (right_dim,)), ((), ())), preferred_element_type=F32
    )


def normalize(features):
    row_mean = jnp.mean(features, axis=-1, keepdims=True)
    centred = features - row_mean
    spread = jnp.mean(centred * centred, axis=-1, keepdims=True)
    factor = lax.rsqrt(spread + EPS)
    return centred * factor, factor


def round_up(size, unit):
    return -(-size // unit) * unit


def head_columns(heads, parts):
    place = np.zeros((heads * parts, LANES, heads * parts * HEAD_DIM), np.float32)
    for b in range(heads * parts):
        for d in range(HEAD_DIM):
            place[b, d, b * HEAD_DIM + d] = 1.0
    return jnp.asarray(place, BF16)


def query_block(rows):
    for size in range(min(rows, 400) // 16 * 16, 15, -16):
        if rows % size == 0:
            return size
    return rows


def forward_kernel(n_seq, heads, n_after, *refs):
    tokens, refs = refs[:n_seq], refs[:n_seq] + refs[n_seq + n_after :]
    gain, shift, weight, bias, key_mask, place = refs[n_seq : n_seq + 6]
    normed_out, qkv_out, attended_out, rows, attended = refs[n_seq + 6 :]
    piece = tokens[0].shape[0]
    total = n_seq * piece
    for r in range(n_seq):
        unit, _ = normalize(tokens[r][...].astype(F32))
        rows[r * piece : (r + 1) * piece, :] = unit * gain[...] + shift[...]
    normed = rows[...].astype(BF16)
    normed_out[...] = normed
    block = query_block(total)
    pad = qkv_out.shape[1] - total
    for h in range(heads):
        parts = []
        for t in range(3):
            b = 3 * h + t
            part = mm(normed, weight[b]) + bias[b]
            if t == 1:
                part = part + key_mask[...]
            part = part.astype(BF16)
            qkv_out[b, :total] = part
            if pad:
                qkv_out[b, total:] = jnp.zeros((pad, LANES), BF16)
            parts.append(part)
        queries, keys, values = parts
        for at in range(0, total, block):
            scores = mm(queries[at : at + block], keys, 1, 1)
            peak = jnp.max(scores, axis=-1, keepdims=True)
            terms = jnp.exp(scores - peak).astype(BF16)
            weighted = mm(terms, values)
            result = (weighted / weighted[:, HEAD_DIM : HEAD_DIM + 1]).astype(BF16)
            placed = mm(result, place[h])
            if h:
                placed = placed + attended[at : at + block, :]
            attended[at : at + block, :] = placed
    for r in range(n_seq):
        attended_out[r] = attended[r * piece : (r + 1) * piece, :].astype(BF16)


def after_specs(after):
    return [pl.BlockSpec(memory_space=pl.ANY)] * len(after)


def whole_specs(count):
    return [pl.BlockSpec(memory_space=pltpu.VMEM)] * count


def slot_forward(pieces, gain, shift, weight, bias, key_mask, after=()):
    n_seq = len(pieces)
    piece, width = pieces[0].shape
    heads = weight.shape[0] // 3
    total = n_seq * piece
    padded = round_up(total, LANES)
    return pl.pallas_call(
        partial(forward_kernel, n_seq, heads, len(after)),
        in_specs=whole_specs(n_seq) + after_specs(after) + whole_specs(6),
        out_shape=(
            jax.ShapeDtypeStruct((total, width), BF16),
            jax.ShapeDtypeStruct((3 * heads, padded, LANES), BF16),
            jax.ShapeDtypeStruct((n_seq, piece, heads * HEAD_DIM), BF16),
        ),
        scratch_shapes=[
            pltpu.VMEM((total, width), F32),
            pltpu.VMEM((total, heads * HEAD_DIM), F32),
        ],
        compiler_params=pltpu.CompilerParams(vmem_limit_bytes=VMEM_BYTES),
        cost_estimate=pl.CostEstimate(
            flops=20 * 10**9, bytes_accessed=12 * 10**6, transcendentals=heads * total * total
        ),
        name="slot_forward",
    )(*pieces, *after, gain, shift, weight, bias, key_mask, head_columns(heads, 1))


def backward_kernel(n_seq, heads, n_after, *refs):
    grads, refs = refs[:n_seq], refs[:n_seq] + refs[n_seq + n_after :]
    qkv, place, spread = refs[n_seq : n_seq + 3]
    grad_out, rows, total_grad = refs[n_seq + 3 :]
    piece = grads[0].shape[0]
    total = n_seq * piece
    padded = qkv.shape[1]
    for r in range(n_seq):
        rows[r * piece : (r + 1) * piece, :] = grads[r][...].astype(F32)
    if padded > total:
        rows[total:, :] = jnp.zeros((padded - total, rows.shape[1]), F32)
    grad_rows = rows[...].astype(BF16)
    block = 3 * LANES if padded % (3 * LANES) == 0 else LANES
    for h in range(heads):
        grad_head = mm(grad_rows, place[h], 1, 1).astype(BF16)
        queries = qkv[3 * h]
        keys = qkv[3 * h + 1, :total]
        values = qkv[3 * h + 2, :total]
        keys_t = jnp.transpose(qkv[3 * h + 1])[:, :total]
        grad_keys = jnp.zeros((total, LANES), F32)
        grad_values = jnp.zeros((total, LANES), F32)
        grad_queries = []
        for at in range(0, padded, block):
            query_part = queries[at : at + block]
            grad_part = grad_head[at : at + block]
            scores = mm(keys, query_part, 1, 1)
            peak = jnp.max(scores, axis=0, keepdims=True)
            terms = jnp.exp(scores - peak)
            probs = terms * (1.0 / jnp.sum(terms, axis=0, keepdims=True))
            grad_probs = mm(values, grad_part, 1, 1)
            inner = jnp.sum(probs * grad_probs, axis=0, keepdims=True)
            grad_scores = (probs * (grad_probs - inner)).astype(BF16)
            grad_values = grad_values + mm(probs.astype(BF16), grad_part)
            grad_keys = grad_keys + mm(grad_scores, query_part)
            grad_queries.append(jnp.transpose(mm(keys_t, grad_scores)))
        grad_queries = jnp.concatenate(grad_queries, axis=0)[:total] * (HEAD_DIM**-0.5)
        for t, part in enumerate((grad_queries, grad_keys, grad_values)):
            placed = mm(part.astype(BF16), spread[3 * h + t])
            if h or t:
                placed = placed + total_grad[...]
            total_grad[...] = placed
    grad_out[...] = total_grad[...].astype(BF16)


def slot_backward(grads, qkv, after=()):
    n_seq = len(grads)
    piece, width = grads[0].shape
    heads = qkv.shape[0] // 3
    total = n_seq * piece
    return pl.pallas_call(
        partial(backward_kernel, n_seq, heads, len(after)),
        in_specs=whole_specs(n_seq) + after_specs(after) + whole_specs(3),
        out_shape=jax.ShapeDtypeStruct((total, 3 * width), BF16),
        scratch_shapes=[
            pltpu.VMEM((qkv.shape[1], width), F32),
            pltpu.VMEM((total, 3 * width), F32),
        ],
        compiler_params=pltpu.CompilerParams(vmem_limit_bytes=VMEM_BYTES),
        cost_estimate=pl.CostEstimate(
            flops=28 * 10**9, bytes_accessed=8 * 10**6, transcendentals=heads * total * total
        ),
        name="slot_backward",
    )(*grads, *after, qkv, head_columns(heads, 1), head_columns(heads, 3))


def mlp_kernel(
    tokens, attended, cotangent, valid, out_weight, bias_out, gain, shift, bias_down, up_own,
    up_other, bias_up, down_own, down_other, layer_out, grad_residual, grad_attended,
    grad_out_weight, vectors, grad_up_own, grad_up_other, grad_up_bias, grad_down_own,
    grad_down_other, staged, residual, output, grad_norm, normed, normed_t, grad_out, heads_in,
):
    step = pl.program_id(0)
    slots, piece, width = tokens.shape
    groups = attended.shape[0]
    rows = slots * piece
    padded = residual.shape[0]

    def stage(source):
        for s in range(slots):
            staged[s * piece : (s + 1) * piece, : source.shape[-1]] = source[s].astype(F32)

    @pl.when(step == 0)
    def _():
        if padded > rows:
            staged[rows:, :] = jnp.zeros((padded - rows, width), F32)
        for r in range(groups):
            stage(attended.at[r])
            heads_in[r] = staged[:, : attended.shape[-1]].astype(BF16)
        stage(cotangent)
        grad_out[...] = (staged[...] * valid[...]).astype(BF16)
        stage(tokens)
        total = staged[...] + bias_out[...]
        for r in range(groups):
            total = total + mm(heads_in[r], out_weight[r])
        residual[...] = total
        unit, _ = normalize(total)
        normed_here = (unit * gain[...] + shift[...]).astype(BF16)
        normed[...] = normed_here
        normed_t[...] = jnp.transpose(normed_here)
        output[...] = total + bias_down[...]
        grad_norm[...] = jnp.zeros_like(grad_norm)

    first = step < pl.num_programs(0) // 2
    up = jnp.where(first, up_own[...], up_other[...])
    down = jnp.where(first, down_own[...], down_other[...])
    hidden = mm(normed[...], up) + bias_up[...]
    share = 0.5 * (1.0 + lax.erf(hidden * np.float32(np.sqrt(0.5))))
    density = jnp.exp(-0.5 * hidden * hidden) * np.float32(1.0 / np.sqrt(2.0 * np.pi))
    activated = (hidden * share).astype(BF16)
    grad_hidden = (mm(grad_out[...], down, 1, 1) * (share + hidden * density)).astype(BF16)
    output[...] += mm(activated, down)
    grad_norm[...] += mm(grad_hidden, up, 1, 1)
    grad_up = mm(normed_t[...], grad_hidden).astype(BF16)
    grad_down = mm(activated, grad_out[...], 0, 0).astype(BF16)

    @pl.when(first)
    def _():
        grad_up_own[...] = grad_up
        grad_down_own[...] = grad_down

    @pl.when(jnp.logical_not(first))
    def _():
        grad_up_other[...] = grad_up
        grad_down_other[...] = grad_down

    grad_up_bias[...] = jnp.sum(grad_hidden.astype(F32), axis=0, keepdims=True)

    @pl.when(step == pl.num_programs(0) - 1)
    def _():
        staged[...] = output[...] * valid[...]
        for s in range(slots):
            layer_out[s] = staged[s * piece : (s + 1) * piece, :].astype(BF16)
        grad_low = grad_out[...].astype(F32)
        unit, factor = normalize(residual[...])
        back = grad_norm[...]
        scaled = back * gain[...]
        mean_scaled = jnp.mean(scaled, axis=-1, keepdims=True)
        mean_product = jnp.mean(scaled * unit, axis=-1, keepdims=True)
        total = grad_low + factor * (scaled - mean_scaled - unit * mean_product)
        staged[...] = total
        for s in range(slots):
            grad_residual[s] = staged[s * piece : (s + 1) * piece, :]
        branch = total.astype(BF16)
        vectors[0:1, :] = jnp.sum(back * unit, axis=0, keepdims=True)
        vectors[1:2, :] = jnp.sum(back, axis=0, keepdims=True)
        vectors[2:3, :] = jnp.sum(branch.astype(F32), axis=0, keepdims=True)
        vectors[3:4, :] = jnp.sum(grad_low, axis=0, keepdims=True)
        vectors[4:8, :] = jnp.zeros((4, width), F32)
        for r in range(groups):
            grad_out_weight[r] = mm(heads_in[r], branch, 0, 0).astype(BF16)
            staged[:, : attended.shape[-1]] = mm(branch, out_weight[r], 1, 1)
            for s in range(slots):
                grad_attended[r, s] = staged[
                    s * piece : (s + 1) * piece, : attended.shape[-1]
                ].astype(BF16)


def feed_forward(
    tokens, attended, cotangent, valid, out_weight, bias_out, gain, shift, bias_down, up_own,
    up_other, bias_up, down_own, down_other,
):
    slots, piece, width = tokens.shape
    groups, head_width = attended.shape[0], attended.shape[-1]
    ff = 2 * up_own.shape[1]
    chunk = 384
    half = ff // 2 // chunk
    padded = round_up(slots * piece, 16)
    whole = lambda shape: pl.BlockSpec(
        shape, lambda i: (0,) * len(shape), pipeline_mode=pl.Buffered(1)
    )
    own = lambda i: jnp.minimum(i, half - 1)
    other = lambda i: jnp.maximum(i - half, 0)
    by_columns = [pl.BlockSpec((width, chunk), lambda i, at=at: (0, at(i))) for at in (own, other)]
    by_rows = [pl.BlockSpec((chunk, width), lambda i, at=at: (at(i), 0)) for at in (own, other)]
    bias_block = pl.BlockSpec((1, chunk), lambda i: (0, i))
    row = whole((1, width))
    return pl.pallas_call(
        mlp_kernel,
        grid=(ff // chunk,),
        in_specs=[
            whole(tokens.shape),
            whole(attended.shape),
            whole(cotangent.shape),
            whole((padded, 1)),
            whole(out_weight.shape),
            row,
            row,
            row,
            row,
            *by_columns,
            bias_block,
            *by_rows,
        ],
        out_specs=[
            whole(tokens.shape),
            whole(tokens.shape),
            whole(attended.shape),
            whole(out_weight.shape),
            whole((8, width)),
            *by_columns,
            bias_block,
            *by_rows,
        ],
        out_shape=[
            jax.ShapeDtypeStruct(tokens.shape, BF16),
            jax.ShapeDtypeStruct(tokens.shape, F32),
            jax.ShapeDtypeStruct(attended.shape, BF16),
            jax.ShapeDtypeStruct(out_weight.shape, BF16),
            jax.ShapeDtypeStruct((8, width), F32),
            jax.ShapeDtypeStruct(up_own.shape, BF16),
            jax.ShapeDtypeStruct(up_own.shape, BF16),
            jax.ShapeDtypeStruct((1, ff), F32),
            jax.ShapeDtypeStruct(down_own.shape, BF16),
            jax.ShapeDtypeStruct(down_own.shape, BF16),
        ],
        scratch_shapes=[
            pltpu.VMEM((padded, width), F32),
            pltpu.VMEM((padded, width), F32),
            pltpu.VMEM((padded, width), F32),
            pltpu.VMEM((padded, width), F32),
            pltpu.VMEM((padded, width), BF16),
            pltpu.VMEM((width, padded), BF16),
            pltpu.VMEM((padded, width), BF16),
            pltpu.VMEM((groups, padded, head_width), BF16),
        ],
        compiler_params=pltpu.CompilerParams(
            vmem_limit_bytes=VMEM_BYTES, dimension_semantics=("arbitrary",)
        ),
        cost_estimate=pl.CostEstimate(
            flops=55 * 10**9, bytes_accessed=40 * 10**6, transcendentals=2 * padded * ff
        ),
        name="feed_forward",
    )(
        tokens, attended, cotangent, valid, out_weight, bias_out, gain, shift, bias_down, up_own,
        up_other, bias_up, down_own, down_other,
    )


def xor_send(block, axis, bits):
    n = lax.axis_size(axis)
    return lax.ppermute(block, axis, [(i, i ^ bits) for i in range(n)])


INNER = 2


def outer_send(block, shift):
    outer = lax.axis_size("img") // INNER
    return lax.ppermute(
        block,
        "img",
        [
            (z * INNER + y, ((z + shift) % outer) * INNER + y)
            for z in range(outer)
            for y in range(INNER)
        ],
    )


def few_devices():
    return lax.axis_size("img") <= 16


def place_outer(block, arrived):
    outer = lax.axis_size("img") // INNER
    z = lax.axis_index("img") // INNER
    placed = jnp.zeros((outer,) + block.shape, block.dtype)
    for k, part in enumerate([block] + arrived):
        placed = lax.dynamic_update_slice_in_dim(placed, part[None], (z + outer - k) % outer, 0)
    return placed


def gather_inner(placed):
    other = xor_send(placed, "img", 1)
    first = (lax.axis_index("img") & 1) == 0
    both = jnp.stack([jnp.where(first, placed, other), jnp.where(first, other, placed)], axis=1)
    return both.reshape((-1,) + placed.shape[1:])


def start_gather(block):
    if not few_devices():
        return lax.all_gather(block, "img", axis=0), None
    outer = lax.axis_size("img") // INNER
    return block, [outer_send(block, k) for k in range(1, outer)]


def end_gather(block, arrived):
    if arrived is None:
        return block
    return gather_inner(place_outer(block, arrived))


def reduce_inner(parts):
    outer = lax.axis_size("img") // INNER
    split = parts.reshape((outer, INNER) + parts.shape[1:])
    me = lax.axis_index("img") % INNER
    send = lax.dynamic_index_in_dim(split, 1 - me, 1, keepdims=False)
    keep = lax.dynamic_index_in_dim(split, me, 1, keepdims=False)
    return keep.astype(F32) + xor_send(send, "img", 1).astype(F32)


def reduce_outer(sums):
    outer = sums.shape[0]
    z = lax.axis_index("img") // INNER
    total = lax.dynamic_index_in_dim(sums, z, 0, keepdims=False)
    for k in range(1, outer):
        send = lax.dynamic_index_in_dim(sums, (z + k) % outer, 0, keepdims=False)
        total = total + outer_send(send.astype(BF16), k).astype(F32)
    return total


def scatter_img(parts):
    return lax.psum_scatter(parts, "img", scatter_dimension=0, tiled=False).astype(F32)


def sum_vectors(parts):
    arrived = [xor_send(parts, "seq", r) for r in range(1, 4)]
    parts = (parts + arrived[0]) + (arrived[1] + arrived[2])
    if not few_devices():
        return lax.psum_scatter(parts, "img", scatter_dimension=0, tiled=False)
    outer = lax.axis_size("img") // INNER
    img = lax.axis_index("img")
    z, y = img // INNER, img % INNER
    split = parts.reshape(outer, INNER, -1)
    mine = lax.dynamic_index_in_dim(split, z, 0, keepdims=False)
    for k in range(1, outer):
        mine = mine + outer_send(
            lax.dynamic_index_in_dim(split, (z + k) % outer, 0, keepdims=False), k
        )
    send = lax.dynamic_index_in_dim(mine, 1 - y, 0, keepdims=False)
    return lax.dynamic_index_in_dim(mine, y, 0, keepdims=False) + xor_send(send, "img", 1)


def in_pair_order(own, other, axis):
    first = (lax.axis_index("seq") & 1) == 0
    return jnp.where(
        first, jnp.concatenate([own, other], axis), jnp.concatenate([other, own], axis)
    )


def half_of(block, axis, which):
    size = block.shape[axis] // 2
    return lax.dynamic_slice_in_dim(block, which * size, size, axis)


def over_pieces(total):
    low = total.astype(BF16)
    low = (low.astype(F32) + xor_send(low, "seq", 2).astype(F32)).astype(BF16)
    return low, xor_send(low, "seq", 1)


def local(
    tokens,
    cotangent,
    images_held,
    piece_rows,
    norm_gain,
    norm_shift,
    qkv_weight,
    qkv_bias,
    out_weight,
    out_bias,
    mlp_gain,
    mlp_shift,
    up_weight,
    up_bias,
    down_weight,
    down_bias,
):
    slot_count, piece_size, model_width = tokens.shape
    n_seq = lax.axis_size("seq")
    n_img = lax.axis_size("img")
    me = lax.axis_index("seq")
    pair_me = me & 1
    own_img = lax.axis_index("img")
    row_count = slot_count * piece_size
    heads_here = HEADS // n_seq
    group = 3 * D // n_seq
    group_width = heads_here * HEAD_DIM
    shard = D // n_img
    ff = up_weight.shape[1]
    ff_half = ff // n_img // 2
    blocks = 3 * heads_here

    rows_of = piece_rows[me ^ jnp.arange(n_seq)]
    key_valid = (jnp.arange(piece_size)[None, :] < rows_of[:, None]).reshape(n_seq * piece_size)
    live_slots = jnp.arange(slot_count) < images_held[0]
    valid_rows = (live_slots[:, None] & key_valid[None, :piece_size]).reshape(row_count)
    valid_rows = jnp.pad(valid_rows, (0, round_up(row_count, 16) - row_count))
    valid_rows = valid_rows.astype(F32)[:, None]
    key_mask = jnp.where(
        key_valid[:, None] | (jnp.arange(LANES) != HEAD_DIM)[None, :], 0.0, NEG
    ).astype(F32)

    small = jnp.concatenate(
        [norm_gain, norm_shift, out_bias, mlp_gain, mlp_shift, down_bias, qkv_bias, up_bias]
    )
    small_rows = round_up(-(-small.shape[0] // group), 16)
    small = jnp.pad(small, (0, small_rows * group - small.shape[0])).reshape(small_rows, group)
    my_columns = lax.dynamic_slice_in_dim(qkv_weight, me * group, group, 1)
    first_part, first_arrived = start_gather(jnp.concatenate([my_columns, small], axis=0))

    slot_tokens = []
    for slot in range(slot_count):
        own = tokens[slot]
        pair = xor_send(own, "seq", 1)
        across = xor_send(own, "seq", 2)
        slot_tokens.append([own, pair, across, xor_send(across, "seq", 1)])
    down_own = lax.all_gather(half_of(down_weight, 0, pair_me), "img", axis=0)
    down_own = down_own.reshape(-1, model_width)

    first_set = end_gather(first_part, first_arrived)
    qkv_cols = first_set[:, :shard].reshape(model_width, group)
    params = first_set[:, shard:].reshape(n_img, -1).astype(F32)

    def param(start, width):
        return params[:, start * shard : (start + width) * shard].reshape(-1)

    gain_first, shift_first, bias_out = param(0, 1)[None], param(1, 1)[None], param(2, 1)[None]
    gain_second, shift_second, bias_down = param(3, 1)[None], param(4, 1)[None], param(5, 1)[None]
    pair_bias, bias_up = param(6, 2), param(8, 4).reshape(n_img, 2, ff_half)
    bias_up = jnp.concatenate(
        [
            lax.dynamic_index_in_dim(bias_up, which, 1, keepdims=False).reshape(1, -1)
            for which in (pair_me, 1 - pair_me)
        ],
        axis=1,
    )

    scale = np.ones((blocks, 1, 1), np.float32)
    scale[0::3] = HEAD_DIM**-0.5
    ones = np.zeros((blocks, 1, LANES), np.float32)
    ones[0::3, 0, HEAD_DIM] = 1.0
    ones[2::3, 0, HEAD_DIM] = 1.0
    lanes = ((0, 0), (0, 0), (0, LANES - HEAD_DIM))
    head_weight = jnp.swapaxes(qkv_cols.reshape(model_width, blocks, HEAD_DIM), 0, 1)
    head_weight = jnp.pad(head_weight * scale.astype(BF16), lanes)
    paired = lax.dynamic_slice_in_dim(
        pair_bias.reshape(HEADS, 2, HEAD_DIM), me * heads_here, heads_here, 0
    )
    head_bias = jnp.concatenate(
        [paired[:, :1], jnp.zeros((heads_here, 1, HEAD_DIM), F32), paired[:, 1:]], axis=1
    ).reshape(blocks, 1, HEAD_DIM)
    head_bias = jnp.pad(head_bias * scale, lanes) + ones

    my_up = lax.dynamic_index_in_dim(
        up_weight.reshape(shard, n_img, 2, ff_half), pair_me, 2, keepdims=False
    ).reshape(shard, -1)
    second_part, second_arrived = start_gather(
        jnp.concatenate([my_up, half_of(out_weight, 1, pair_me)], axis=1)
    )

    slot_normed, slot_qkv, slot_attended = [], [], []
    for slot in range(slot_count):
        after = ()
        if slot == 1 and second_arrived is not None:
            after = tuple(second_arrived)
        normed, qkv_rows, attended = slot_forward(
            slot_tokens[slot], gain_first, shift_first, head_weight, head_bias, key_mask, after
        )
        slot_normed.append(normed)
        slot_qkv.append(qkv_rows)
        slot_attended.append(
            [attended[0]] + [xor_send(attended[r], "seq", r) for r in range(1, n_seq)]
        )
    second_set = end_gather(second_part, second_arrived).reshape(model_width, -1)
    up_own, out_own = second_set[:, : ff // 2], second_set[:, ff // 2 :]
    up_other = xor_send(up_own, "seq", 1)
    down_other = xor_send(down_own, "seq", 1)
    out_full = in_pair_order(out_own, xor_send(out_own, "seq", 1), 1)
    out_full = out_full.reshape(n_seq, group_width, model_width)
    out_groups = jnp.stack(
        [lax.dynamic_index_in_dim(out_full, me ^ r, 0, keepdims=False) for r in range(n_seq)]
    )
    attended_groups = jnp.stack(
        [jnp.stack([parts[r] for parts in slot_attended]) for r in range(n_seq)]
    )

    (
        layer_out,
        grad_residual,
        grad_attended,
        grad_out_groups,
        vectors,
        grad_up_own,
        grad_up_other,
        grad_up_bias,
        grad_down_own,
        grad_down_other,
    ) = feed_forward(
        tokens,
        attended_groups,
        cotangent,
        valid_rows,
        out_groups,
        bias_out,
        gain_second,
        shift_second,
        bias_down,
        up_own,
        up_other,
        bias_up,
        down_own,
        down_other,
    )

    slot_grads = []
    for slot in range(slot_count):
        slot_grads.append(
            [grad_attended[0, slot]]
            + [xor_send(grad_attended[r, slot], "seq", r) for r in range(1, n_seq)]
        )

    down_sum = grad_down_own.astype(F32) + xor_send(grad_down_other, "seq", 1).astype(F32)
    own_down = scatter_img(down_sum.astype(BF16).reshape(n_img, ff_half, model_width))
    up_sum = grad_up_own.astype(F32) + xor_send(grad_up_other, "seq", 1).astype(F32)
    grad_out_weight = jnp.concatenate(
        [lax.dynamic_index_in_dim(grad_out_groups, me ^ r, 0, keepdims=False) for r in range(n_seq)],
        axis=0,
    )
    out_sum = half_of(grad_out_weight, 1, pair_me).astype(F32) + xor_send(
        half_of(grad_out_weight, 1, 1 - pair_me), "seq", 1
    ).astype(F32)
    second_grads = jnp.concatenate([up_sum, out_sum], axis=1).astype(BF16)
    second_grads = second_grads.reshape(n_img, shard, -1)
    stages = [(), (), ()]
    if few_devices():
        sums = reduce_inner(second_grads)
        own_second = reduce_outer(sums)
        stages = [(), (sums,), (own_second,)]
    else:
        own_second = scatter_img(second_grads)

    grad_columns = jnp.zeros((model_width, group), F32)
    bias_sums = jnp.zeros((group,), F32)
    own_sums = []
    for slot in range(slot_count):
        grad_qkv = slot_backward(slot_grads[slot], slot_qkv[slot], stages[min(slot, 2)])
        partial_in = mm(grad_qkv, qkv_cols, 1, 1).reshape(n_seq, piece_size, model_width)
        low = partial_in.astype(BF16)
        pair = xor_send(low[1], "seq", 1).astype(F32)
        across = xor_send(low[3], "seq", 1).astype(F32)
        across = xor_send((partial_in[2] + across).astype(BF16), "seq", 2)
        own_sums.append(partial_in[0] + pair + across.astype(F32))
        grad_columns += mm(slot_normed[slot], grad_qkv, 0, 0)
        bias_sums += jnp.sum(grad_qkv.astype(F32), axis=0)
    columns = grad_columns.astype(BF16).reshape(n_img, shard, group)
    if few_devices():
        own_columns = reduce_outer(reduce_inner(columns))
    else:
        own_columns = scatter_img(columns)
    own_columns = own_columns.astype(BF16)

    grad_norm_first = jnp.concatenate(own_sums, axis=0)
    unit, factor = normalize(tokens.reshape(row_count, model_width).astype(F32))
    scaled = grad_norm_first * gain_first
    mean_scaled = jnp.mean(scaled, axis=-1, keepdims=True)
    mean_product = jnp.mean(scaled * unit, axis=-1, keepdims=True)
    grad_inputs = factor * (scaled - mean_scaled - unit * mean_product)
    tokens_grad = grad_residual + grad_inputs.reshape(grad_residual.shape)
    grad_norm_gain = jnp.sum(grad_norm_first * unit, axis=0)
    grad_norm_shift = jnp.sum(grad_norm_first, axis=0)

    by_sender = jnp.stack(
        [own_columns] + [xor_send(own_columns, "seq", r) for r in range(1, n_seq)]
    )
    share_qkv = jnp.concatenate(
        [lax.dynamic_index_in_dim(by_sender, me ^ g, 0, keepdims=False) for g in range(n_seq)],
        axis=1,
    ).astype(F32)
    second_low, second_other = over_pieces(own_second)
    up_low = second_low[:, : ff // 2].reshape(shard, n_img, 1, ff_half)
    up_there = second_other[:, : ff // 2].reshape(shard, n_img, 1, ff_half)
    share_up = in_pair_order(up_low, up_there, 2).reshape(shard, ff).astype(F32)
    share_out = in_pair_order(second_low[:, ff // 2 :], second_other[:, ff // 2 :], 1).astype(F32)
    share_down = in_pair_order(*over_pieces(own_down), 0).astype(F32)

    bias_sums = bias_sums.reshape(heads_here, 3, HEAD_DIM)
    grad_pairs = jnp.concatenate([bias_sums[:, :1], bias_sums[:, 2:]], axis=1).reshape(-1)
    grad_pairs = lax.dynamic_update_slice_in_dim(
        jnp.zeros((2 * D,), F32), grad_pairs, me * grad_pairs.shape[0], 0
    )
    up_halves = grad_up_bias.reshape(2, n_img, 1, ff_half)
    grad_up_bias = in_pair_order(up_halves[0], up_halves[1], 1).reshape(-1)
    all_vectors = [
        grad_norm_gain,
        grad_norm_shift,
        grad_pairs,
        vectors[2],
        vectors[0],
        vectors[1],
        grad_up_bias,
        vectors[3],
    ]
    mine = sum_vectors(jnp.concatenate([v.reshape(n_img, -1) for v in all_vectors], axis=1))
    shares, at = [], 0
    for v in all_vectors:
        size = v.shape[0] // n_img
        shares.append(mine[at : at + size])
        at += size
    return (
        layer_out,
        tokens_grad,
        shares[0],
        shares[1],
        share_qkv,
        shares[2],
        share_out,
        shares[3],
        shares[4],
        shares[5],
        share_up,
        shares[6],
        share_down,
        shares[7],
    )


def solution(mesh):
    placed = (
        P("img", "seq", None),
        P("img", "seq", None),
        P("img"),
        P(),
        P("img"),
        P("img"),
        P("img", None),
        P("img"),
        P("img", None),
        P("img"),
        P("img"),
        P("img"),
        P("img", None),
        P("img"),
        P("img", None),
        P("img"),
    )
    return jax.shard_map(
        local,
        mesh=mesh,
        in_specs=placed,
        out_specs=(
            P("img", "seq", None),
            P("img", "seq", None),
            P("img"),
            P("img"),
            P("img", None),
            P("img"),
            P("img", None),
            P("img"),
            P("img"),
            P("img"),
            P("img", None),
            P("img"),
            P("img", None),
            P("img"),
        ),
        check_vma=False,
    )
```

time: 674 us -> 510 us (0.76)
  matrix products: 251 us -> 19.8 us
  Pallas kernels: 0 us -> 170 us
  waiting for transfers between devices: 178 us -> 133 us
  local copies, waits for them, and re-layouts: 97.8 us -> 55.5 us
  other arithmetic: 87.4 us -> 49.3 us
  between operations: 4.32 us -> 16.2 us
  starting transfers between devices: 47.6 us -> 57.1 us
    dot_general x33 -> x6, matrix products: 218 us -> 19.8 us  [mm(): lax.dot_general(left, right, (((left_dim,), (right_dim,)), ((), ())), pre...]
    pallas_call x0 -> x7, Pallas kernels: none -> 170 us  [the longest x3 67.2 us: slot_backward(): pl.pallas_call(partial(backward_kernel, n_seq, heads, len(after)), in_spe...]
    ppermute x18 -> x15, waiting for transfers between devices: 94.1 us -> 52.2 us  [outer_send(): lax.ppermute(block, 'img', [(z * INNER + y, (z + shift) % outer * INNER +...]
    sub x3 -> x0, matrix products: 33.2 us -> none  [attend_forward(): probs = jax.nn.softmax(scores, axis=-1).astype(jnp.bfloat16)]
    convert_element_type x21 -> x12, other arithmetic: 31.3 us -> 15.2 us  [the longest x3 4.86 us: local(): across = xor_send((partial_in[2] + across).astype(BF16), 'seq', 2)]
    ppermute x18 -> x15, starting transfers between devices: 10.2 us -> 24.3 us  [outer_send(): lax.ppermute(block, 'img', [(z * INNER + y, (z + shift) % outer * INNER +...]
    convert_element_type x13 -> x6, local copies, waits for them, and re-layouts: 17.4 us -> 5.69 us  [the longest x2 3.86 us: local(): share_up = in_pair_order(up_low, up_there, 2).reshape(shard, ff).astype(F32)]
    reduce_sum x20 -> x11, other arithmetic: 21.5 us -> 11.8 us  [the longest x4 6.18 us: local(): grad_norm_shift = jnp.sum(grad_norm_first, axis=0)]
  transfers between devices with their start and end apart: 80 -> 74, of which waited for: 30 -> 29; matrix products, arithmetic and copies ran while one was open for 55% -> 22% of each run, Pallas kernels for 0% -> 24%
where the time goes in v2:
time: 510 us; the launch traced here: 501 us
  Pallas kernels  170 us (33%)
  waiting for transfers between devices  133 us (26%)
  starting transfers between devices  57.1 us (11%)
  local copies, waits for them, and re-layouts  55.5 us (11%)
  other arithmetic  49.3 us (10%)
  matrix products  19.8 us (4%)
  between operations  16.2 us (3%)
    ppermute x57, waiting for transfers between devices, xor_send(): return lax.ppermute(block, axis, [(i, i ^ bits) for i in range(n)])  81 us
    pallas_call x3, Pallas kernels, slot_backward(): pl.pallas_call(partial(backward_kernel, n_seq, heads, len(after)), in_spe...  67.2 us
    ppermute x15, waiting for transfers between devices, outer_send(): lax.ppermute(block, 'img', [(z * INNER + y, (z + shift) % outer * INNER +...  52.2 us
    pallas_call x3, Pallas kernels, slot_forward(): pl.pallas_call(partial(forward_kernel, n_seq, heads, len(after)), in_spec...  52.2 us
    pallas_call x1, Pallas kernels, feed_forward(): pl.pallas_call(mlp_kernel, grid=(ff // chunk,), in_specs=[whole(tokens.sh...  50.7 us
    ppermute x57, starting transfers between devices, xor_send(): return lax.ppermute(block, axis, [(i, i ^ bits) for i in range(n)])  32.7 us
    ppermute x15, starting transfers between devices, outer_send(): lax.ppermute(block, 'img', [(z * INNER + y, (z + shift) % outer * INNER +...  24.3 us
    dot_general x6, matrix products, mm(): lax.dot_general(left, right, (((left_dim,), (right_dim,)), ((), ())), pre...  19.8 us
  transfers between devices with their start and end apart: 74, of which 29 were waited for; matrix products, arithmetic and copies ran while one was open for 22% of the time, Pallas kernels for 24%

profile of v2, /device:TPU:0, one launch (start us, length us, event | category | flops | bytes accessed | tf_op | source)
XLA Modules:
  0.0 501.1 jit_solution(11166680587646248666)
XLA Ops:
  14.0 3.0 collective-permute-start.10
  30.6 24.2 %collective-permute-done.3 = bf16[112,576]{1,0:T(8,128)(2,1)} collective-permute-done((bf16[112,576]{1,0:T(8,128)(2,1)S(1)}, bf16[112,576]{1,0:T(8,128)(2,1)}, u32[]{:S(2)}, u32[]{:S(2)}) %collective-permute-start.3) | collective-permute-done | bytes 129056 | tf_op jit(solution)/shard_map/ppermute | solution.py:377
  55.7 14.8 %collective-permute-done.4 = bf16[112,576]{1,0:T(8,128)(2,1)} collective-permute-done((bf16[112,576]{1,0:T(8,128)(2,1)S(1)}, bf16[112,576]{1,0:T(8,128)(2,1)}, u32[]{:S(2)}, u32[]{:S(2)}) %collective-permute-start.4) | collective-permute-done | bytes 129056 | tf_op jit(solution)/shard_map/ppermute | solution.py:377
  72.9 7.2 %collective-permute-done.5 = bf16[112,576]{1,0:T(8,128)(2,1)S(1)} collective-permute-done((bf16[112,576]{1,0:T(8,128)(2,1)S(1)}, bf16[112,576]{1,0:T(8,128)(2,1)S(1)}, u32[]{:S(2)}, u32[]{:S(2)}) %collective-permute-start.5) | collective-permute-done | bytes 129056 | tf_op jit(solution)/shard_map/ppermute | solution.py:377
  85.1 11.8 %collective-permute-done.6 = bf16[4,112,576]{2,1,0:T(8,128)(2,1)S(1)} collective-permute-done((bf16[4,112,576]{2,1,0:T(8,128)(2,1)S(1)}, bf16[4,112,576]{2,1,0:T(8,128)(2,1)S(1)}, u32[]{:S(2)}, u32[]{:S(2)}) %collective-permute-start.6) | collective-permute-done | bytes 516128 | tf_op jit(solution)/shard_map/ppermute | solution.py:369
  110.0 17.4 %slot_forward.4 = (bf16[1056,768]{1,0:T(8,128)(2,1)}, bf16[9,1152,128]{2,1,0:T(8,128)(2,1)}, bf16[4,264,192]{2,1,0:T(8,128)(2,1)}) custom-call(bf16[264,768]{1,0:T(8,128)(2,1)} %get-tuple-element.99.refs_0_, bf16[264,768]{1,0:T(8,128)(2,1)} %collective-permute-done.7.refs_1_, bf16[264,768]{1,0:T(8,128)(2,1)} %collective-permute-done.8.refs_2_, ...), custom_call_target="tpu_custom_call" | custom-call | flops 20000000000 | bytes 12000000 | tf_op jit(solution)/shard_map/slot_forward/pallas_call | solution.py:109
  127.4 17.3 %slot_forward.3 = (bf16[1056,768]{1,0:T(8,128)(2,1)}, bf16[9,1152,128]{2,1,0:T(8,128)(2,1)}, bf16[4,264,192]{2,1,0:T(8,128)(2,1)}) custom-call(bf16[264,768]{1,0:T(8,128)(2,1)} %get-tuple-element.97.refs_0_, bf16[264,768]{1,0:T(8,128)(2,1)} %collective-permute-done.refs_1_, bf16[264,768]{1,0:T(8,128)(2,1)} %collective-permute-done.1.refs_2_, ...), custom_call_target="tpu_custom_call" | custom-call | flops 20000000000 | bytes 12000000 | tf_op jit(solution)/shard_map/slot_forward/pallas_call | solution.py:109
  150.3 17.5 %slot_forward.5 = (bf16[1056,768]{1,0:T(8,128)(2,1)}, bf16[9,1152,128]{2,1,0:T(8,128)(2,1)}, bf16[4,264,192]{2,1,0:T(8,128)(2,1)}) custom-call(bf16[264,768]{1,0:T(8,128)(2,1)} %get-tuple-element.98.refs_0_, bf16[264,768]{1,0:T(8,128)(2,1)} %copy-done.46, bf16[264,768]{1,0:T(8,128)(2,1)} %collective-permute-done.14.refs_2_, ...), custom_call_target="tpu_custom_call" | custom-call | flops 20000000000 | bytes 12000000 | tf_op jit(solution)/shard_map/slot_forward/pallas_call | solution.py:109
  177.4 3.5 collective-permute-done.19
  198.1 50.7 %feed_forward.1 = (bf16[3,264,768]{2,1,0:T(8,128)(2,1)}, f32[3,264,768]{2,1,0:T(8,128)}, bf16[4,3,264,192]{3,2,1,0:T(8,128)(2,1)}, bf16[4,192,768]{2,1,0:T(8,128...) custom-call(bf16[3,264,768]{2,1,0:T(8,128)(2,1)} %tokens.1, ...), custom_call_target="tpu_custom_call" | custom-call | flops 54999998464 | bytes 40000000 | tf_op jit(solution)/shard_map/feed_forward/pallas_call | solution.py:305
  253.8 4.5 collective-permute-done.30.refs_2_
  260.7 22.4 %slot_backward.3 = bf16[1056,576]{1,0:T(8,128)(2,1)} custom-call(bf16[264,192]{1,0:T(8,128)(2,1)} %get-tuple-element.92.refs_0_, bf16[264,192]{1,0:T(8,128)(2,1)} %copy-done.49, bf16[264,192]{1,0:T(8,128)(2,1)} %copy-done.50, bf16[264,192]{1,0:T(8,128)(2,1)} %copy-done.51, bf16[9,1152,128]{2,1,0:T(8,128)(2,1)} %get-tuple-element.39.refs_4_, ...), custom_call_target="tpu_custom_call" | custom-call | flops 28000000000 | bytes 8000000 | tf_op jit(solution)/shard_map/slot_backward/pallas_call | solution.py:178
  283.1 4.6 fusion.66
  307.8 3.8 add_convert_fusion
  311.6 25.0 %collective-permute-done.40 = bf16[4,96,1920]{2,1,0:T(8,128)(2,1)} collective-permute-done((bf16[4,96,1920]{2,1,0:T(8,128)(2,1)S(1)}, bf16[4,96,1920]{2,1,0:T(8,128)(2,1)}, u32[]{:S(2)}, u32[]{:S(2)}) %collective-permute-start.40) | collective-permute-done | bytes 1474592 | tf_op jit(solution)/shard_map/ppermute | solution.py:369
  341.6 5.1 %collective-permute-start.48 = (bf16[96,1920]{1,0:T(8,128)(2,1)S(1)}, bf16[96,1920]{1,0:T(8,128)(2,1)S(1)}, u32[]{:S(2)}, u32[]{:S(2)}) collective-permute-start(bf16[96,1920]{1,0:T(8,128)(2,1)S(1)} %get-tuple-element.74), channel_id=1, source_target_pairs={{0,16},{4,20},{8,24},{12,28},{16,0},{20,4},{24,8},{28,12},{1,17},{... | collective-permute-start | bytes 1105928 | tf_op jit(solution)/shard_map/ppermute | solution.py:377
  346.8 22.4 %slot_backward.4 = bf16[1056,576]{1,0:T(8,128)(2,1)} custom-call(bf16[264,192]{1,0:T(8,128)(2,1)} %get-tuple-element.89.refs_0_, bf16[264,192]{1,0:T(8,128)(2,1)} %collective-permute-done.35.refs_1_, bf16[264,192]{1,0:T(8,128)(2,1)} %collective-permute-done.36.refs_2_, bf16[264,192]{1,0:T(8,128)(2,1)} %collective-permute-done.37.refs_3_, ...), custom_call_target="tpu_custom_call" | custom-call | flops 28000000000 | bytes 8000000 | tf_op jit(solution)/shard_map/slot_backward/pallas_call | solution.py:178
  369.2 4.5 fusion.65
  384.5 22.3 %slot_backward.5 = bf16[1056,576]{1,0:T(8,128)(2,1)} custom-call(bf16[264,192]{1,0:T(8,128)(2,1)} %get-tuple-element.85.refs_0_, bf16[264,192]{1,0:T(8,128)(2,1)} %collective-permute-done.44.refs_1_, bf16[264,192]{1,0:T(8,128)(2,1)} %copy-done.47, bf16[264,192]{1,0:T(8,128)(2,1)} %copy-done.48, f32[96,1920]{1,0:T(8,128)} %get-tuple-element.65.refs_4_, ...), custom_call_target="tpu_custom_call" | custom-call | flops 28000000000 | bytes 8000000 | tf_op jit(solution)/shard_map/slot_backward/pallas_call | solution.py:178
  408.6 3.2 fusion.64
  423.6 6.9 %collective-permute-done.60 = bf16[4,96,576]{2,1,0:T(8,128)(2,1)} collective-permute-done((bf16[4,96,576]{2,1,0:T(8,128)(2,1)}, bf16[4,96,576]{2,1,0:T(8,128)(2,1)}, u32[]{:S(2)}, u32[]{:S(2)}) %collective-permute-start.60) | collective-permute-done | bytes 442400 | tf_op jit(solution)/shard_map/ppermute | solution.py:369
  439.9 3.1 collective-permute-done.62
  480.2 4.8 collective-permute-done.70
  486.1 4.7 fusion.8
  (421 shorter events, 180.1 us)
Async XLA Ops:
  7.2 142.4 %all-gather.3.cloned.1.call-start = ((), (), s32[]{:S(2)}) async-start(), calls=%async_computation.2 | async-start | bytes 2654208 | tf_op jit(solution)/shard_map/all_gather | solution.py:537
  14.0 66.2 %collective-permute-start.10 = (bf16[96,1920]{1,0:T(8,128)(2,1)}, bf16[96,1920]{1,0:T(8,128)(2,1)S(1)}, u32[]{:S(2)}, u32[]{:S(2)}) collective-permute-start(bf16[96,1920]{1,0:T(8,128)(2,1)} %pad_maximum_fusion.7), channel_id=1, source_target_pairs={{0,8},{4,12},{8,16},{12,20},{16,24},{20,28},{24,0},{28,4},{1,9},{5... | collective-permute-start | bytes 1105928 | tf_op jit(solution)/shard_map/ppermute | solution.py:377
  17.0 64.8 %collective-permute-start.11 = (bf16[96,1920]{1,0:T(8,128)(2,1)}, bf16[96,1920]{1,0:T(8,128)(2,1)S(1)}, u32[]{:S(2)}, u32[]{:S(2)}) collective-permute-start(bf16[96,1920]{1,0:T(8,128)(2,1)} %pad_maximum_fusion.7), channel_id=1, source_target_pairs={{0,16},{4,20},{8,24},{12,28},{16,0},{20,4},{24,8},{28,12},{1,17},{... | collective-permute-start | bytes 1105928 | tf_op jit(solution)/shard_map/ppermute | solution.py:377
  19.6 63.8 %collective-permute-start.12 = (bf16[96,1920]{1,0:T(8,128)(2,1)}, bf16[96,1920]{1,0:T(8,128)(2,1)}, u32[]{:S(2)}, u32[]{:S(2)}) collective-permute-start(bf16[96,1920]{1,0:T(8,128)(2,1)} %pad_maximum_fusion.7), channel_id=1, source_target_pairs={{0,24},{4,28},{8,0},{12,4},{16,8},{20,12},{24,16},{28,20},{1,25},{... | collective-permute-start | bytes 1105928 | tf_op jit(solution)/shard_map/ppermute | solution.py:377
  23.0 47.5 %collective-permute-start.4 = (bf16[112,576]{1,0:T(8,128)(2,1)S(1)}, bf16[112,576]{1,0:T(8,128)(2,1)}, u32[]{:S(2)}, u32[]{:S(2)}) collective-permute-start(bf16[112,576]{1,0:T(8,128)(2,1)S(1)} %pad_maximum_fusion.8), channel_id=1, source_target_pairs={{0,16},{4,20},{8,24},{12,28},{16,0},{20,4},{24,8},{28,12},{1,17},{... | collective-permute-start | bytes 387080 | tf_op jit(solution)/shard_map/ppermute | solution.py:377
  24.1 452.2 %reduce-scatter.2.cloned.1.call-start = ((), (), s32[]{:S(2)}) async-start(), calls=%async_computation.1 | async-start | bytes 2654208 | tf_op jit(solution)/shard_map/reduce_scatter | solution.py:441
  83.4 44.0 %collective-permute-start = (bf16[264,768]{1,0:T(8,128)(2,1)}, bf16[264,768]{1,0:T(8,128)(2,1)}, u32[]{:S(2)}, u32[]{:S(2)}) collective-permute-start(bf16[264,768]{1,0:T(8,128)(2,1)} %get-tuple-element.97.refs_0_), channel_id=1, source_target_pairs={{0,1},{1,0},{2,3},{3,2},{4,5},{5,4},{6,7},{7,6},{8,9},{9,8},{10,11... | collective-permute-start | bytes 1216520 | tf_op jit(solution)/shard_map/ppermute | solution.py:369
  107.4 42.1 %collective-permute-start.13 = (bf16[264,768]{1,0:T(8,128)(2,1)}, bf16[264,768]{1,0:T(8,128)(2,1)S(1)}, u32[]{:S(2)}, u32[]{:S(2)}) collective-permute-start(bf16[264,768]{1,0:T(8,128)(2,1)} %get-tuple-element.98.refs_0_), channel_id=1, source_target_pairs={{0,1},{1,0},{2,3},{3,2},{4,5},{5,4},{6,7},{7,6},{8,9},{9,8},{10,11... | collective-permute-start | bytes 1216520 | tf_op jit(solution)/shard_map/ppermute | solution.py:369
  107.9 39.4 %collective-permute-start.25 = (bf16[4,96,1920]{2,1,0:T(8,128)(2,1)S(1)}, bf16[4,96,1920]{2,1,0:T(8,128)(2,1)S(1)}, u32[]{:S(2)}, u32[]{:S(2)}) collective-permute-start(bf16[4,96,1920]{2,1,0:T(8,128)(2,1)S(1)} %copy-done.11), channel_id=1, source_target_pairs={{0,4},{4,0},{8,12},{12,8},{16,20},{20,16},{24,28},{28,24},{1,5},{5... | collective-permute-start | bytes 4423688 | tf_op jit(solution)/shard_map/ppermute | solution.py:369
  109.5 40.5 %collective-permute-start.15 = (bf16[264,768]{1,0:T(8,128)(2,1)}, bf16[264,768]{1,0:T(8,128)(2,1)}, u32[]{:S(2)}, u32[]{:S(2)}) collective-permute-start(bf16[264,768]{1,0:T(8,128)(2,1)} %collective-permute-done.14.refs_2_), channel_id=1, source_target_pairs={{0,1},{1,0},{2,3},{3,2},{4,5},{5,4},{6,7},{7,6},{8,9},{9,8},{10,11... | collective-permute-start | bytes 1216520 | tf_op jit(solution)/shard_map/ppermute | solution.py:369
  149.5 48.6 %collective-permute-start.27 = (bf16[768,1536]{1,0:T(8,128)(2,1)}, bf16[768,1536]{1,0:T(8,128)(2,1)}, u32[]{:S(2)}, u32[]{:S(2)}) collective-permute-start(bf16[768,1536]{1,0:T(8,128)(2,1)} %slice.324.up_own), channel_id=1, source_target_pairs={{0,1},{1,0},{2,3},{3,2},{4,5},{5,4},{6,7},{7,6},{8,9},{9,8},{10,11... | collective-permute-start | bytes 7077896 | tf_op jit(solution)/shard_map/ppermute | solution.py:369
  149.6 48.6 %collective-permute-start.28 = (bf16[1536,768]{1,0:T(8,128)(2,1)}, bf16[1536,768]{1,0:T(8,128)(2,1)}, u32[]{:S(2)}, u32[]{:S(2)}) collective-permute-start(bf16[1536,768]{1,0:T(8,128)(2,1)} %all-gather.3.cloned.1.call-done.down_own), channel_id=1, source_target_pairs={{0,1},{1,0},{2,3},{3,2},{4,5},{5,4},{6,7},{7,6},{8,9},{9,8},{10,11... | collective-permute-start | bytes 7077896 | tf_op jit(solution)/shard_map/ppermute | solution.py:369
  248.8 57.8 %collective-permute-start.69 = (bf16[1536,768]{1,0:T(8,128)(2,1)}, bf16[1536,768]{1,0:T(8,128)(2,1)}, u32[]{:S(2)}, u32[]{:S(2)}) collective-permute-start(bf16[1536,768]{1,0:T(8,128)(2,1)} %get-tuple-element.51), channel_id=1, source_target_pairs={{0,1},{1,0},{2,3},{3,2},{4,5},{5,4},{6,7},{7,6},{8,9},{9,8},{10,11... | collective-permute-start | bytes 7077896 | tf_op jit(solution)/shard_map/ppermute | solution.py:369
  250.3 43.7 %collective-permute-start.38 = (bf16[768,1536]{1,0:T(8,128)(2,1)}, bf16[768,1536]{1,0:T(8,128)(2,1)}, u32[]{:S(2)}, u32[]{:S(2)}) collective-permute-start(bf16[768,1536]{1,0:T(8,128)(2,1)} %get-tuple-element.41), channel_id=1, source_target_pairs={{0,1},{1,0},{2,3},{3,2},{4,5},{5,4},{6,7},{7,6},{8,9},{9,8},{10,11... | collective-permute-start | bytes 7077896 | tf_op jit(solution)/shard_map/ppermute | solution.py:369
  289.3 51.2 %collective-permute-start.35 = (bf16[264,192]{1,0:T(8,128)(2,1)}, bf16[264,192]{1,0:T(8,128)(2,1)}, u32[]{:S(2)}, u32[]{:S(2)}) collective-permute-start(bf16[264,192]{1,0:T(8,128)(2,1)} %get-tuple-element.88), channel_id=1, source_target_pairs={{0,1},{1,0},{2,3},{3,2},{4,5},{5,4},{6,7},{7,6},{8,9},{9,8},{10,11... | collective-permute-start | bytes 304136 | tf_op jit(solution)/shard_map/ppermute | solution.py:369
  297.8 38.8 %collective-permute-start.40 = (bf16[4,96,1920]{2,1,0:T(8,128)(2,1)S(1)}, bf16[4,96,1920]{2,1,0:T(8,128)(2,1)}, u32[]{:S(2)}, u32[]{:S(2)}) collective-permute-start(bf16[4,96,1920]{2,1,0:T(8,128)(2,1)S(1)} %fusion.12), channel_id=1, source_target_pairs={{0,4},{4,0},{8,12},{12,8},{16,20},{20,16},{24,28},{28,24},{1,5},{5... | collective-permute-start | bytes 4423688 | tf_op jit(solution)/shard_map/ppermute | solution.py:369
  301.7 40.0 %collective-permute-start.36 = (bf16[264,192]{1,0:T(8,128)(2,1)}, bf16[264,192]{1,0:T(8,128)(2,1)}, u32[]{:S(2)}, u32[]{:S(2)}) collective-permute-start(bf16[264,192]{1,0:T(8,128)(2,1)} %get-tuple-element.87), channel_id=1, source_target_pairs={{0,2},{1,3},{2,0},{3,1},{4,6},{5,7},{6,4},{7,5},{8,10},{9,11},{10,... | collective-permute-start | bytes 304136 | tf_op jit(solution)/shard_map/ppermute | solution.py:369
  304.1 42.6 %collective-permute-start.37 = (bf16[264,192]{1,0:T(8,128)(2,1)}, bf16[264,192]{1,0:T(8,128)(2,1)}, u32[]{:S(2)}, u32[]{:S(2)}) collective-permute-start(bf16[264,192]{1,0:T(8,128)(2,1)} %get-tuple-element.86), channel_id=1, source_target_pairs={{0,3},{1,2},{2,1},{3,0},{4,7},{5,6},{6,5},{7,4},{8,11},{9,10},{10,... | collective-permute-start | bytes 304136 | tf_op jit(solution)/shard_map/ppermute | solution.py:369
  306.6 75.2 %collective-permute-start.44 = (bf16[264,192]{1,0:T(8,128)(2,1)S(1)}, bf16[264,192]{1,0:T(8,128)(2,1)}, u32[]{:S(2)}, u32[]{:S(2)}) collective-permute-start(bf16[264,192]{1,0:T(8,128)(2,1)S(1)} %copy-done.25), channel_id=1, source_target_pairs={{0,1},{1,0},{2,3},{3,2},{4,5},{5,4},{6,7},{7,6},{8,9},{9,8},{10,11... | collective-permute-start | bytes 304136 | tf_op jit(solution)/shard_map/ppermute | solution.py:369
  336.7 45.1 %collective-permute-start.45 = (bf16[264,192]{1,0:T(8,128)(2,1)S(1)}, bf16[264,192]{1,0:T(8,128)(2,1)S(1)}, u32[]{:S(2)}, u32[]{:S(2)}) collective-permute-start(bf16[264,192]{1,0:T(8,128)(2,1)S(1)} %copy-done.24), channel_id=1, source_target_pairs={{0,2},{1,3},{2,0},{3,1},{4,6},{5,7},{6,4},{7,5},{8,10},{9,11},{10,... | collective-permute-start | bytes 304136 | tf_op jit(solution)/shard_map/ppermute | solution.py:369
  340.5 38.0 %collective-permute-start.47 = (bf16[96,1920]{1,0:T(8,128)(2,1)S(1)}, bf16[96,1920]{1,0:T(8,128)(2,1)S(1)}, u32[]{:S(2)}, u32[]{:S(2)}) collective-permute-start(bf16[96,1920]{1,0:T(8,128)(2,1)S(1)} %get-tuple-element.72), channel_id=1, source_target_pairs={{0,8},{4,12},{8,16},{12,20},{16,24},{20,28},{24,0},{28,4},{1,9},{5... | collective-permute-start | bytes 1105928 | tf_op jit(solution)/shard_map/ppermute | solution.py:377
  341.6 36.8 %collective-permute-start.48 = (bf16[96,1920]{1,0:T(8,128)(2,1)S(1)}, bf16[96,1920]{1,0:T(8,128)(2,1)S(1)}, u32[]{:S(2)}, u32[]{:S(2)}) collective-permute-start(bf16[96,1920]{1,0:T(8,128)(2,1)S(1)} %get-tuple-element.74), channel_id=1, source_target_pairs={{0,16},{4,20},{8,24},{12,28},{16,0},{20,4},{24,8},{28,12},{1,17},{... | collective-permute-start | bytes 1105928 | tf_op jit(solution)/shard_map/ppermute | solution.py:377
  378.5 40.6 %collective-permute-start.42 = (bf16[264,768]{1,0:T(8,128)(2,1)}, bf16[264,768]{1,0:T(8,128)(2,1)}, u32[]{:S(2)}, u32[]{:S(2)}) collective-permute-start(bf16[264,768]{1,0:T(8,128)(2,1)} %get-tuple-element.94), channel_id=1, source_target_pairs={{0,1},{1,0},{2,3},{3,2},{4,5},{5,4},{6,7},{7,6},{8,9},{9,8},{10,11... | collective-permute-start | bytes 1216520 | tf_op jit(solution)/shard_map/ppermute | solution.py:369
  379.6 64.1 %collective-permute-start.41 = (bf16[264,768]{1,0:T(8,128)(2,1)}, bf16[264,768]{1,0:T(8,128)(2,1)}, u32[]{:S(2)}, u32[]{:S(2)}) collective-permute-start(bf16[264,768]{1,0:T(8,128)(2,1)} %get-tuple-element.93), channel_id=1, source_target_pairs={{0,1},{1,0},{2,3},{3,2},{4,5},{5,4},{6,7},{7,6},{8,9},{9,8},{10,11... | collective-permute-start | bytes 1216520 | tf_op jit(solution)/shard_map/ppermute | solution.py:369
  (108 other events, 967.2 us)
Sparse Core Ops, SparseCore 0:
  24.2 70.8 all-gather.2
  311.8 84.4 reduce-scatter.1

commit v3 on v2

--- a/solution.py
+++ b/solution.py
@@ -45,6 +45,18 @@
     return jnp.asarray(place, BF16)
 
 
+def lane_columns(heads):
+    pick = np.zeros((3 * heads, LANES, LANES), np.float32)
+    ones = np.zeros((3 * heads, 1, LANES), np.float32)
+    for b in range(3 * heads):
+        start = b * HEAD_DIM % LANES
+        for d in range(HEAD_DIM):
+            pick[b, start + d, d] = HEAD_DIM**-0.5 if b % 3 == 0 else 1.0
+        if b % 3 != 1:
+            ones[b, 0, HEAD_DIM] = 1.0
+    return jnp.asarray(pick, BF16), jnp.asarray(ones, F32)
+
+
 def query_block(rows):
     for size in range(min(rows, 400) // 16 * 16, 15, -16):
         if rows % size == 0:
@@ -52,10 +64,18 @@
     return rows
 
 
+def after_specs(after):
+    return [pl.BlockSpec(memory_space=pl.ANY)] * len(after)
+
+
+def whole_specs(count):
+    return [pl.BlockSpec(memory_space=pltpu.VMEM)] * count
+
+
 def forward_kernel(n_seq, heads, n_after, *refs):
-    tokens, refs = refs[:n_seq], refs[:n_seq] + refs[n_seq + n_after :]
-    gain, shift, weight, bias, key_mask, place = refs[n_seq : n_seq + 6]
-    normed_out, qkv_out, attended_out, rows, attended = refs[n_seq + 6 :]
+    tokens, refs = refs[:n_seq], refs[n_seq + n_after :]
+    gain, shift, weight, bias, key_mask, pick, ones, place = refs[:8]
+    normed_out, qkv_out, attended_out, rows, attended = refs[8:]
     piece = tokens[0].shape[0]
     total = n_seq * piece
     for r in range(n_seq):
@@ -63,52 +83,55 @@
         rows[r * piece : (r + 1) * piece, :] = unit * gain[...] + shift[...]
     normed = rows[...].astype(BF16)
     normed_out[...] = normed
+    qkv = (mm(normed, weight[...]) + bias[...]).astype(BF16)
+    width = qkv.shape[1]
     block = query_block(total)
     pad = qkv_out.shape[1] - total
-    for h in range(heads):
-        parts = []
-        for t in range(3):
-            b = 3 * h + t
-            part = mm(normed, weight[b]) + bias[b]
-            if t == 1:
-                part = part + key_mask[...]
-            part = part.astype(BF16)
-            qkv_out[b, :total] = part
-            if pad:
-                qkv_out[b, total:] = jnp.zeros((pad, LANES), BF16)
-            parts.append(part)
-        queries, keys, values = parts
-        for at in range(0, total, block):
-            scores = mm(queries[at : at + block], keys, 1, 1)
-            peak = jnp.max(scores, axis=-1, keepdims=True)
-            terms = jnp.exp(scores - peak).astype(BF16)
-            weighted = mm(terms, values)
-            result = (weighted / weighted[:, HEAD_DIM : HEAD_DIM + 1]).astype(BF16)
-            placed = mm(result, place[h])
-            if h:
-                placed = placed + attended[at : at + block, :]
+    parts = []
+    for b in range(3 * heads):
+        start = b * HEAD_DIM // LANES * LANES
+        size = min(LANES, width - start)
+        part = mm(qkv[:, start : start + size], pick[b, :size]) + ones[b]
+        if b % 3 == 1:
+            part = part + key_mask[...]
+        part = part.astype(BF16)
+        qkv_out[b, :total] = part
+        if pad:
+            qkv_out[b, total:] = jnp.zeros((pad, LANES), BF16)
+        parts.append(part)
+
+    tasks = [(at, h) for at in range(0, total, block) for h in range(heads)]
+
+    def score(task):
+        at, h = task
+        return mm(parts[3 * h][at : at + block], parts[3 * h + 1], 1, 1)
+
+    scores = score(tasks[0])
+    placed = None
+    for index, (at, h) in enumerate(tasks):
+        following = score(tasks[index + 1]) if index + 1 < len(tasks) else None
+        peak = jnp.max(scores, axis=-1, keepdims=True)
+        terms = jnp.exp(scores - peak).astype(BF16)
+        weighted = mm(terms, parts[3 * h + 2])
+        result = (weighted / weighted[:, HEAD_DIM : HEAD_DIM + 1]).astype(BF16)
+        here = mm(result, place[h])
+        placed = here if h == 0 else placed + here
+        if h == heads - 1:
             attended[at : at + block, :] = placed
+        scores = following
     for r in range(n_seq):
         attended_out[r] = attended[r * piece : (r + 1) * piece, :].astype(BF16)
-
-
-def after_specs(after):
-    return [pl.BlockSpec(memory_space=pl.ANY)] * len(after)
-
-
-def whole_specs(count):
-    return [pl.BlockSpec(memory_space=pltpu.VMEM)] * count
 
 
 def slot_forward(pieces, gain, shift, weight, bias, key_mask, after=()):
     n_seq = len(pieces)
     piece, width = pieces[0].shape
-    heads = weight.shape[0] // 3
+    heads = weight.shape[1] // (3 * HEAD_DIM)
     total = n_seq * piece
     padded = round_up(total, LANES)
     return pl.pallas_call(
         partial(forward_kernel, n_seq, heads, len(after)),
-        in_specs=whole_specs(n_seq) + after_specs(after) + whole_specs(6),
+        in_specs=whole_specs(n_seq) + after_specs(after) + whole_specs(8),
         out_shape=(
             jax.ShapeDtypeStruct((total, width), BF16),
             jax.ShapeDtypeStruct((3 * heads, padded, LANES), BF16),
@@ -123,13 +146,18 @@
             flops=20 * 10**9, bytes_accessed=12 * 10**6, transcendentals=heads * total * total
         ),
         name="slot_forward",
-    )(*pieces, *after, gain, shift, weight, bias, key_mask, head_columns(heads, 1))
+    )(
+        *pieces, *after, gain, shift, weight, bias, key_mask, *lane_columns(heads),
+        head_columns(heads, 1),
+    )
 
 
 def backward_kernel(n_seq, heads, n_after, *refs):
-    grads, refs = refs[:n_seq], refs[:n_seq] + refs[n_seq + n_after :]
-    qkv, place, spread = refs[n_seq : n_seq + 3]
-    grad_out, rows, total_grad = refs[n_seq + 3 :]
+    grads, refs = refs[:n_seq], refs[n_seq + n_after :]
+    tokens, refs = refs[:n_seq], refs[n_seq:]
+    qkv, normed, weight, before, place, spread = refs[:6]
+    outs, refs = refs[6 : 6 + n_seq], refs[6 + n_seq :]
+    grad_weight, vectors, grad_bias, rows, wide = refs
     piece = grads[0].shape[0]
     total = n_seq * piece
     padded = qkv.shape[1]
@@ -138,57 +166,105 @@
     if padded > total:
         rows[total:, :] = jnp.zeros((padded - total, rows.shape[1]), F32)
     grad_rows = rows[...].astype(BF16)
-    block = 3 * LANES if padded % (3 * LANES) == 0 else LANES
-    for h in range(heads):
-        grad_head = mm(grad_rows, place[h], 1, 1).astype(BF16)
-        queries = qkv[3 * h]
-        keys = qkv[3 * h + 1, :total]
-        values = qkv[3 * h + 2, :total]
-        keys_t = jnp.transpose(qkv[3 * h + 1])[:, :total]
-        grad_keys = jnp.zeros((total, LANES), F32)
-        grad_values = jnp.zeros((total, LANES), F32)
-        grad_queries = []
-        for at in range(0, padded, block):
-            query_part = queries[at : at + block]
-            grad_part = grad_head[at : at + block]
-            scores = mm(keys, query_part, 1, 1)
-            peak = jnp.max(scores, axis=0, keepdims=True)
-            terms = jnp.exp(scores - peak)
-            probs = terms * (1.0 / jnp.sum(terms, axis=0, keepdims=True))
-            grad_probs = mm(values, grad_part, 1, 1)
-            inner = jnp.sum(probs * grad_probs, axis=0, keepdims=True)
-            grad_scores = (probs * (grad_probs - inner)).astype(BF16)
-            grad_values = grad_values + mm(probs.astype(BF16), grad_part)
-            grad_keys = grad_keys + mm(grad_scores, query_part)
-            grad_queries.append(jnp.transpose(mm(keys_t, grad_scores)))
-        grad_queries = jnp.concatenate(grad_queries, axis=0)[:total] * (HEAD_DIM**-0.5)
-        for t, part in enumerate((grad_queries, grad_keys, grad_values)):
-            placed = mm(part.astype(BF16), spread[3 * h + t])
-            if h or t:
-                placed = placed + total_grad[...]
-            total_grad[...] = placed
-    grad_out[...] = total_grad[...].astype(BF16)
-
-
-def slot_backward(grads, qkv, after=()):
+    grad_heads = [mm(grad_rows, place[h], 1, 1).astype(BF16) for h in range(heads)]
+    block = 4 * LANES
+    tasks = [(h, at) for h in range(heads) for at in range(0, padded, block)]
+
+    def products(task):
+        h, at = task
+        end = min(at + block, padded)
+        scores = mm(qkv[3 * h + 1, :total], qkv[3 * h, at:end], 1, 1)
+        return scores, mm(qkv[3 * h + 2, :total], grad_heads[h][at:end], 1, 1)
+
+    current = products(tasks[0])
+    grad_qkv = None
+    for index, (h, at) in enumerate(tasks):
+        following = products(tasks[index + 1]) if index + 1 < len(tasks) else None
+        if at == 0:
+            keys_t = jnp.transpose(qkv[3 * h + 1])[:, :total]
+            grad_keys = jnp.zeros((total, LANES), F32)
+            grad_values = jnp.zeros((total, LANES), F32)
+            grad_queries = []
+        end = min(at + block, padded)
+        scores, grad_probs = current
+        peak = jnp.max(scores, axis=0, keepdims=True)
+        terms = jnp.exp(scores - peak)
+        probs = terms * (1.0 / jnp.sum(terms, axis=0, keepdims=True))
+        inner = jnp.sum(probs * grad_probs, axis=0, keepdims=True)
+        grad_scores = (probs * (grad_probs - inner)).astype(BF16)
+        grad_values = grad_values + mm(probs.astype(BF16), grad_heads[h][at:end])
+        grad_keys = grad_keys + mm(grad_scores, qkv[3 * h, at:end])
+        grad_queries.append(jnp.transpose(mm(keys_t, grad_scores)))
+        if end == padded:
+            queries = jnp.concatenate(grad_queries, axis=0)[:total] * (HEAD_DIM**-0.5)
+            for t, part in enumerate((queries, grad_keys, grad_values)):
+                placed = mm(part.astype(BF16), spread[3 * h + t])
+                grad_qkv = placed if grad_qkv is None else grad_qkv + placed
+        current = following
+    grad_low = grad_qkv.astype(BF16)
+    grad_bias[...] = jnp.broadcast_to(
+        jnp.sum(grad_low.astype(F32), axis=0, keepdims=True), grad_bias.shape
+    )
+    grad_weight[...] = before[...] + mm(normed[...], grad_low, 0, 0)
+    wide[...] = mm(grad_low, weight[...], 1, 1)
+    by_unit = jnp.zeros((1, wide.shape[1]), F32)
+    by_one = jnp.zeros((1, wide.shape[1]), F32)
+    for r in range(n_seq):
+        share = wide[r * piece : (r + 1) * piece, :]
+        unit, _ = normalize(tokens[r][...].astype(F32))
+        by_unit = by_unit + jnp.sum(share * unit, axis=0, keepdims=True)
+        by_one = by_one + jnp.sum(share, axis=0, keepdims=True)
+        outs[r][...] = share.astype(outs[r].dtype)
+    vectors[...] = jnp.zeros(vectors.shape, F32)
+    vectors[0:1, :] = by_unit
+    vectors[1:2, :] = by_one
+
+
+def slot_backward(grads, tokens, qkv, normed, weight, before, after=()):
     n_seq = len(grads)
     piece, width = grads[0].shape
     heads = qkv.shape[0] // 3
     total = n_seq * piece
+    model = normed.shape[1]
+    share = lambda r: jax.ShapeDtypeStruct((piece, model), BF16 if r & 1 else F32)
     return pl.pallas_call(
         partial(backward_kernel, n_seq, heads, len(after)),
-        in_specs=whole_specs(n_seq) + after_specs(after) + whole_specs(3),
-        out_shape=jax.ShapeDtypeStruct((total, 3 * width), BF16),
+        in_specs=whole_specs(n_seq) + after_specs(after) + whole_specs(n_seq + 6),
+        out_shape=(
+            *(share(r) for r in range(n_seq)),
+            jax.ShapeDtypeStruct((model, 3 * width), F32),
+            jax.ShapeDtypeStruct((8, model), F32),
+            jax.ShapeDtypeStruct((8, 3 * width), F32),
+        ),
         scratch_shapes=[
             pltpu.VMEM((qkv.shape[1], width), F32),
-            pltpu.VMEM((total, 3 * width), F32),
+            pltpu.VMEM((total, model), F32),
         ],
         compiler_params=pltpu.CompilerParams(vmem_limit_bytes=VMEM_BYTES),
         cost_estimate=pl.CostEstimate(
-            flops=28 * 10**9, bytes_accessed=8 * 10**6, transcendentals=heads * total * total
+            flops=28 * 10**9, bytes_accessed=12 * 10**6, transcendentals=heads * total * total
         ),
         name="slot_backward",
-    )(*grads, *after, qkv, head_columns(heads, 1), head_columns(heads, 3))
+    )(
+        *grads, *after, *tokens, qkv, normed, weight, before, head_columns(heads, 1),
+        head_columns(heads, 3),
+    )
+
+
+def copy_kernel(count, n_after, *refs):
+    for source, target in zip(refs[:count], refs[count + n_after :]):
+        target[...] = source[...]
+
+
+def once_there(arrays, after):
+    if not after:
+        return arrays
+    return pl.pallas_call(
+        partial(copy_kernel, len(arrays), len(after)),
+        in_specs=whole_specs(len(arrays)) + after_specs(after),
+        out_shape=tuple(jax.ShapeDtypeStruct(a.shape, a.dtype) for a in arrays),
+        name="once_there",
+    )(*arrays, *after)
 
 
 def mlp_kernel(
@@ -534,8 +610,19 @@
         pair = xor_send(own, "seq", 1)
         across = xor_send(own, "seq", 2)
         slot_tokens.append([own, pair, across, xor_send(across, "seq", 1)])
-    down_own = lax.all_gather(half_of(down_weight, 0, pair_me), "img", axis=0)
-    down_own = down_own.reshape(-1, model_width)
+
+    my_up = lax.dynamic_index_in_dim(
+        up_weight.reshape(shard, n_img, 2, ff_half), pair_me, 2, keepdims=False
+    ).reshape(shard, -1)
+    my_down, my_second = once_there(
+        (
+            half_of(down_weight, 0, pair_me),
+            jnp.concatenate([my_up, half_of(out_weight, 1, pair_me)], axis=1),
+        ),
+        tuple(first_arrived or ()),
+    )
+    down_own = lax.all_gather(my_down, "img", axis=0).reshape(-1, model_width)
+    second_part, second_arrived = start_gather(my_second)
 
     first_set = end_gather(first_part, first_arrived)
     qkv_cols = first_set[:, :shard].reshape(model_width, group)
@@ -555,28 +642,12 @@
         axis=1,
     )
 
-    scale = np.ones((blocks, 1, 1), np.float32)
-    scale[0::3] = HEAD_DIM**-0.5
-    ones = np.zeros((blocks, 1, LANES), np.float32)
-    ones[0::3, 0, HEAD_DIM] = 1.0
-    ones[2::3, 0, HEAD_DIM] = 1.0
-    lanes = ((0, 0), (0, 0), (0, LANES - HEAD_DIM))
-    head_weight = jnp.swapaxes(qkv_cols.reshape(model_width, blocks, HEAD_DIM), 0, 1)
-    head_weight = jnp.pad(head_weight * scale.astype(BF16), lanes)
     paired = lax.dynamic_slice_in_dim(
         pair_bias.reshape(HEADS, 2, HEAD_DIM), me * heads_here, heads_here, 0
     )
     head_bias = jnp.concatenate(
         [paired[:, :1], jnp.zeros((heads_here, 1, HEAD_DIM), F32), paired[:, 1:]], axis=1
-    ).reshape(blocks, 1, HEAD_DIM)
-    head_bias = jnp.pad(head_bias * scale, lanes) + ones
-
-    my_up = lax.dynamic_index_in_dim(
-        up_weight.reshape(shard, n_img, 2, ff_half), pair_me, 2, keepdims=False
-    ).reshape(shard, -1)
-    second_part, second_arrived = start_gather(
-        jnp.concatenate([my_up, half_of(out_weight, 1, pair_me)], axis=1)
-    )
+    ).reshape(1, group)
 
     slot_normed, slot_qkv, slot_attended = [], [], []
     for slot in range(slot_count):
@@ -584,7 +655,7 @@
         if slot == 1 and second_arrived is not None:
             after = tuple(second_arrived)
         normed, qkv_rows, attended = slot_forward(
-            slot_tokens[slot], gain_first, shift_first, head_weight, head_bias, key_mask, after
+            slot_tokens[slot], gain_first, shift_first, qkv_cols, head_bias, key_mask, after
         )
         slot_normed.append(normed)
         slot_qkv.append(qkv_rows)
@@ -655,23 +726,30 @@
     if few_devices():
         sums = reduce_inner(second_grads)
         own_second = reduce_outer(sums)
-        stages = [(), (sums,), (own_second,)]
+        stages = [(), (), (sums,)]
     else:
         own_second = scatter_img(second_grads)
 
     grad_columns = jnp.zeros((model_width, group), F32)
     bias_sums = jnp.zeros((group,), F32)
+    norm_sums = jnp.zeros((8, model_width), F32)
     own_sums = []
     for slot in range(slot_count):
-        grad_qkv = slot_backward(slot_grads[slot], slot_qkv[slot], stages[min(slot, 2)])
-        partial_in = mm(grad_qkv, qkv_cols, 1, 1).reshape(n_seq, piece_size, model_width)
-        low = partial_in.astype(BF16)
-        pair = xor_send(low[1], "seq", 1).astype(F32)
-        across = xor_send(low[3], "seq", 1).astype(F32)
-        across = xor_send((partial_in[2] + across).astype(BF16), "seq", 2)
-        own_sums.append(partial_in[0] + pair + across.astype(F32))
-        grad_columns += mm(slot_normed[slot], grad_qkv, 0, 0)
-        bias_sums += jnp.sum(grad_qkv.astype(F32), axis=0)
+        *shares, grad_columns, slot_norm, slot_bias = slot_backward(
+            slot_grads[slot],
+            slot_tokens[slot],
+            slot_qkv[slot],
+            slot_normed[slot],
+            qkv_cols,
+            grad_columns,
+            stages[min(slot, 2)],
+        )
+        norm_sums += slot_norm
+        bias_sums += slot_bias[0]
+        pair = xor_send(shares[1], "seq", 1).astype(F32)
+        across = xor_send(shares[3], "seq", 1).astype(F32)
+        across = xor_send((shares[2] + across).astype(BF16), "seq", 2)
+        own_sums.append(shares[0] + pair + across.astype(F32))
     columns = grad_columns.astype(BF16).reshape(n_img, shard, group)
     if few_devices():
         own_columns = reduce_outer(reduce_inner(columns))
@@ -686,8 +764,6 @@
     mean_product = jnp.mean(scaled * unit, axis=-1, keepdims=True)
     grad_inputs = factor * (scaled - mean_scaled - unit * mean_product)
     tokens_grad = grad_residual + grad_inputs.reshape(grad_residual.shape)
-    grad_norm_gain = jnp.sum(grad_norm_first * unit, axis=0)
-    grad_norm_shift = jnp.sum(grad_norm_first, axis=0)
 
     by_sender = jnp.stack(
         [own_columns] + [xor_send(own_columns, "seq", r) for r in range(1, n_seq)]
@@ -711,8 +787,8 @@
     up_halves = grad_up_bias.reshape(2, n_img, 1, ff_half)
     grad_up_bias = in_pair_order(up_halves[0], up_halves[1], 1).reshape(-1)
     all_vectors = [
-        grad_norm_gain,
-        grad_norm_shift,
+        norm_sums[0],
+        norm_sums[1],
         grad_pairs,
         vectors[2],
         vectors[0],

time: 510 us -> 513 us (level)
  starting transfers between devices: 57.1 us -> 83.9 us
  matrix products: 19.8 us -> 0 us
    dot_general x6 -> x0, matrix products: 19.8 us -> none  [mm(): lax.dot_general(left, right, (((left_dim,), (right_dim,)), ((), ())), pre...]
    ppermute x15, starting transfers between devices: 24.3 us -> 43.3 us  [outer_send(): lax.ppermute(block, 'img', [(z * INNER + y, (z + shift) % outer * INNER +...]
    pallas_call x3, Pallas kernels: 52.2 us -> 36.1 us  [slot_forward(): pl.pallas_call(partial(forward_kernel, n_seq, heads, len(after)), in_spec...]
    pallas_call x3, Pallas kernels: 67.2 us -> 79.6 us  [slot_backward(): pl.pallas_call(partial(backward_kernel, n_seq, heads, len(after)), in_spe...]
    reduce_sum x8 -> x1, other arithmetic: 9.43 us -> 0.76 us  [local(): mean_product = jnp.mean(scaled * unit, axis=-1, keepdims=True)]
    ppermute x57, starting transfers between devices: 32.7 us -> 40.5 us  [xor_send(): return lax.ppermute(block, axis, [(i, i ^ bits) for i in range(n)])]
    add x2 -> x5, other arithmetic: 0.61 us -> 6.74 us  [the longest x3 5.22 us: local(): own_sums.append(shares[0] + pair + across.astype(F32))]
    concatenate x1, local copies, waits for them, and re-layouts: 0.09 us -> 5.56 us  [local(): jnp.concatenate([norm_gain, norm_shift, out_bias, mlp_gain, mlp_shift, do...]
  transfers between devices with their start and end apart: 74 -> 74, of which waited for: 29 -> 23; matrix products, arithmetic and copies ran while one was open for 22% -> 18% of each run, Pallas kernels for 24% -> 23%
where the time goes in v3:
time: 513 us; the launch traced here: 506 us
  Pallas kernels  169 us (33%)
  waiting for transfers between devices  134 us (26%)
  starting transfers between devices  83.9 us (16%)
  local copies, waits for them, and re-layouts  56.3 us (11%)
  other arithmetic  47.8 us (9%)
  between operations  16.1 us (3%)
    ppermute x57, waiting for transfers between devices, xor_send(): return lax.ppermute(block, axis, [(i, i ^ bits) for i in range(n)])  81 us
    pallas_call x3, Pallas kernels, slot_backward(): pl.pallas_call(partial(backward_kernel, n_seq, heads, len(after)), in_spe...  79.6 us
    ppermute x15, waiting for transfers between devices, outer_send(): lax.ppermute(block, 'img', [(z * INNER + y, (z + shift) % outer * INNER +...  52.6 us
    pallas_call x1, Pallas kernels, feed_forward(): pl.pallas_call(mlp_kernel, grid=(ff // chunk,), in_specs=[whole(tokens.sh...  51 us
    ppermute x15, starting transfers between devices, outer_send(): lax.ppermute(block, 'img', [(z * INNER + y, (z + shift) % outer * INNER +...  43.3 us
    ppermute x57, starting transfers between devices, xor_send(): return lax.ppermute(block, axis, [(i, i ^ bits) for i in range(n)])  40.5 us
    pallas_call x3, Pallas kernels, slot_forward(): pl.pallas_call(partial(forward_kernel, n_seq, heads, len(after)), in_spec...  36.1 us
  transfers between devices with their start and end apart: 74, of which 23 were waited for; matrix products, arithmetic and copies ran while one was open for 18% of the time, Pallas kernels for 23%

profile of v3, /device:TPU:0, one launch (start us, length us, event | category | flops | bytes accessed | tf_op | source)
XLA Modules:
  0.0 506.4 jit_solution(5961068492263381385)
XLA Ops:
  7.3 5.6 %concatenate.77 = bf16[1152]{0:T(1024)(128)(2,1)S(1)} concatenate(bf16[96]{0:T(256)(128)(2,1)} %param.35, bf16[96]{0:T(256)(128)(2,1)} %param.36, bf16[96]{0:T(256)(128)(2,1)} %param.40, bf16[96]{0:T(256)(128)(2,1)} %param.41, bf16[96]{0:T(256)(128)(2,1)} %param.42, bf16[96]{0:T(256)(128)(2,1)} %param.46, bf16[192]{0:T(256)(128)(2,1)} %param.38, bf16[384]{0:T(512)(128)(2,1)} %param.44), dimensions={0} | concatenate | bytes 4608 | tf_op jit(solution)/shard_map/concatenate | solution.py:599
  47.2 9.5 %collective-permute-done.10.refs_4_ = bf16[96,1920]{1,0:T(8,128)(2,1)S(1)} collective-permute-done((bf16[96,1920]{1,0:T(8,128)(2,1)}, bf16[96,1920]{1,0:T(8,128)(2,1)S(1)}, u32[]{:S(2)}, u32[]{:S(2)}) %collective-permute-start.10) | collective-permute-done | bytes 368672 | tf_op jit(solution)/shard_map/ppermute | solution.py:453
  57.1 22.5 %collective-permute-done.11.refs_5_ = bf16[96,1920]{1,0:T(8,128)(2,1)S(1)} collective-permute-done((bf16[96,1920]{1,0:T(8,128)(2,1)}, bf16[96,1920]{1,0:T(8,128)(2,1)S(1)}, u32[]{:S(2)}, u32[]{:S(2)}) %collective-permute-start.11) | collective-permute-done | bytes 368672 | tf_op jit(solution)/shard_map/ppermute | solution.py:453
  82.9 12.0 %collective-permute-done.6 = bf16[4,112,576]{2,1,0:T(8,128)(2,1)S(1)} collective-permute-done((bf16[4,112,576]{2,1,0:T(8,128)(2,1)S(1)}, bf16[4,112,576]{2,1,0:T(8,128)(2,1)S(1)}, u32[]{:S(2)}, u32[]{:S(2)}) %collective-permute-start.6) | collective-permute-done | bytes 516128 | tf_op jit(solution)/shard_map/ppermute | solution.py:445
  102.6 11.9 %slot_forward.4 = (bf16[1056,768]{1,0:T(8,128)(2,1)}, bf16[9,1152,128]{2,1,0:T(8,128)(2,1)}, bf16[4,264,192]{2,1,0:T(8,128)(2,1)}) custom-call(bf16[264,768]{1,0:T(8,128)(2,1)} %get-tuple-element.131.refs_0_.refs_4_, bf16[264,768]{1,0:T(8,128)(2,1)} %collective-permute-done.7.refs_1_.refs_5_, bf16[264,768]{1,0:T(8,128)(2,1)} %collective-permute-done.8.refs_2_.refs_6_, ...), custom_call_target="tpu_custom_call" | custom-call | flops 20000000000 | bytes 12000000 | tf_op jit(solution)/shard_map/slot_forward/pallas_call | solution.py:132
  114.6 12.1 %slot_forward.3 = (bf16[1056,768]{1,0:T(8,128)(2,1)}, bf16[9,1152,128]{2,1,0:T(8,128)(2,1)}, bf16[4,264,192]{2,1,0:T(8,128)(2,1)}) custom-call(bf16[264,768]{1,0:T(8,128)(2,1)} %get-tuple-element.129.refs_0_.refs_4_, bf16[264,768]{1,0:T(8,128)(2,1)} %collective-permute-done.refs_1_.refs_5_, bf16[264,768]{1,0:T(8,128)(2,1)} %collective-permute-done.1.refs_2_.refs_6_, ...), custom_call_target="tpu_custom_call" | custom-call | flops 20000000000 | bytes 12000000 | tf_op jit(solution)/shard_map/slot_forward/pallas_call | solution.py:132
  129.3 7.6 %collective-permute-done.25 = bf16[4,96,1920]{2,1,0:T(8,128)(2,1)S(1)} collective-permute-done((bf16[4,96,1920]{2,1,0:T(8,128)(2,1)S(1)}, bf16[4,96,1920]{2,1,0:T(8,128)(2,1)S(1)}, u32[]{:S(2)}, u32[]{:S(2)}) %collective-permute-start.25) | collective-permute-done | bytes 1474592 | tf_op jit(solution)/shard_map/ppermute | solution.py:445
  139.9 12.1 %slot_forward.5 = (bf16[1056,768]{1,0:T(8,128)(2,1)}, bf16[9,1152,128]{2,1,0:T(8,128)(2,1)}, bf16[4,264,192]{2,1,0:T(8,128)(2,1)}) custom-call(bf16[264,768]{1,0:T(8,128)(2,1)} %get-tuple-element.130.refs_0_.refs_5_, bf16[264,768]{1,0:T(8,128)(2,1)} %copy-done.39, bf16[264,768]{1,0:T(8,128)(2,1)} %collective-permute-done.14.refs_2_.refs_7_, ...), custom_call_target="tpu_custom_call" | custom-call | flops 20000000000 | bytes 12000000 | tf_op jit(solution)/shard_map/slot_forward/pallas_call | solution.py:132
  182.8 51.0 %feed_forward.1 = (bf16[3,264,768]{2,1,0:T(8,128)(2,1)}, f32[3,264,768]{2,1,0:T(8,128)}, bf16[4,3,264,192]{3,2,1,0:T(8,128)(2,1)}, bf16[4,192,768]{2,1,0:T(8,128...) custom-call(bf16[3,264,768]{2,1,0:T(8,128)(2,1)} %tokens.1, ...), custom_call_target="tpu_custom_call" | custom-call | flops 54999998464 | bytes 40000000 | tf_op jit(solution)/shard_map/feed_forward/pallas_call | solution.py:381
  240.5 4.1 collective-permute-done.30.refs_2_
  249.3 26.3 %slot_backward.3 = (f32[264,768]{1,0:T(8,128)}, bf16[264,768]{1,0:T(8,128)(2,1)}, f32[264,768]{1,0:T(8,128)}, bf16[264,768]{1,0:T(8,128)(2,1)}, f32[768,576]{1,0...) custom-call(bf16[264,192]{1,0:T(8,128)(2,1)} %get-tuple-element.128.refs_0_, bf16[264,192]{1,0:T(8,128)(2,1)} %copy-done.43, ...), custom_call_target="tpu_custom_call" | custom-call | flops 28000000000 | bytes 12000000 | tf_op jit(solution)/shard_map/slot_backward/pallas_call | solution.py:230
  277.5 26.7 %slot_backward.4 = (f32[264,768]{1,0:T(8,128)}, bf16[264,768]{1,0:T(8,128)(2,1)}, f32[264,768]{1,0:T(8,128)}, bf16[264,768]{1,0:T(8,128)(2,1)}, f32[768,576]{1,0...) custom-call(bf16[264,192]{1,0:T(8,128)(2,1)} %get-tuple-element.125.refs_0_, bf16[264,192]{1,0:T(8,128)(2,1)} %copy-done.40, ...), custom_call_target="tpu_custom_call" | custom-call | flops 28000000000 | bytes 12000000 | tf_op jit(solution)/shard_map/slot_backward/pallas_call | solution.py:230
  315.9 7.7 %collective-permute-done.34 = bf16[264,768]{1,0:T(8,128)(2,1)} collective-permute-done((bf16[264,768]{1,0:T(8,128)(2,1)}, bf16[264,768]{1,0:T(8,128)(2,1)}, u32[]{:S(2)}, u32[]{:S(2)}) %collective-permute-start.34) | collective-permute-done | bytes 405536 | tf_op jit(solution)/shard_map/ppermute | solution.py:445
  326.9 3.7 add_convert_fusion
  330.6 13.1 %collective-permute-done.46 = bf16[4,96,1920]{2,1,0:T(8,128)(2,1)} collective-permute-done((bf16[4,96,1920]{2,1,0:T(8,128)(2,1)}, bf16[4,96,1920]{2,1,0:T(8,128)(2,1)}, u32[]{:S(2)}, u32[]{:S(2)}) %collective-permute-start.46) | collective-permute-done | bytes 1474592 | tf_op jit(solution)/shard_map/ppermute | solution.py:445
  348.1 26.6 %slot_backward.5 = (f32[264,768]{1,0:T(8,128)}, bf16[264,768]{1,0:T(8,128)(2,1)}, f32[264,768]{1,0:T(8,128)}, bf16[264,768]{1,0:T(8,128)(2,1)}, f32[768,576]{1,0...) custom-call(bf16[264,192]{1,0:T(8,128)(2,1)} %get-tuple-element.121.refs_0_, ...), custom_call_target="tpu_custom_call" | custom-call | flops 28000000000 | bytes 12000000 | tf_op jit(solution)/shard_map/slot_backward/pallas_call | solution.py:230
  382.3 13.9 %collective-permute-start.53 = (f32[2,1152]{1,0:T(2,128)S(1)}, f32[2,1152]{1,0:T(2,128)S(1)}, u32[]{:S(2)}, u32[]{:S(2)}) collective-permute-start(f32[2,1152]{1,0:T(2,128)S(1)} %get-tuple-element.167), channel_id=1, source_target_pairs={{0,8},{4,12},{8,16},{12,20},{16,24},{20,28},{24,0},{28,4},{1,9},{5... | collective-permute-start | bytes 27656 | tf_op jit(solution)/shard_map/ppermute | solution.py:453
  396.2 5.0 collective-permute-start.54
  410.7 4.7 collective-permute-done.56
  421.0 15.6 %collective-permute-done.65 = bf16[96,1920]{1,0:T(8,128)(2,1)S(1)} collective-permute-done((bf16[96,1920]{1,0:T(8,128)(2,1)S(1)}, bf16[96,1920]{1,0:T(8,128)(2,1)S(1)}, u32[]{:S(2)}, u32[]{:S(2)}) %collective-permute-start.65) | collective-permute-done | bytes 368672 | tf_op jit(solution)/shard_map/ppermute | solution.py:453
  436.7 11.9 %collective-permute-start.60 = (bf16[96,576]{1,0:T(8,128)(2,1)S(1)}, bf16[96,576]{1,0:T(8,128)(2,1)S(1)}, u32[]{:S(2)}, u32[]{:S(2)}) collective-permute-start(bf16[96,576]{1,0:T(8,128)(2,1)S(1)} %get-tuple-element.143), channel_id=1, source_target_pairs={{0,24},{4,28},{8,0},{12,4},{16,8},{20,12},{24,16},{28,20},{1,25},{... | collective-permute-start | bytes 331784 | tf_op jit(solution)/shard_map/ppermute | solution.py:453
  456.2 7.7 %collective-permute-done.62 = bf16[96,576]{1,0:T(8,128)(2,1)S(1)} collective-permute-done((bf16[96,576]{1,0:T(8,128)(2,1)S(1)}, bf16[96,576]{1,0:T(8,128)(2,1)S(1)}, u32[]{:S(2)}, u32[]{:S(2)}) %collective-permute-start.62) | collective-permute-done | bytes 110624 | tf_op jit(solution)/shard_map/ppermute | solution.py:445
  478.4 6.6 %collective-permute-done.70 = bf16[192,768]{1,0:T(8,128)(2,1)S(1)} collective-permute-done((bf16[192,768]{1,0:T(8,128)(2,1)}, bf16[192,768]{1,0:T(8,128)(2,1)S(1)}, u32[]{:S(2)}, u32[]{:S(2)}) %collective-permute-start.70) | collective-permute-done | bytes 294944 | tf_op jit(solution)/shard_map/ppermute | solution.py:445
  486.1 4.7 fusion.7
  (378 shorter events, 167.7 us)
Async XLA Ops:
  7.2 131.9 %all-gather.3.cloned.1.call-start = ((), (), s32[]{:S(2)}) async-start(), calls=%async_computation.2 | async-start | bytes 2654208 | tf_op jit(solution)/shard_map/all_gather | solution.py:624
  23.9 57.5 %collective-permute-start.8 = (bf16[264,768]{1,0:T(8,128)(2,1)}, bf16[264,768]{1,0:T(8,128)(2,1)}, u32[]{:S(2)}, u32[]{:S(2)}) collective-permute-start(bf16[264,768]{1,0:T(8,128)(2,1)} %get-tuple-element.131.refs_0_.refs_4_), channel_id=1, source_target_pairs={{0,2},{1,3},{2,0},{3,1},{4,6},{5,7},{6,4},{7,5},{8,10},{9,11},{10,... | collective-permute-start | bytes 1216520 | tf_op jit(solution)/shard_map/ppermute | solution.py:445
  25.4 73.7 %collective-permute-start.7 = (bf16[264,768]{1,0:T(8,128)(2,1)}, bf16[264,768]{1,0:T(8,128)(2,1)}, u32[]{:S(2)}, u32[]{:S(2)}) collective-permute-start(bf16[264,768]{1,0:T(8,128)(2,1)} %get-tuple-element.131.refs_0_.refs_4_), channel_id=1, source_target_pairs={{0,1},{1,0},{2,3},{3,2},{4,5},{5,4},{6,7},{7,6},{8,9},{9,8},{10,11... | collective-permute-start | bytes 1216520 | tf_op jit(solution)/shard_map/ppermute | solution.py:445
  39.3 60.3 %collective-permute-start.1 = (bf16[264,768]{1,0:T(8,128)(2,1)}, bf16[264,768]{1,0:T(8,128)(2,1)}, u32[]{:S(2)}, u32[]{:S(2)}) collective-permute-start(bf16[264,768]{1,0:T(8,128)(2,1)} %get-tuple-element.129.refs_0_.refs_4_), channel_id=1, source_target_pairs={{0,2},{1,3},{2,0},{3,1},{4,6},{5,7},{6,4},{7,5},{8,10},{9,11},{10,... | collective-permute-start | bytes 1216520 | tf_op jit(solution)/shard_map/ppermute | solution.py:445
  43.8 35.9 %collective-permute-start.11 = (bf16[96,1920]{1,0:T(8,128)(2,1)}, bf16[96,1920]{1,0:T(8,128)(2,1)S(1)}, u32[]{:S(2)}, u32[]{:S(2)}) collective-permute-start(bf16[96,1920]{1,0:T(8,128)(2,1)} %get-tuple-element.57), channel_id=1, source_target_pairs={{0,16},{4,20},{8,24},{12,28},{16,0},{20,4},{24,8},{28,12},{1,17},{... | collective-permute-start | bytes 1105928 | tf_op jit(solution)/shard_map/ppermute | solution.py:453
  44.1 432.7 %reduce-scatter.2.cloned.1.call-start = ((), (), s32[]{:S(2)}) async-start(), calls=%async_computation.1 | async-start | bytes 2654208 | tf_op jit(solution)/shard_map/reduce_scatter | solution.py:517
  81.2 33.3 %collective-permute-start = (bf16[264,768]{1,0:T(8,128)(2,1)}, bf16[264,768]{1,0:T(8,128)(2,1)}, u32[]{:S(2)}, u32[]{:S(2)}) collective-permute-start(bf16[264,768]{1,0:T(8,128)(2,1)} %get-tuple-element.129.refs_0_.refs_4_), channel_id=1, source_target_pairs={{0,1},{1,0},{2,3},{3,2},{4,5},{5,4},{6,7},{7,6},{8,9},{9,8},{10,11... | collective-permute-start | bytes 1216520 | tf_op jit(solution)/shard_map/ppermute | solution.py:445
  99.1 40.0 %collective-permute-start.13 = (bf16[264,768]{1,0:T(8,128)(2,1)}, bf16[264,768]{1,0:T(8,128)(2,1)S(1)}, u32[]{:S(2)}, u32[]{:S(2)}) collective-permute-start(bf16[264,768]{1,0:T(8,128)(2,1)} %get-tuple-element.130.refs_0_.refs_5_), channel_id=1, source_target_pairs={{0,1},{1,0},{2,3},{3,2},{4,5},{5,4},{6,7},{7,6},{8,9},{9,8},{10,11... | collective-permute-start | bytes 1216520 | tf_op jit(solution)/shard_map/ppermute | solution.py:445
  99.7 39.9 %collective-permute-start.15 = (bf16[264,768]{1,0:T(8,128)(2,1)}, bf16[264,768]{1,0:T(8,128)(2,1)}, u32[]{:S(2)}, u32[]{:S(2)}) collective-permute-start(bf16[264,768]{1,0:T(8,128)(2,1)} %collective-permute-done.14.refs_2_.refs_7_), channel_id=1, source_target_pairs={{0,1},{1,0},{2,3},{3,2},{4,5},{5,4},{6,7},{7,6},{8,9},{9,8},{10,11... | collective-permute-start | bytes 1216520 | tf_op jit(solution)/shard_map/ppermute | solution.py:445
  100.2 36.8 %collective-permute-start.25 = (bf16[4,96,1920]{2,1,0:T(8,128)(2,1)S(1)}, bf16[4,96,1920]{2,1,0:T(8,128)(2,1)S(1)}, u32[]{:S(2)}, u32[]{:S(2)}) collective-permute-start(bf16[4,96,1920]{2,1,0:T(8,128)(2,1)S(1)} %bitcast_dynamic-update-slice_fusion), channel_id=1, source_target_pairs={{0,4},{4,0},{8,12},{12,8},{16,20},{20,16},{24,28},{28,24},{1,5},{5... | collective-permute-start | bytes 4423688 | tf_op jit(solution)/shard_map/ppermute | solution.py:445
  139.1 43.7 %collective-permute-start.27 = (bf16[768,1536]{1,0:T(8,128)(2,1)}, bf16[768,1536]{1,0:T(8,128)(2,1)}, u32[]{:S(2)}, u32[]{:S(2)}) collective-permute-start(bf16[768,1536]{1,0:T(8,128)(2,1)} %slice.284.up_own), channel_id=1, source_target_pairs={{0,1},{1,0},{2,3},{3,2},{4,5},{5,4},{6,7},{7,6},{8,9},{9,8},{10,11... | collective-permute-start | bytes 7077896 | tf_op jit(solution)/shard_map/ppermute | solution.py:445
  139.1 43.7 %collective-permute-start.28 = (bf16[1536,768]{1,0:T(8,128)(2,1)}, bf16[1536,768]{1,0:T(8,128)(2,1)}, u32[]{:S(2)}, u32[]{:S(2)}) collective-permute-start(bf16[1536,768]{1,0:T(8,128)(2,1)} %all-gather.3.cloned.1.call-done.down_own), channel_id=1, source_target_pairs={{0,1},{1,0},{2,3},{3,2},{4,5},{5,4},{6,7},{7,6},{8,9},{9,8},{10,11... | collective-permute-start | bytes 7077896 | tf_op jit(solution)/shard_map/ppermute | solution.py:445
  233.9 91.7 %collective-permute-start.69 = (bf16[1536,768]{1,0:T(8,128)(2,1)}, bf16[1536,768]{1,0:T(8,128)(2,1)}, u32[]{:S(2)}, u32[]{:S(2)}) collective-permute-start(bf16[1536,768]{1,0:T(8,128)(2,1)} %get-tuple-element.97), channel_id=1, source_target_pairs={{0,1},{1,0},{2,3},{3,2},{4,5},{5,4},{6,7},{7,6},{8,9},{9,8},{10,11... | collective-permute-start | bytes 7077896 | tf_op jit(solution)/shard_map/ppermute | solution.py:445
  235.6 68.6 %collective-permute-start.45 = (bf16[768,384]{1,0:T(8,128)(2,1)S(1)}, bf16[768,384]{1,0:T(8,128)(2,1)S(1)}, u32[]{:S(2)}, u32[]{:S(2)}) collective-permute-start(bf16[768,384]{1,0:T(8,128)(2,1)S(1)} %constant_dynamic-slice_fusion.7), channel_id=1, source_target_pairs={{0,1},{1,0},{2,3},{3,2},{4,5},{5,4},{6,7},{7,6},{8,9},{9,8},{10,11... | collective-permute-start | bytes 1769480 | tf_op jit(solution)/shard_map/ppermute | solution.py:445
  239.8 35.8 %collective-permute-start.35 = (bf16[264,192]{1,0:T(8,128)(2,1)S(1)}, bf16[264,192]{1,0:T(8,128)(2,1)S(1)}, u32[]{:S(2)}, u32[]{:S(2)}) collective-permute-start(bf16[264,192]{1,0:T(8,128)(2,1)S(1)} %get-tuple-element.124), channel_id=1, source_target_pairs={{0,1},{1,0},{2,3},{3,2},{4,5},{5,4},{6,7},{7,6},{8,9},{9,8},{10,11... | collective-permute-start | bytes 304136 | tf_op jit(solution)/shard_map/ppermute | solution.py:445
  276.4 33.9 %collective-permute-start.33 = (bf16[264,768]{1,0:T(8,128)(2,1)}, bf16[264,768]{1,0:T(8,128)(2,1)S(1)}, u32[]{:S(2)}, u32[]{:S(2)}) collective-permute-start(bf16[264,768]{1,0:T(8,128)(2,1)} %get-tuple-element.69), channel_id=1, source_target_pairs={{0,1},{1,0},{2,3},{3,2},{4,5},{5,4},{6,7},{7,6},{8,9},{9,8},{10,11... | collective-permute-start | bytes 1216520 | tf_op jit(solution)/shard_map/ppermute | solution.py:445
  276.9 38.2 %collective-permute-start.32 = (bf16[264,768]{1,0:T(8,128)(2,1)}, bf16[264,768]{1,0:T(8,128)(2,1)S(1)}, u32[]{:S(2)}, u32[]{:S(2)}) collective-permute-start(bf16[264,768]{1,0:T(8,128)(2,1)} %get-tuple-element.67), channel_id=1, source_target_pairs={{0,1},{1,0},{2,3},{3,2},{4,5},{5,4},{6,7},{7,6},{8,9},{9,8},{10,11... | collective-permute-start | bytes 1216520 | tf_op jit(solution)/shard_map/ppermute | solution.py:445
  308.7 35.0 %collective-permute-start.46 = (bf16[4,96,1920]{2,1,0:T(8,128)(2,1)}, bf16[4,96,1920]{2,1,0:T(8,128)(2,1)}, u32[]{:S(2)}, u32[]{:S(2)}) collective-permute-start(bf16[4,96,1920]{2,1,0:T(8,128)(2,1)} %fusion.10), channel_id=1, source_target_pairs={{0,4},{4,0},{8,12},{12,8},{16,20},{20,16},{24,28},{28,24},{1,5},{5... | collective-permute-start | bytes 4423688 | tf_op jit(solution)/shard_map/ppermute | solution.py:445
  312.7 35.4 %collective-permute-start.41 = (bf16[264,192]{1,0:T(8,128)(2,1)}, bf16[264,192]{1,0:T(8,128)(2,1)}, u32[]{:S(2)}, u32[]{:S(2)}) collective-permute-start(bf16[264,192]{1,0:T(8,128)(2,1)} %get-tuple-element.120), channel_id=1, source_target_pairs={{0,1},{1,0},{2,3},{3,2},{4,5},{5,4},{6,7},{7,6},{8,9},{9,8},{10,11... | collective-permute-start | bytes 304136 | tf_op jit(solution)/shard_map/ppermute | solution.py:445
  315.0 33.1 %collective-permute-start.42 = (bf16[264,192]{1,0:T(8,128)(2,1)}, bf16[264,192]{1,0:T(8,128)(2,1)}, u32[]{:S(2)}, u32[]{:S(2)}) collective-permute-start(bf16[264,192]{1,0:T(8,128)(2,1)} %get-tuple-element.119), channel_id=1, source_target_pairs={{0,2},{1,3},{2,0},{3,1},{4,6},{5,7},{6,4},{7,5},{8,10},{9,11},{10,... | collective-permute-start | bytes 304136 | tf_op jit(solution)/shard_map/ppermute | solution.py:445
  325.6 53.5 %collective-permute-start.38 = (bf16[264,768]{1,0:T(8,128)(2,1)}, bf16[264,768]{1,0:T(8,128)(2,1)S(1)}, u32[]{:S(2)}, u32[]{:S(2)}) collective-permute-start(bf16[264,768]{1,0:T(8,128)(2,1)} %get-tuple-element.74), channel_id=1, source_target_pairs={{0,1},{1,0},{2,3},{3,2},{4,5},{5,4},{6,7},{7,6},{8,9},{9,8},{10,11... | collective-permute-start | bytes 1216520 | tf_op jit(solution)/shard_map/ppermute | solution.py:445
  343.7 35.4 %collective-permute-start.40 = (bf16[264,768]{1,0:T(8,128)(2,1)}, bf16[264,768]{1,0:T(8,128)(2,1)}, u32[]{:S(2)}, u32[]{:S(2)}) collective-permute-start(bf16[264,768]{1,0:T(8,128)(2,1)} %add_convert_fusion.4), channel_id=1, source_target_pairs={{0,2},{1,3},{2,0},{3,1},{4,6},{5,7},{6,4},{7,5},{8,10},{9,11},{10,... | collective-permute-start | bytes 1216520 | tf_op jit(solution)/shard_map/ppermute | solution.py:445
  415.4 38.1 %collective-permute-start.48 = (bf16[264,768]{1,0:T(8,128)(2,1)}, bf16[264,768]{1,0:T(8,128)(2,1)S(1)}, u32[]{:S(2)}, u32[]{:S(2)}) collective-permute-start(bf16[264,768]{1,0:T(8,128)(2,1)} %get-tuple-element.86), channel_id=1, source_target_pairs={{0,1},{1,0},{2,3},{3,2},{4,5},{5,4},{6,7},{7,6},{8,9},{9,8},{10,11... | collective-permute-start | bytes 1216520 | tf_op jit(solution)/shard_map/ppermute | solution.py:445
  417.3 54.5 %collective-permute-start.47 = (bf16[264,768]{1,0:T(8,128)(2,1)}, bf16[264,768]{1,0:T(8,128)(2,1)}, u32[]{:S(2)}, u32[]{:S(2)}) collective-permute-start(bf16[264,768]{1,0:T(8,128)(2,1)} %get-tuple-element.84), channel_id=1, source_target_pairs={{0,1},{1,0},{2,3},{3,2},{4,5},{5,4},{6,7},{7,6},{8,9},{9,8},{10,11... | collective-permute-start | bytes 1216520 | tf_op jit(solution)/shard_map/ppermute | solution.py:445
  (94 other events, 1223.8 us)
Sparse Core Ops, SparseCore 0:
  44.3 74.9 all-gather.2
  330.8 99.0 reduce-scatter.1

commit v4 on v3

--- a/solution.py
+++ b/solution.py
@@ -17,6 +17,10 @@
 F32 = jnp.float32
 BF16 = jnp.bfloat16
 VMEM_BYTES = 60 * 1024 * 1024
+def cost(giga_flops):
+    return pl.CostEstimate(
+        flops=giga_flops * 10**9, bytes_accessed=10**7, transcendentals=10**6
+    )
 
 
 def mm(left, right, left_dim=1, right_dim=0):
@@ -68,6 +72,15 @@
     return [pl.BlockSpec(memory_space=pl.ANY)] * len(after)
 
 
+def piece_spec(array, *at):
+    rest = array.shape[len(at) :]
+    return pl.BlockSpec((None,) * len(at) + rest, lambda i: at + (0,) * len(rest))
+
+
+def piece_specs(pieces):
+    return [piece_spec(*piece) for piece in pieces]
+
+
 def whole_specs(count):
     return [pl.BlockSpec(memory_space=pltpu.VMEM)] * count
 
@@ -75,7 +88,8 @@
 def forward_kernel(n_seq, heads, n_after, *refs):
     tokens, refs = refs[:n_seq], refs[n_seq + n_after :]
     gain, shift, weight, bias, key_mask, pick, ones, place = refs[:8]
-    normed_out, qkv_out, attended_out, rows, attended = refs[8:]
+    normed_out, qkv_out = refs[8:10]
+    attended_out, (rows, attended) = refs[10 : 10 + n_seq], refs[10 + n_seq :]
     piece = tokens[0].shape[0]
     total = n_seq * piece
     for r in range(n_seq):
@@ -120,34 +134,33 @@
             attended[at : at + block, :] = placed
         scores = following
     for r in range(n_seq):
-        attended_out[r] = attended[r * piece : (r + 1) * piece, :].astype(BF16)
+        attended_out[r][...] = attended[r * piece : (r + 1) * piece, :].astype(BF16)
 
 
 def slot_forward(pieces, gain, shift, weight, bias, key_mask, after=()):
     n_seq = len(pieces)
-    piece, width = pieces[0].shape
+    piece, width = pieces[0][0].shape[-2:]
     heads = weight.shape[1] // (3 * HEAD_DIM)
     total = n_seq * piece
     padded = round_up(total, LANES)
     return pl.pallas_call(
         partial(forward_kernel, n_seq, heads, len(after)),
-        in_specs=whole_specs(n_seq) + after_specs(after) + whole_specs(8),
+        grid=(1,),
+        in_specs=piece_specs(pieces) + after_specs(after) + whole_specs(8),
         out_shape=(
             jax.ShapeDtypeStruct((total, width), BF16),
             jax.ShapeDtypeStruct((3 * heads, padded, LANES), BF16),
-            jax.ShapeDtypeStruct((n_seq, piece, heads * HEAD_DIM), BF16),
+            *[jax.ShapeDtypeStruct((piece, heads * HEAD_DIM), BF16)] * n_seq,
         ),
         scratch_shapes=[
             pltpu.VMEM((total, width), F32),
             pltpu.VMEM((total, heads * HEAD_DIM), F32),
         ],
         compiler_params=pltpu.CompilerParams(vmem_limit_bytes=VMEM_BYTES),
-        cost_estimate=pl.CostEstimate(
-            flops=20 * 10**9, bytes_accessed=12 * 10**6, transcendentals=heads * total * total
-        ),
+        cost_estimate=cost(14),
         name="slot_forward",
     )(
-        *pieces, *after, gain, shift, weight, bias, key_mask, *lane_columns(heads),
+        *[p[0] for p in pieces], *after, gain, shift, weight, bias, key_mask, *lane_columns(heads),
         head_columns(heads, 1),
     )
 
@@ -156,8 +169,7 @@
     grads, refs = refs[:n_seq], refs[n_seq + n_after :]
     tokens, refs = refs[:n_seq], refs[n_seq:]
     qkv, normed, weight, before, place, spread = refs[:6]
-    outs, refs = refs[6 : 6 + n_seq], refs[6 + n_seq :]
-    grad_weight, vectors, grad_bias, rows, wide = refs
+    own, across, pairs, grad_weight, vectors, grad_bias, rows, wide = refs[6:]
     piece = grads[0].shape[0]
     total = n_seq * piece
     padded = qkv.shape[1]
@@ -214,7 +226,10 @@
         unit, _ = normalize(tokens[r][...].astype(F32))
         by_unit = by_unit + jnp.sum(share * unit, axis=0, keepdims=True)
         by_one = by_one + jnp.sum(share, axis=0, keepdims=True)
-        outs[r][...] = share.astype(outs[r].dtype)
+        if r & 1:
+            pairs[r // 2] = share.astype(BF16)
+        else:
+            (own if r == 0 else across)[...] = share
     vectors[...] = jnp.zeros(vectors.shape, F32)
     vectors[0:1, :] = by_unit
     vectors[1:2, :] = by_one
@@ -222,16 +237,18 @@
 
 def slot_backward(grads, tokens, qkv, normed, weight, before, after=()):
     n_seq = len(grads)
-    piece, width = grads[0].shape
+    piece, width = grads[0][0].shape[-2:]
     heads = qkv.shape[0] // 3
     total = n_seq * piece
     model = normed.shape[1]
-    share = lambda r: jax.ShapeDtypeStruct((piece, model), BF16 if r & 1 else F32)
     return pl.pallas_call(
         partial(backward_kernel, n_seq, heads, len(after)),
-        in_specs=whole_specs(n_seq) + after_specs(after) + whole_specs(n_seq + 6),
+        grid=(1,),
+        in_specs=piece_specs(grads) + after_specs(after) + piece_specs(tokens) + whole_specs(6),
         out_shape=(
-            *(share(r) for r in range(n_seq)),
+            jax.ShapeDtypeStruct((piece, model), F32),
+            jax.ShapeDtypeStruct((piece, model), F32),
+            jax.ShapeDtypeStruct((n_seq // 2, piece, model), BF16),
             jax.ShapeDtypeStruct((model, 3 * width), F32),
             jax.ShapeDtypeStruct((8, model), F32),
             jax.ShapeDtypeStruct((8, 3 * width), F32),
@@ -241,41 +258,46 @@
             pltpu.VMEM((total, model), F32),
         ],
         compiler_params=pltpu.CompilerParams(vmem_limit_bytes=VMEM_BYTES),
-        cost_estimate=pl.CostEstimate(
-            flops=28 * 10**9, bytes_accessed=12 * 10**6, transcendentals=heads * total * total
-        ),
+        cost_estimate=cost(12),
         name="slot_backward",
     )(
-        *grads, *after, *tokens, qkv, normed, weight, before, head_columns(heads, 1),
-        head_columns(heads, 3),
-    )
-
-
-def copy_kernel(count, n_after, *refs):
-    for source, target in zip(refs[:count], refs[count + n_after :]):
-        target[...] = source[...]
-
-
-def once_there(arrays, after):
+        *[g[0] for g in grads], *after, *[t[0] for t in tokens], qkv, normed, weight, before,
+        head_columns(heads, 1), head_columns(heads, 3),
+    )
+
+
+def gate_kernel(*refs):
+    pass
+
+
+def once_there(array, after):
     if not after:
-        return arrays
+        return array
     return pl.pallas_call(
-        partial(copy_kernel, len(arrays), len(after)),
-        in_specs=whole_specs(len(arrays)) + after_specs(after),
-        out_shape=tuple(jax.ShapeDtypeStruct(a.shape, a.dtype) for a in arrays),
+        gate_kernel,
+        in_specs=after_specs((array,) + tuple(after)),
+        out_specs=pl.BlockSpec(memory_space=pl.ANY),
+        out_shape=jax.ShapeDtypeStruct(array.shape, array.dtype),
+        input_output_aliases={0: 0},
         name="once_there",
-    )(*arrays, *after)
-
-
-def mlp_kernel(
-    tokens, attended, cotangent, valid, out_weight, bias_out, gain, shift, bias_down, up_own,
-    up_other, bias_up, down_own, down_other, layer_out, grad_residual, grad_attended,
-    grad_out_weight, vectors, grad_up_own, grad_up_other, grad_up_bias, grad_down_own,
-    grad_down_other, staged, residual, output, grad_norm, normed, normed_t, grad_out, heads_in,
-):
+    )(array, *after)
+
+
+def mlp_kernel(slots, groups, *refs):
+    attended, refs = refs[: slots * groups], refs[slots * groups :]
+    (
+        tokens, cotangent, valid, out_weight, bias_out, gain, shift, bias_down, up_own, up_other,
+        bias_up, down_own, down_other, layer_out, grad_residual,
+    ) = refs[:15]
+    grad_first, refs = refs[15 : 15 + groups], refs[15 + groups :]
+    grad_rest, refs = refs[:groups], refs[groups:]
+    (
+        grad_out_weight, vectors, grad_up_own, grad_up_other, grad_up_bias, grad_down_own,
+        grad_down_other, staged, residual, output, grad_norm, normed, normed_t, grad_out, heads_in,
+    ) = refs
     step = pl.program_id(0)
-    slots, piece, width = tokens.shape
-    groups = attended.shape[0]
+    piece, width = tokens.shape[1:]
+    head_width = attended[0].shape[-1]
     rows = slots * piece
     padded = residual.shape[0]
 
@@ -288,8 +310,11 @@
         if padded > rows:
             staged[rows:, :] = jnp.zeros((padded - rows, width), F32)
         for r in range(groups):
-            stage(attended.at[r])
-            heads_in[r] = staged[:, : attended.shape[-1]].astype(BF16)
+            for s in range(slots):
+                staged[s * piece : (s + 1) * piece, :head_width] = attended[r * slots + s][
+                    ...
+                ].astype(F32)
+            heads_in[r] = staged[:, :head_width].astype(BF16)
         stage(cotangent)
         grad_out[...] = (staged[...] * valid[...]).astype(BF16)
         stage(tokens)
@@ -352,19 +377,20 @@
         vectors[4:8, :] = jnp.zeros((4, width), F32)
         for r in range(groups):
             grad_out_weight[r] = mm(heads_in[r], branch, 0, 0).astype(BF16)
-            staged[:, : attended.shape[-1]] = mm(branch, out_weight[r], 1, 1)
-            for s in range(slots):
-                grad_attended[r, s] = staged[
-                    s * piece : (s + 1) * piece, : attended.shape[-1]
-                ].astype(BF16)
+            staged[:, :head_width] = mm(branch, out_weight[r], 1, 1)
+            grad_first[r][...] = staged[:piece, :head_width].astype(BF16)
+            for s in range(1, slots):
+                grad_rest[r][s - 1] = staged[s * piece : (s + 1) * piece, :head_width].astype(BF16)
 
 
 def feed_forward(
-    tokens, attended, cotangent, valid, out_weight, bias_out, gain, shift, bias_down, up_own,
+    attended, tokens, cotangent, valid, out_weight, bias_out, gain, shift, bias_down, up_own,
     up_other, bias_up, down_own, down_other,
 ):
     slots, piece, width = tokens.shape
-    groups, head_width = attended.shape[0], attended.shape[-1]
+    groups, head_width = len(attended), attended[0][0].shape[-1]
+    first = jax.ShapeDtypeStruct((piece, head_width), BF16)
+    others = jax.ShapeDtypeStruct((slots - 1, piece, head_width), BF16)
     ff = 2 * up_own.shape[1]
     chunk = 384
     half = ff // 2 // chunk
@@ -379,11 +405,11 @@
     bias_block = pl.BlockSpec((1, chunk), lambda i: (0, i))
     row = whole((1, width))
     return pl.pallas_call(
-        mlp_kernel,
+        partial(mlp_kernel, slots, groups),
         grid=(ff // chunk,),
         in_specs=[
+            *[whole(first.shape)] * (groups * slots),
             whole(tokens.shape),
-            whole(attended.shape),
             whole(cotangent.shape),
             whole((padded, 1)),
             whole(out_weight.shape),
@@ -398,7 +424,8 @@
         out_specs=[
             whole(tokens.shape),
             whole(tokens.shape),
-            whole(attended.shape),
+            *[whole(first.shape)] * groups,
+            *[whole(others.shape)] * groups,
             whole(out_weight.shape),
             whole((8, width)),
             *by_columns,
@@ -408,7 +435,8 @@
         out_shape=[
             jax.ShapeDtypeStruct(tokens.shape, BF16),
             jax.ShapeDtypeStruct(tokens.shape, F32),
-            jax.ShapeDtypeStruct(attended.shape, BF16),
+            *[first] * groups,
+            *[others] * groups,
             jax.ShapeDtypeStruct(out_weight.shape, BF16),
             jax.ShapeDtypeStruct((8, width), F32),
             jax.ShapeDtypeStruct(up_own.shape, BF16),
@@ -430,12 +458,10 @@
         compiler_params=pltpu.CompilerParams(
             vmem_limit_bytes=VMEM_BYTES, dimension_semantics=("arbitrary",)
         ),
-        cost_estimate=pl.CostEstimate(
-            flops=55 * 10**9, bytes_accessed=40 * 10**6, transcendentals=2 * padded * ff
-        ),
+        cost_estimate=cost(55),
         name="feed_forward",
     )(
-        tokens, attended, cotangent, valid, out_weight, bias_out, gain, shift, bias_down, up_own,
+        *[part for group in attended for part in group], tokens, cotangent, valid, out_weight, bias_out, gain, shift, bias_down, up_own,
         up_other, bias_up, down_own, down_other,
     )
 
@@ -515,24 +541,6 @@
 
 def scatter_img(parts):
     return lax.psum_scatter(parts, "img", scatter_dimension=0, tiled=False).astype(F32)
-
-
-def sum_vectors(parts):
-    arrived = [xor_send(parts, "seq", r) for r in range(1, 4)]
-    parts = (parts + arrived[0]) + (arrived[1] + arrived[2])
-    if not few_devices():
-        return lax.psum_scatter(parts, "img", scatter_dimension=0, tiled=False)
-    outer = lax.axis_size("img") // INNER
-    img = lax.axis_index("img")
-    z, y = img // INNER, img % INNER
-    split = parts.reshape(outer, INNER, -1)
-    mine = lax.dynamic_index_in_dim(split, z, 0, keepdims=False)
-    for k in range(1, outer):
-        mine = mine + outer_send(
-            lax.dynamic_index_in_dim(split, (z + k) % outer, 0, keepdims=False), k
-        )
-    send = lax.dynamic_index_in_dim(mine, 1 - y, 0, keepdims=False)
-    return lax.dynamic_index_in_dim(mine, y, 0, keepdims=False) + xor_send(send, "img", 1)
 
 
 def in_pair_order(own, other, axis):
@@ -596,44 +604,39 @@
         key_valid[:, None] | (jnp.arange(LANES) != HEAD_DIM)[None, :], 0.0, NEG
     ).astype(F32)
 
-    small = jnp.concatenate(
-        [norm_gain, norm_shift, out_bias, mlp_gain, mlp_shift, down_bias, qkv_bias, up_bias]
-    )
-    small_rows = round_up(-(-small.shape[0] // group), 16)
-    small = jnp.pad(small, (0, small_rows * group - small.shape[0])).reshape(small_rows, group)
+    small = [norm_gain, norm_shift, out_bias, mlp_gain, mlp_shift, down_bias, qkv_bias, up_bias]
+    small = [jnp.pad(v[None], ((0, 0), (0, group - v.shape[0]))) for v in small]
+    small.append(jnp.zeros((8, group), BF16))
     my_columns = lax.dynamic_slice_in_dim(qkv_weight, me * group, group, 1)
-    first_part, first_arrived = start_gather(jnp.concatenate([my_columns, small], axis=0))
-
-    slot_tokens = []
-    for slot in range(slot_count):
-        own = tokens[slot]
-        pair = xor_send(own, "seq", 1)
-        across = xor_send(own, "seq", 2)
-        slot_tokens.append([own, pair, across, xor_send(across, "seq", 1)])
+    first_part, first_arrived = start_gather(jnp.concatenate([my_columns] + small, axis=0))
+
+    pair = xor_send(tokens, "seq", 1)
+    across = [xor_send(tokens[0], "seq", 2), xor_send(tokens[1:], "seq", 2)]
+    diagonal = [xor_send(part, "seq", 1) for part in across]
+    slot_tokens = [[(tokens, 0), (pair, 0), (across[0],), (diagonal[0],)]]
+    for slot in range(1, slot_count):
+        slot_tokens.append(
+            [(tokens, slot), (pair, slot), (across[1], slot - 1), (diagonal[1], slot - 1)]
+        )
 
     my_up = lax.dynamic_index_in_dim(
         up_weight.reshape(shard, n_img, 2, ff_half), pair_me, 2, keepdims=False
     ).reshape(shard, -1)
-    my_down, my_second = once_there(
-        (
-            half_of(down_weight, 0, pair_me),
-            jnp.concatenate([my_up, half_of(out_weight, 1, pair_me)], axis=1),
-        ),
-        tuple(first_arrived or ()),
-    )
+    my_down = once_there(half_of(down_weight, 0, pair_me), tuple(first_arrived or ()))
     down_own = lax.all_gather(my_down, "img", axis=0).reshape(-1, model_width)
-    second_part, second_arrived = start_gather(my_second)
 
     first_set = end_gather(first_part, first_arrived)
+    my_second = jnp.concatenate([my_up, half_of(out_weight, 1, pair_me)], axis=1)
+    second_part, second_arrived = start_gather(once_there(my_second, (first_set,)))
     qkv_cols = first_set[:, :shard].reshape(model_width, group)
-    params = first_set[:, shard:].reshape(n_img, -1).astype(F32)
-
-    def param(start, width):
-        return params[:, start * shard : (start + width) * shard].reshape(-1)
+    params = first_set[:, shard:].astype(F32)
+
+    def param(row, width):
+        return params[:, row, : width * shard].reshape(-1)
 
     gain_first, shift_first, bias_out = param(0, 1)[None], param(1, 1)[None], param(2, 1)[None]
     gain_second, shift_second, bias_down = param(3, 1)[None], param(4, 1)[None], param(5, 1)[None]
-    pair_bias, bias_up = param(6, 2), param(8, 4).reshape(n_img, 2, ff_half)
+    pair_bias, bias_up = param(6, 2), param(7, 4).reshape(n_img, 2, ff_half)
     bias_up = jnp.concatenate(
         [
             lax.dynamic_index_in_dim(bias_up, which, 1, keepdims=False).reshape(1, -1)
@@ -652,9 +655,11 @@
     slot_normed, slot_qkv, slot_attended = [], [], []
     for slot in range(slot_count):
         after = ()
-        if slot == 1 and second_arrived is not None:
-            after = tuple(second_arrived)
-        normed, qkv_rows, attended = slot_forward(
+        if slot > 0:
+            after = (slot_attended[-1][0],)
+        if slot > 1:
+            after = after + tuple(slot_attended[-2][1:])
+        normed, qkv_rows, *attended = slot_forward(
             slot_tokens[slot], gain_first, shift_first, qkv_cols, head_bias, key_mask, after
         )
         slot_normed.append(normed)
@@ -662,6 +667,9 @@
         slot_attended.append(
             [attended[0]] + [xor_send(attended[r], "seq", r) for r in range(1, n_seq)]
         )
+    down_own = once_there(down_own, (slot_attended[-1][0],))
+    if second_arrived is not None:
+        second_arrived = [once_there(part, (slot_attended[1][0],)) for part in second_arrived]
     second_set = end_gather(second_part, second_arrived).reshape(model_width, -1)
     up_own, out_own = second_set[:, : ff // 2], second_set[:, ff // 2 :]
     up_other = xor_send(up_own, "seq", 1)
@@ -671,24 +679,11 @@
     out_groups = jnp.stack(
         [lax.dynamic_index_in_dim(out_full, me ^ r, 0, keepdims=False) for r in range(n_seq)]
     )
-    attended_groups = jnp.stack(
-        [jnp.stack([parts[r] for parts in slot_attended]) for r in range(n_seq)]
-    )
-
-    (
-        layer_out,
-        grad_residual,
-        grad_attended,
-        grad_out_groups,
-        vectors,
-        grad_up_own,
-        grad_up_other,
-        grad_up_bias,
-        grad_down_own,
-        grad_down_other,
-    ) = feed_forward(
+    attended_groups = [[parts[r] for parts in slot_attended] for r in range(n_seq)]
+
+    layer_out, grad_residual, *rest = feed_forward(
+        attended_groups,
         tokens,
-        attended_groups,
         cotangent,
         valid_rows,
         out_groups,
@@ -702,16 +697,19 @@
         down_own,
         down_other,
     )
-
-    slot_grads = []
-    for slot in range(slot_count):
-        slot_grads.append(
-            [grad_attended[0, slot]]
-            + [xor_send(grad_attended[r, slot], "seq", r) for r in range(1, n_seq)]
-        )
+    grad_first, grad_rest, rest = rest[:n_seq], rest[n_seq : 2 * n_seq], rest[2 * n_seq :]
+    grad_out_groups, vectors, grad_up_own, grad_up_other = rest[:4]
+    grad_up_bias, grad_down_own, grad_down_other = rest[4:]
+    for r in range(1, n_seq):
+        grad_first[r] = xor_send(grad_first[r], "seq", r)
+        grad_rest[r] = xor_send(grad_rest[r], "seq", r)
+    slot_grads = [[(part,) for part in grad_first]]
+    for slot in range(1, slot_count):
+        slot_grads.append([(part, slot - 1) for part in grad_rest])
 
     down_sum = grad_down_own.astype(F32) + xor_send(grad_down_other, "seq", 1).astype(F32)
-    own_down = scatter_img(down_sum.astype(BF16).reshape(n_img, ff_half, model_width))
+    down_sum = down_sum.astype(BF16).reshape(n_img, ff_half, model_width)
+    own_down = scatter_img(down_sum)
     up_sum = grad_up_own.astype(F32) + xor_send(grad_up_other, "seq", 1).astype(F32)
     grad_out_weight = jnp.concatenate(
         [lax.dynamic_index_in_dim(grad_out_groups, me ^ r, 0, keepdims=False) for r in range(n_seq)],
@@ -722,11 +720,11 @@
     ).astype(F32)
     second_grads = jnp.concatenate([up_sum, out_sum], axis=1).astype(BF16)
     second_grads = second_grads.reshape(n_img, shard, -1)
-    stages = [(), (), ()]
+    stages = [(down_sum, second_grads), (), ()]
     if few_devices():
         sums = reduce_inner(second_grads)
         own_second = reduce_outer(sums)
-        stages = [(), (), (sums,)]
+        stages[1:] = [(sums,), (own_second,)]
     else:
         own_second = scatter_img(second_grads)
 
@@ -735,7 +733,7 @@
     norm_sums = jnp.zeros((8, model_width), F32)
     own_sums = []
     for slot in range(slot_count):
-        *shares, grad_columns, slot_norm, slot_bias = slot_backward(
+        own, across, pairs, grad_columns, slot_norm, slot_bias = slot_backward(
             slot_grads[slot],
             slot_tokens[slot],
             slot_qkv[slot],
@@ -746,39 +744,9 @@
         )
         norm_sums += slot_norm
         bias_sums += slot_bias[0]
-        pair = xor_send(shares[1], "seq", 1).astype(F32)
-        across = xor_send(shares[3], "seq", 1).astype(F32)
-        across = xor_send((shares[2] + across).astype(BF16), "seq", 2)
-        own_sums.append(shares[0] + pair + across.astype(F32))
-    columns = grad_columns.astype(BF16).reshape(n_img, shard, group)
-    if few_devices():
-        own_columns = reduce_outer(reduce_inner(columns))
-    else:
-        own_columns = scatter_img(columns)
-    own_columns = own_columns.astype(BF16)
-
-    grad_norm_first = jnp.concatenate(own_sums, axis=0)
-    unit, factor = normalize(tokens.reshape(row_count, model_width).astype(F32))
-    scaled = grad_norm_first * gain_first
-    mean_scaled = jnp.mean(scaled, axis=-1, keepdims=True)
-    mean_product = jnp.mean(scaled * unit, axis=-1, keepdims=True)
-    grad_inputs = factor * (scaled - mean_scaled - unit * mean_product)
-    tokens_grad = grad_residual + grad_inputs.reshape(grad_residual.shape)
-
-    by_sender = jnp.stack(
-        [own_columns] + [xor_send(own_columns, "seq", r) for r in range(1, n_seq)]
-    )
-    share_qkv = jnp.concatenate(
-        [lax.dynamic_index_in_dim(by_sender, me ^ g, 0, keepdims=False) for g in range(n_seq)],
-        axis=1,
-    ).astype(F32)
-    second_low, second_other = over_pieces(own_second)
-    up_low = second_low[:, : ff // 2].reshape(shard, n_img, 1, ff_half)
-    up_there = second_other[:, : ff // 2].reshape(shard, n_img, 1, ff_half)
-    share_up = in_pair_order(up_low, up_there, 2).reshape(shard, ff).astype(F32)
-    share_out = in_pair_order(second_low[:, ff // 2 :], second_other[:, ff // 2 :], 1).astype(F32)
-    share_down = in_pair_order(*over_pieces(own_down), 0).astype(F32)
-
+        pairs = xor_send(pairs, "seq", 1)
+        across = xor_send((across + pairs[1].astype(F32)).astype(BF16), "seq", 2)
+        own_sums.append(own + pairs[0].astype(F32) + across.astype(F32))
     bias_sums = bias_sums.reshape(heads_here, 3, HEAD_DIM)
     grad_pairs = jnp.concatenate([bias_sums[:, :1], bias_sums[:, 2:]], axis=1).reshape(-1)
     grad_pairs = lax.dynamic_update_slice_in_dim(
@@ -796,7 +764,43 @@
         grad_up_bias,
         vectors[3],
     ]
-    mine = sum_vectors(jnp.concatenate([v.reshape(n_img, -1) for v in all_vectors], axis=1))
+    extra = jnp.concatenate([v.reshape(n_img, -1) for v in all_vectors], axis=1)
+    extra_rows = -(-extra.shape[1] // group)
+    extra = jnp.pad(extra, ((0, 0), (0, extra_rows * group - extra.shape[1])))
+    extra = jnp.pad(
+        extra.reshape(n_img, extra_rows, group), ((0, 0), (0, 16 - extra_rows), (0, 0))
+    )
+    columns = jnp.concatenate([grad_columns.reshape(n_img, shard, group), extra], axis=1)
+    columns = columns.astype(BF16)
+    if few_devices():
+        own_columns = reduce_outer(once_there(reduce_inner(columns), (pairs,)))
+    else:
+        own_columns = scatter_img(columns)
+    own_columns = own_columns.astype(BF16)
+
+    grad_norm_first = jnp.concatenate(own_sums, axis=0)
+    unit, factor = normalize(tokens.reshape(row_count, model_width).astype(F32))
+    scaled = grad_norm_first * gain_first
+    mean_scaled = jnp.mean(scaled, axis=-1, keepdims=True)
+    mean_product = jnp.mean(scaled * unit, axis=-1, keepdims=True)
+    grad_inputs = factor * (scaled - mean_scaled - unit * mean_product)
+    tokens_grad = grad_residual + grad_inputs.reshape(grad_residual.shape)
+
+    by_sender = jnp.stack(
+        [own_columns] + [xor_send(own_columns, "seq", r) for r in range(1, n_seq)]
+    )
+    by_sender = [
+        lax.dynamic_index_in_dim(by_sender, me ^ g, 0, keepdims=False) for g in range(n_seq)
+    ]
+    share_qkv = jnp.concatenate([part[:shard] for part in by_sender], axis=1).astype(F32)
+    mine = sum(part[shard : shard + extra_rows].astype(F32) for part in by_sender).reshape(-1)
+    second_low, second_other = over_pieces(own_second)
+    up_low = second_low[:, : ff // 2].reshape(shard, n_img, 1, ff_half)
+    up_there = second_other[:, : ff // 2].reshape(shard, n_img, 1, ff_half)
+    share_up = in_pair_order(up_low, up_there, 2).reshape(shard, ff).astype(F32)
+    share_out = in_pair_order(second_low[:, ff // 2 :], second_other[:, ff // 2 :], 1).astype(F32)
+    share_down = in_pair_order(*over_pieces(own_down), 0).astype(F32)
+
     shares, at = [], 0
     for v in all_vectors:
         size = v.shape[0] // n_img

time: 513 us -> 477 us (0.930)
  waiting for transfers between devices: 134 us -> 93.6 us
    ppermute x15 -> x12, waiting for transfers between devices: 52.6 us -> 5.23 us  [outer_send(): lax.ppermute(block, 'img', [(z * INNER + y, (z + shift) % outer * INNER +...]
    ppermute x15 -> x12, starting transfers between devices: 43.3 us -> 55.1 us  [outer_send(): lax.ppermute(block, 'img', [(z * INNER + y, (z + shift) % outer * INNER +...]
    ppermute x57 -> x43, starting transfers between devices: 40.5 us -> 31.5 us  [xor_send(): return lax.ppermute(block, axis, [(i, i ^ bits) for i in range(n)])]
    ppermute x57 -> x43, waiting for transfers between devices: 81 us -> 88.3 us  [xor_send(): return lax.ppermute(block, axis, [(i, i ^ bits) for i in range(n)])]
    unnamed x88 -> x108, local copies, waits for them, and re-layouts: 5.2 us -> 11.9 us
    concatenate x3, local copies, waits for them, and re-layouts: 5.86 us -> 0.42 us  [the longest x1 0.22 us: local(): jnp.concatenate([part[:shard] for part in by_sender], axis=1).astype(F32)]
    pallas_call x8 -> x14, Pallas kernels: 169 us -> 164 us  [the longest x3 77.2 us: slot_backward(): pl.pallas_call(partial(backward_kernel, n_seq, heads, len(after)), grid=(...]
    convert_element_type x7 -> x6, other arithmetic: 9.67 us -> 10.3 us  [the longest x3 4.73 us: local(): across = xor_send((across + pairs[1].astype(F32)).astype(BF16), 'seq', 2)]
  transfers between devices with their start and end apart: 74 -> 57, of which waited for: 23 -> 17; matrix products, arithmetic and copies ran while one was open for 18% -> 19% of each run, Pallas kernels for 23% -> 19%
where the time goes in v4:
time: 477 us; the launch traced here: 469 us
  Pallas kernels  164 us (34%)
  waiting for transfers between devices  93.6 us (20%)
  starting transfers between devices  86.6 us (18%)
  local copies, waits for them, and re-layouts  60.3 us (13%)
  other arithmetic  48.6 us (10%)
  between operations  15.8 us (3%)
    ppermute x43, waiting for transfers between devices, xor_send(): return lax.ppermute(block, axis, [(i, i ^ bits) for i in range(n)])  88.3 us
    pallas_call x3, Pallas kernels, slot_backward(): pl.pallas_call(partial(backward_kernel, n_seq, heads, len(after)), grid=(...  77.2 us
    ppermute x12, starting transfers between devices, outer_send(): lax.ppermute(block, 'img', [(z * INNER + y, (z + shift) % outer * INNER +...  55.1 us
    pallas_call x1, Pallas kernels, feed_forward(): pl.pallas_call(partial(mlp_kernel, slots, groups), grid=(ff // chunk,), i...  51.2 us
    pallas_call x3, Pallas kernels, slot_forward(): pl.pallas_call(partial(forward_kernel, n_seq, heads, len(after)), grid=(1...  35.8 us
    ppermute x43, starting transfers between devices, xor_send(): return lax.ppermute(block, axis, [(i, i ^ bits) for i in range(n)])  31.5 us
    unnamed x108, local copies, waits for them, and re-layouts  11.9 us
  transfers between devices with their start and end apart: 57, of which 17 were waited for; matrix products, arithmetic and copies ran while one was open for 19% of the time, Pallas kernels for 19%

profile of v4, /device:TPU:0, one launch (start us, length us, event | category | flops | bytes accessed | tf_op | source)
XLA Modules:
  0.0 469.1 jit_solution(17233112648505658774)
XLA Ops:
  13.7 3.1 collective-permute-start.3
  24.0 2.9 reshape.297
  40.2 15.1 %collective-permute-done.6 = bf16[4,112,576]{2,1,0:T(8,128)(2,1)S(1)} collective-permute-done((bf16[4,112,576]{2,1,0:T(8,128)(2,1)S(1)}, bf16[4,112,576]{2,1,0:T(8,128)(2,1)S(1)}, u32[]{:S(2)}, u32[]{:S(2)}) %collective-permute-start.6) | collective-permute-done | bytes 516128 | tf_op jit(solution)/shard_map/ppermute | solution.py:471
  61.6 3.4 collective-permute-start.20
  65.0 11.7 %slot_forward.3 = (bf16[1056,768]{1,0:T(8,128)(2,1)}, bf16[9,1152,128]{2,1,0:T(8,128)(2,1)}, bf16[264,192]{1,0:T(8,128)(2,1)}, bf16[264,192]{1,0:T(8,128)(2,1)},...) custom-call(bf16[3,264,768]{2,1,0:T(8,128)(2,1)} %refs_5_.3, ...), custom_call_target="tpu_custom_call" | custom-call | flops 14000000000 | bytes 10000000 | tf_op jit(solution)/shard_map/slot_forward/pallas_call | solution.py:146
  76.7 12.1 %slot_forward.4 = (bf16[1056,768]{1,0:T(8,128)(2,1)}, bf16[9,1152,128]{2,1,0:T(8,128)(2,1)}, bf16[264,192]{1,0:T(8,128)(2,1)}, bf16[264,192]{1,0:T(8,128)(2,1)},...) custom-call(bf16[3,264,768]{2,1,0:T(8,128)(2,1)} %refs_5_.3, ...), custom_call_target="tpu_custom_call" | custom-call | flops 14000000000 | bytes 10000000 | tf_op jit(solution)/shard_map/slot_forward/pallas_call | solution.py:146
  96.9 4.5 collective-permute-done.10.refs_6_
  104.1 11.9 %slot_forward.5 = (bf16[1056,768]{1,0:T(8,128)(2,1)}, bf16[9,1152,128]{2,1,0:T(8,128)(2,1)}, bf16[264,192]{1,0:T(8,128)(2,1)}, bf16[264,192]{1,0:T(8,128)(2,1)},...) custom-call(bf16[3,264,768]{2,1,0:T(8,128)(2,1)} %refs_5_.3, ...), custom_call_target="tpu_custom_call" | custom-call | flops 14000000000 | bytes 10000000 | tf_op jit(solution)/shard_map/slot_forward/pallas_call | solution.py:146
  116.0 11.9 %collective-permute-done.21 = bf16[4,96,1920]{2,1,0:T(8,128)(2,1)S(1)} collective-permute-done((bf16[4,96,1920]{2,1,0:T(8,128)(2,1)S(1)}, bf16[4,96,1920]{2,1,0:T(8,128)(2,1)S(1)}, u32[]{:S(2)}, u32[]{:S(2)}) %collective-permute-start.21) | collective-permute-done | bytes 1474592 | tf_op jit(solution)/shard_map/ppermute | solution.py:471
  140.6 3.6 collective-permute-done.15.refs_8_
  152.0 51.2 %feed_forward.1 = (bf16[3,264,768]{2,1,0:T(8,128)(2,1)}, f32[3,264,768]{2,1,0:T(8,128)}, bf16[264,192]{1,0:T(8,128)(2,1)}, bf16[264,192]{1,0:T(8,128)(2,1)}, bf1...) custom-call(bf16[264,192]{1,0:T(8,128)(2,1)} %get-tuple-element.67.r, ...), custom_call_target="tpu_custom_call" | custom-call | flops 54999998464 | bytes 10000000 | tf_op jit(solution)/shard_map/feed_forward/pallas_call | solution.py:407
  211.3 4.6 add_convert_fusion.1
  222.8 25.5 %slot_backward.3 = (f32[264,768]{1,0:T(8,128)}, f32[264,768]{1,0:T(8,128)}, bf16[2,264,768]{2,1,0:T(8,128)(2,1)}, f32[768,576]{1,0:T(8,128)}, f32[8,768]{1,0:T(8,128)}, /*index=5*/f32[8,576]{1,0:T(8,128)}) custom-call(bf16[264,192]{1,0:T(8,128)(2,1)} %get-tuple-element.81.refs_0_, bf16[264,192]{1,0:T(8,128)(2,1)} %copy-done.51, bf16[264,192]{1,0:T(8,128)(2,1)} %copy-done.52, ...), custom_call_target="tpu_custom_call" | custom-call | flops 12000000000 | bytes 10000000 | tf_op jit(solution)/shard_map/slot_backward/pallas_call | solution.py:244
  259.1 8.5 %collective-permute-done.32 = bf16[264,768]{1,0:T(8,128)(2,1)S(1)} collective-permute-done((bf16[264,768]{1,0:T(8,128)(2,1)}, bf16[264,768]{1,0:T(8,128)(2,1)S(1)}, u32[]{:S(2)}, u32[]{:S(2)}) %collective-permute-start.32) | collective-permute-done | bytes 405536 | tf_op jit(solution)/shard_map/ppermute | solution.py:471
  269.9 17.4 %collective-permute-done.36 = bf16[4,96,1920]{2,1,0:T(8,128)(2,1)} collective-permute-done((bf16[4,96,1920]{2,1,0:T(8,128)(2,1)}, bf16[4,96,1920]{2,1,0:T(8,128)(2,1)}, u32[]{:S(2)}, u32[]{:S(2)}) %collective-permute-start.36) | collective-permute-done | bytes 1474592 | tf_op jit(solution)/shard_map/ppermute | solution.py:471
  290.6 25.7 %collective-permute-start.39 = (bf16[96,1920]{1,0:T(8,128)(2,1)S(1)}, bf16[96,1920]{1,0:T(8,128)(2,1)S(1)}, u32[]{:S(2)}, u32[]{:S(2)}) collective-permute-start(bf16[96,1920]{1,0:T(8,128)(2,1)S(1)} %get-tuple-element.138), channel_id=1, source_target_pairs={{0,8},{4,12},{8,16},{12,20},{16,24},{20,28},{24,0},{28,4},{1,9},{5... | collective-permute-start | bytes 1105928 | tf_op jit(solution)/shard_map/ppermute | solution.py:479
  318.9 25.9 %slot_backward.4 = (f32[264,768]{1,0:T(8,128)}, f32[264,768]{1,0:T(8,128)}, bf16[2,264,768]{2,1,0:T(8,128)(2,1)}, f32[768,576]{1,0:T(8,128)}, f32[8,768]{1,0:T(8,128)}, /*index=5*/f32[8,576]{1,0:T(8,128)}) custom-call(bf16[2,264,192]{2,1,0:T(8,128)(2,1)} %get-tuple-element.95.refs_0_, bf16[2,264,192]{2,1,0:T(8,128)(2,1)} %collective-permute-done.33.refs_1_, ...), custom_call_target="tpu_custom_call" | custom-call | flops 12000000000 | bytes 10000000 | tf_op jit(solution)/shard_map/slot_backward/pallas_call | solution.py:244
  348.1 25.8 %slot_backward.5 = (f32[264,768]{1,0:T(8,128)}, f32[264,768]{1,0:T(8,128)}, bf16[2,264,768]{2,1,0:T(8,128)(2,1)}, f32[768,576]{1,0:T(8,128)}, f32[8,768]{1,0:T(8,128)}, /*index=5*/f32[8,576]{1,0:T(8,128)}) custom-call(bf16[2,264,192]{2,1,0:T(8,128)(2,1)} %get-tuple-element.95.refs_0_, bf16[2,264,192]{2,1,0:T(8,128)(2,1)} %collective-permute-done.33.refs_1_, ...), custom_call_target="tpu_custom_call" | custom-call | flops 12000000000 | bytes 10000000 | tf_op jit(solution)/shard_map/slot_backward/pallas_call | solution.py:244
  385.5 8.4 %collective-permute-done.44 = bf16[4,112,576]{2,1,0:T(8,128)(2,1)} collective-permute-done((bf16[4,112,576]{2,1,0:T(8,128)(2,1)}, bf16[4,112,576]{2,1,0:T(8,128)(2,1)}, u32[]{:S(2)}, u32[]{:S(2)}) %collective-permute-start.44) | collective-permute-done | bytes 516128 | tf_op jit(solution)/shard_map/ppermute | solution.py:471
  405.4 13.2 %collective-permute-start.45 = (bf16[112,576]{1,0:T(8,128)(2,1)S(1)}, bf16[112,576]{1,0:T(8,128)(2,1)S(1)}, u32[]{:S(2)}, u32[]{:S(2)}) collective-permute-start(bf16[112,576]{1,0:T(8,128)(2,1)S(1)} %get-tuple-element.153), channel_id=1, source_target_pairs={{0,8},{4,12},{8,16},{12,20},{16,24},{20,28},{24,0},{28,4},{1,9},{5... | collective-permute-start | bytes 387080 | tf_op jit(solution)/shard_map/ppermute | solution.py:479
  424.3 3.9 collective-permute-done.46
  433.2 2.8 collective-permute-done.49
  447.3 7.8 %collective-permute-done.53 = bf16[192,768]{1,0:T(8,128)(2,1)S(1)} collective-permute-done((bf16[192,768]{1,0:T(8,128)(2,1)}, bf16[192,768]{1,0:T(8,128)(2,1)S(1)}, u32[]{:S(2)}, u32[]{:S(2)}) %collective-permute-start.53) | collective-permute-done | bytes 294944 | tf_op jit(solution)/shard_map/ppermute | solution.py:471
  456.2 4.7 %fusion.7 = f32[3,264,768]{2,1,0:T(8,128)} fusion(f32[3,264,768]{2,1,0:T(8,128)} %get-tuple-element.80, bf16[3,264,768]{2,1,0:T(8,128)(2,1)S(1)} %copy-done.5, f32[3,264,768]{2,1,0:T(8,128)} %bitcast.160, f32[3,264]{1,0:T(4,128)S(1)} %broadcast_multiply_fusion, f32[3,264]{1,0:T(4,128)S(1)} %div.31, f32[768]{0:T(1024)S(1)} %mul.76, ...), kind=kLoop, calls=%fused_computation.19 | loop fusion | flops 5474304 | bytes 8531328 | tf_op jit(solution)/shard_map/add | solution.py:787
  (370 shorter events, 147.7 us)
Async XLA Ops:
  7.2 122.9 %all-gather.3.cloned.1.call-start = ((), (), s32[]{:S(2)}) async-start(), calls=%async_computation.2 | async-start | bytes 2654208 | tf_op jit(solution)/shard_map/all_gather | solution.py:626
  13.7 20.2 %collective-permute-start.3 = (bf16[112,576]{1,0:T(8,128)(2,1)S(1)}, bf16[112,576]{1,0:T(8,128)(2,1)}, u32[]{:S(2)}, u32[]{:S(2)}) collective-permute-start(bf16[112,576]{1,0:T(8,128)(2,1)S(1)} %concatenate.92), channel_id=1, source_target_pairs={{0,8},{4,12},{8,16},{12,20},{16,24},{20,28},{24,0},{28,4},{1,9},{5... | collective-permute-start | bytes 387080 | tf_op jit(solution)/shard_map/ppermute | solution.py:479
  20.8 44.2 %collective-permute-start = (bf16[3,264,768]{2,1,0:T(8,128)(2,1)}, bf16[3,264,768]{2,1,0:T(8,128)(2,1)}, u32[]{:S(2)}, u32[]{:S(2)}) collective-permute-start(bf16[3,264,768]{2,1,0:T(8,128)(2,1)} %refs_5_.3), channel_id=1, source_target_pairs={{0,1},{1,0},{2,3},{3,2},{4,5},{5,4},{6,7},{7,6},{8,9},{9,8},{10,11... | collective-permute-start | bytes 3649544 | tf_op jit(solution)/shard_map/ppermute | solution.py:471
  33.9 31.0 %collective-permute-start.7 = (bf16[2,264,768]{2,1,0:T(8,128)(2,1)}, bf16[2,264,768]{2,1,0:T(8,128)(2,1)}, u32[]{:S(2)}, u32[]{:S(2)}) collective-permute-start(bf16[2,264,768]{2,1,0:T(8,128)(2,1)} %slice.201), channel_id=1, source_target_pairs={{0,2},{1,3},{2,0},{3,1},{4,6},{5,7},{6,4},{7,5},{8,10},{9,11},{10,... | collective-permute-start | bytes 2433032 | tf_op jit(solution)/shard_map/ppermute | solution.py:471
  40.1 405.6 %reduce-scatter.2.cloned.1.call-start = ((), (), s32[]{:S(2)}) async-start(), calls=%async_computation.1 | async-start | bytes 2654208 | tf_op jit(solution)/shard_map/reduce_scatter | solution.py:543
  40.1 21.4 %collective-permute-start.2 = (bf16[264,768]{1,0:T(8,128)(2,1)}, bf16[264,768]{1,0:T(8,128)(2,1)}, u32[]{:S(2)}, u32[]{:S(2)}) collective-permute-start(bf16[264,768]{1,0:T(8,128)(2,1)} %collective-permute-done.1.refs_2_.refs_8_), channel_id=1, source_target_pairs={{0,1},{1,0},{2,3},{3,2},{4,5},{5,4},{6,7},{7,6},{8,9},{9,8},{10,11... | collective-permute-start | bytes 1216520 | tf_op jit(solution)/shard_map/ppermute | solution.py:471
  57.0 31.9 %collective-permute-start.18 = (bf16[96,1920]{1,0:T(8,128)(2,1)}, bf16[96,1920]{1,0:T(8,128)(2,1)S(1)}, u32[]{:S(2)}, u32[]{:S(2)}) collective-permute-start(bf16[96,1920]{1,0:T(8,128)(2,1)} %once_there.7), channel_id=1, source_target_pairs={{0,8},{4,12},{8,16},{12,20},{16,24},{20,28},{24,0},{28,4},{1,9},{5... | collective-permute-start | bytes 1105928 | tf_op jit(solution)/shard_map/ppermute | solution.py:479
  57.6 32.2 %collective-permute-start.19 = (bf16[96,1920]{1,0:T(8,128)(2,1)}, bf16[96,1920]{1,0:T(8,128)(2,1)S(1)}, u32[]{:S(2)}, u32[]{:S(2)}) collective-permute-start(bf16[96,1920]{1,0:T(8,128)(2,1)} %once_there.7), channel_id=1, source_target_pairs={{0,16},{4,20},{8,24},{12,28},{16,0},{20,4},{24,8},{28,12},{1,17},{... | collective-permute-start | bytes 1105928 | tf_op jit(solution)/shard_map/ppermute | solution.py:479
  61.6 29.0 %collective-permute-start.20 = (bf16[96,1920]{1,0:T(8,128)(2,1)S(1)}, bf16[96,1920]{1,0:T(8,128)(2,1)S(1)}, u32[]{:S(2)}, u32[]{:S(2)}) collective-permute-start(bf16[96,1920]{1,0:T(8,128)(2,1)S(1)} %copy-done.9), channel_id=1, source_target_pairs={{0,24},{4,28},{8,0},{12,4},{16,8},{20,12},{24,16},{28,20},{1,25},{... | collective-permute-start | bytes 1105928 | tf_op jit(solution)/shard_map/ppermute | solution.py:479
  93.4 34.5 %collective-permute-start.21 = (bf16[4,96,1920]{2,1,0:T(8,128)(2,1)S(1)}, bf16[4,96,1920]{2,1,0:T(8,128)(2,1)S(1)}, u32[]{:S(2)}, u32[]{:S(2)}) collective-permute-start(bf16[4,96,1920]{2,1,0:T(8,128)(2,1)S(1)} %bitcast_dynamic-update-slice_fusion), channel_id=1, source_target_pairs={{0,4},{4,0},{8,12},{12,8},{16,20},{20,16},{24,28},{28,24},{1,5},{5... | collective-permute-start | bytes 4423688 | tf_op jit(solution)/shard_map/ppermute | solution.py:471
  130.1 21.2 %collective-permute-start.23 = (bf16[768,1536]{1,0:T(8,128)(2,1)}, bf16[768,1536]{1,0:T(8,128)(2,1)}, u32[]{:S(2)}, u32[]{:S(2)}) collective-permute-start(bf16[768,1536]{1,0:T(8,128)(2,1)} %slice.266.refs_20_), channel_id=1, source_target_pairs={{0,1},{1,0},{2,3},{3,2},{4,5},{5,4},{6,7},{7,6},{8,9},{9,8},{10,11... | collective-permute-start | bytes 7077896 | tf_op jit(solution)/shard_map/ppermute | solution.py:471
  130.1 21.2 %collective-permute-start.24 = (bf16[1536,768]{1,0:T(8,128)(2,1)}, bf16[1536,768]{1,0:T(8,128)(2,1)}, u32[]{:S(2)}, u32[]{:S(2)}) collective-permute-start(bf16[1536,768]{1,0:T(8,128)(2,1)} %once_there.12.refs_23_), channel_id=1, source_target_pairs={{0,1},{1,0},{2,3},{3,2},{4,5},{5,4},{6,7},{7,6},{8,9},{9,8},{10,11... | collective-permute-start | bytes 7077896 | tf_op jit(solution)/shard_map/ppermute | solution.py:471
  251.3 35.9 %collective-permute-start.36 = (bf16[4,96,1920]{2,1,0:T(8,128)(2,1)}, bf16[4,96,1920]{2,1,0:T(8,128)(2,1)}, u32[]{:S(2)}, u32[]{:S(2)}) collective-permute-start(bf16[4,96,1920]{2,1,0:T(8,128)(2,1)} %fusion.10), channel_id=1, source_target_pairs={{0,4},{4,0},{8,12},{12,8},{16,20},{20,16},{24,28},{28,24},{1,5},{5... | collective-permute-start | bytes 4423688 | tf_op jit(solution)/shard_map/ppermute | solution.py:471
  256.8 60.3 %collective-permute-start.33 = (bf16[2,264,192]{2,1,0:T(8,128)(2,1)}, bf16[2,264,192]{2,1,0:T(8,128)(2,1)}, u32[]{:S(2)}, u32[]{:S(2)}) collective-permute-start(bf16[2,264,192]{2,1,0:T(8,128)(2,1)} %get-tuple-element.96), channel_id=1, source_target_pairs={{0,1},{1,0},{2,3},{3,2},{4,5},{5,4},{6,7},{7,6},{8,9},{9,8},{10,11... | collective-permute-start | bytes 608264 | tf_op jit(solution)/shard_map/ppermute | solution.py:471
  256.8 62.1 %collective-permute-start.34 = (bf16[2,264,192]{2,1,0:T(8,128)(2,1)}, bf16[2,264,192]{2,1,0:T(8,128)(2,1)}, u32[]{:S(2)}, u32[]{:S(2)}) collective-permute-start(bf16[2,264,192]{2,1,0:T(8,128)(2,1)} %get-tuple-element.97), channel_id=1, source_target_pairs={{0,2},{1,3},{2,0},{3,1},{4,6},{5,7},{6,4},{7,5},{8,10},{9,11},{10,... | collective-permute-start | bytes 608264 | tf_op jit(solution)/shard_map/ppermute | solution.py:471
  258.3 60.6 %collective-permute-start.35 = (bf16[2,264,192]{2,1,0:T(8,128)(2,1)}, bf16[2,264,192]{2,1,0:T(8,128)(2,1)}, u32[]{:S(2)}, u32[]{:S(2)}) collective-permute-start(bf16[2,264,192]{2,1,0:T(8,128)(2,1)} %get-tuple-element.98), channel_id=1, source_target_pairs={{0,3},{1,2},{2,1},{3,0},{4,7},{5,6},{6,5},{7,4},{8,11},{9,10},{10,... | collective-permute-start | bytes 608264 | tf_op jit(solution)/shard_map/ppermute | solution.py:471
  290.6 54.3 %collective-permute-start.39 = (bf16[96,1920]{1,0:T(8,128)(2,1)S(1)}, bf16[96,1920]{1,0:T(8,128)(2,1)S(1)}, u32[]{:S(2)}, u32[]{:S(2)}) collective-permute-start(bf16[96,1920]{1,0:T(8,128)(2,1)S(1)} %get-tuple-element.138), channel_id=1, source_target_pairs={{0,8},{4,12},{8,16},{12,20},{16,24},{20,28},{24,0},{28,4},{1,9},{5... | collective-permute-start | bytes 1105928 | tf_op jit(solution)/shard_map/ppermute | solution.py:479
  316.3 28.6 %collective-permute-start.40 = (bf16[96,1920]{1,0:T(8,128)(2,1)S(1)}, bf16[96,1920]{1,0:T(8,128)(2,1)S(1)}, u32[]{:S(2)}, u32[]{:S(2)}) collective-permute-start(bf16[96,1920]{1,0:T(8,128)(2,1)S(1)} %get-tuple-element.140), channel_id=1, source_target_pairs={{0,16},{4,20},{8,24},{12,28},{16,0},{20,4},{24,8},{28,12},{1,17},{... | collective-permute-start | bytes 1105928 | tf_op jit(solution)/shard_map/ppermute | solution.py:479
  317.0 28.9 %collective-permute-start.41 = (bf16[96,1920]{1,0:T(8,128)(2,1)S(1)}, bf16[96,1920]{1,0:T(8,128)(2,1)S(1)}, u32[]{:S(2)}, u32[]{:S(2)}) collective-permute-start(bf16[96,1920]{1,0:T(8,128)(2,1)S(1)} %get-tuple-element.139), channel_id=1, source_target_pairs={{0,24},{4,28},{8,0},{12,4},{16,8},{20,12},{24,16},{28,20},{1,25},{... | collective-permute-start | bytes 1105928 | tf_op jit(solution)/shard_map/ppermute | solution.py:479
  344.8 36.6 %collective-permute-start.37 = (bf16[2,264,768]{2,1,0:T(8,128)(2,1)}, bf16[2,264,768]{2,1,0:T(8,128)(2,1)}, u32[]{:S(2)}, u32[]{:S(2)}) collective-permute-start(bf16[2,264,768]{2,1,0:T(8,128)(2,1)} %get-tuple-element.103), channel_id=1, source_target_pairs={{0,1},{1,0},{2,3},{3,2},{4,5},{5,4},{6,7},{7,6},{8,9},{9,8},{10,11... | collective-permute-start | bytes 2433032 | tf_op jit(solution)/shard_map/ppermute | solution.py:471
  348.1 32.3 %collective-permute-start.51 = (bf16[96,1920]{1,0:T(8,128)(2,1)S(1)}, bf16[96,1920]{1,0:T(8,128)(2,1)S(1)}, u32[]{:S(2)}, u32[]{:S(2)}) collective-permute-start(bf16[96,1920]{1,0:T(8,128)(2,1)S(1)} %get-tuple-element.136), channel_id=1, source_target_pairs={{0,2},{1,3},{2,0},{3,1},{4,6},{5,7},{6,4},{7,5},{8,10},{9,11},{10,... | collective-permute-start | bytes 1105928 | tf_op jit(solution)/shard_map/ppermute | solution.py:471
  380.4 22.9 %collective-permute-start.42 = (bf16[2,264,768]{2,1,0:T(8,128)(2,1)}, bf16[2,264,768]{2,1,0:T(8,128)(2,1)S(1)}, u32[]{:S(2)}, u32[]{:S(2)}) collective-permute-start(bf16[2,264,768]{2,1,0:T(8,128)(2,1)} %get-tuple-element.109), channel_id=1, source_target_pairs={{0,1},{1,0},{2,3},{3,2},{4,5},{5,4},{6,7},{7,6},{8,9},{9,8},{10,11... | collective-permute-start | bytes 2433032 | tf_op jit(solution)/shard_map/ppermute | solution.py:471
  383.5 47.7 %collective-permute-start.38 = (bf16[264,768]{1,0:T(8,128)(2,1)}, bf16[264,768]{1,0:T(8,128)(2,1)S(1)}, u32[]{:S(2)}, u32[]{:S(2)}) collective-permute-start(bf16[264,768]{1,0:T(8,128)(2,1)} %fusion.15), channel_id=1, source_target_pairs={{0,2},{1,3},{2,0},{3,1},{4,6},{5,7},{6,4},{7,5},{8,10},{9,11},{10,... | collective-permute-start | bytes 1216520 | tf_op jit(solution)/shard_map/ppermute | solution.py:471
  422.9 19.0 %collective-permute-start.43 = (bf16[264,768]{1,0:T(8,128)(2,1)}, bf16[264,768]{1,0:T(8,128)(2,1)}, u32[]{:S(2)}, u32[]{:S(2)}) collective-permute-start(bf16[264,768]{1,0:T(8,128)(2,1)} %fusion.13), channel_id=1, source_target_pairs={{0,2},{1,3},{2,0},{3,1},{4,6},{5,7},{6,4},{7,5},{8,10},{9,11},{10,... | collective-permute-start | bytes 1216520 | tf_op jit(solution)/shard_map/ppermute | solution.py:471
  (87 other events, 604.6 us)
Sparse Core Ops, SparseCore 0:
  40.2 71.5 all-gather.2
  259.2 98.5 reduce-scatter.1

commit v5 on v4

--- a/solution.py
+++ b/solution.py
@@ -258,7 +258,7 @@
             pltpu.VMEM((total, model), F32),
         ],
         compiler_params=pltpu.CompilerParams(vmem_limit_bytes=VMEM_BYTES),
-        cost_estimate=cost(12),
+        cost_estimate=cost(1),
         name="slot_backward",
     )(
         *[g[0] for g in grads], *after, *[t[0] for t in tokens], qkv, normed, weight, before,
@@ -500,8 +500,8 @@
     return placed
 
 
-def gather_inner(placed):
-    other = xor_send(placed, "img", 1)
+def gather_inner(placed, after=()):
+    other = once_there(xor_send(placed, "img", 1), after)
     first = (lax.axis_index("img") & 1) == 0
     both = jnp.stack([jnp.where(first, placed, other), jnp.where(first, other, placed)], axis=1)
     return both.reshape((-1,) + placed.shape[1:])
@@ -514,10 +514,10 @@
     return block, [outer_send(block, k) for k in range(1, outer)]
 
 
-def end_gather(block, arrived):
+def end_gather(block, arrived, after=()):
     if arrived is None:
         return block
-    return gather_inner(place_outer(block, arrived))
+    return gather_inner(place_outer(block, arrived), after)
 
 
 def reduce_inner(parts):
@@ -670,7 +670,8 @@
     down_own = once_there(down_own, (slot_attended[-1][0],))
     if second_arrived is not None:
         second_arrived = [once_there(part, (slot_attended[1][0],)) for part in second_arrived]
-    second_set = end_gather(second_part, second_arrived).reshape(model_width, -1)
+    sent = tuple(part for parts in slot_attended for part in parts[1:])
+    second_set = end_gather(second_part, second_arrived, sent).reshape(model_width, -1)
     up_own, out_own = second_set[:, : ff // 2], second_set[:, ff // 2 :]
     up_other = xor_send(up_own, "seq", 1)
     down_other = xor_send(down_own, "seq", 1)
@@ -708,8 +709,6 @@
         slot_grads.append([(part, slot - 1) for part in grad_rest])
 
     down_sum = grad_down_own.astype(F32) + xor_send(grad_down_other, "seq", 1).astype(F32)
-    down_sum = down_sum.astype(BF16).reshape(n_img, ff_half, model_width)
-    own_down = scatter_img(down_sum)
     up_sum = grad_up_own.astype(F32) + xor_send(grad_up_other, "seq", 1).astype(F32)
     grad_out_weight = jnp.concatenate(
         [lax.dynamic_index_in_dim(grad_out_groups, me ^ r, 0, keepdims=False) for r in range(n_seq)],
@@ -718,21 +717,20 @@
     out_sum = half_of(grad_out_weight, 1, pair_me).astype(F32) + xor_send(
         half_of(grad_out_weight, 1, 1 - pair_me), "seq", 1
     ).astype(F32)
-    second_grads = jnp.concatenate([up_sum, out_sum], axis=1).astype(BF16)
-    second_grads = second_grads.reshape(n_img, shard, -1)
-    stages = [(down_sum, second_grads), (), ()]
-    if few_devices():
-        sums = reduce_inner(second_grads)
-        own_second = reduce_outer(sums)
-        stages[1:] = [(sums,), (own_second,)]
-    else:
-        own_second = scatter_img(second_grads)
+    second_grads = jnp.concatenate(
+        [up_sum.astype(BF16), out_sum.astype(BF16), down_sum.astype(BF16).reshape(model_width, -1)],
+        axis=1,
+    ).reshape(n_img, shard, -1)
+    own_second = scatter_img(second_grads)
 
     grad_columns = jnp.zeros((model_width, group), F32)
     bias_sums = jnp.zeros((group,), F32)
     norm_sums = jnp.zeros((8, model_width), F32)
-    own_sums = []
+    own_sums, arrivals = [], []
     for slot in range(slot_count):
+        after = (second_grads,) if slot == 0 else ()
+        if slot > 1:
+            after = (arrivals[-2][0],)
         own, across, pairs, grad_columns, slot_norm, slot_bias = slot_backward(
             slot_grads[slot],
             slot_tokens[slot],
@@ -740,13 +738,14 @@
             slot_normed[slot],
             qkv_cols,
             grad_columns,
-            stages[min(slot, 2)],
+            after,
         )
         norm_sums += slot_norm
         bias_sums += slot_bias[0]
         pairs = xor_send(pairs, "seq", 1)
         across = xor_send((across + pairs[1].astype(F32)).astype(BF16), "seq", 2)
         own_sums.append(own + pairs[0].astype(F32) + across.astype(F32))
+        arrivals.append((pairs, across))
     bias_sums = bias_sums.reshape(heads_here, 3, HEAD_DIM)
     grad_pairs = jnp.concatenate([bias_sums[:, :1], bias_sums[:, 2:]], axis=1).reshape(-1)
     grad_pairs = lax.dynamic_update_slice_in_dim(
@@ -771,7 +770,7 @@
         extra.reshape(n_img, extra_rows, group), ((0, 0), (0, 16 - extra_rows), (0, 0))
     )
     columns = jnp.concatenate([grad_columns.reshape(n_img, shard, group), extra], axis=1)
-    columns = columns.astype(BF16)
+    columns = once_there(columns.astype(BF16), (arrivals[-2][0],))
     if few_devices():
         own_columns = reduce_outer(once_there(reduce_inner(columns), (pairs,)))
     else:
@@ -795,11 +794,16 @@
     share_qkv = jnp.concatenate([part[:shard] for part in by_sender], axis=1).astype(F32)
     mine = sum(part[shard : shard + extra_rows].astype(F32) for part in by_sender).reshape(-1)
     second_low, second_other = over_pieces(own_second)
-    up_low = second_low[:, : ff // 2].reshape(shard, n_img, 1, ff_half)
-    up_there = second_other[:, : ff // 2].reshape(shard, n_img, 1, ff_half)
+    cuts = (ff // 2, ff // 2 + model_width // 2)
+    up_low, out_low, down_low = jnp.split(second_low, cuts, axis=1)
+    up_there, out_there, down_there = jnp.split(second_other, cuts, axis=1)
+    up_low = up_low.reshape(shard, n_img, 1, ff_half)
+    up_there = up_there.reshape(shard, n_img, 1, ff_half)
     share_up = in_pair_order(up_low, up_there, 2).reshape(shard, ff).astype(F32)
-    share_out = in_pair_order(second_low[:, ff // 2 :], second_other[:, ff // 2 :], 1).astype(F32)
-    share_down = in_pair_order(*over_pieces(own_down), 0).astype(F32)
+    share_out = in_pair_order(out_low, out_there, 1).astype(F32)
+    down_low = down_low.reshape(ff_half, model_width)
+    down_there = down_there.reshape(ff_half, model_width)
+    share_down = in_pair_order(down_low, down_there, 0).astype(F32)
 
     shares, at = [], 0
     for v in all_vectors:

time: 477 us -> 455 us (0.954)
  starting transfers between devices: 86.6 us -> 45.6 us
  Pallas kernels: 164 us -> 177 us
  local copies, waits for them, and re-layouts: 60.3 us -> 70.5 us
    ppermute x12 -> x9, starting transfers between devices: 55.1 us -> 20.2 us  [outer_send(): lax.ppermute(block, 'img', [(z * INNER + y, (z + shift) % outer * INNER +...]
    pallas_call x3, Pallas kernels: 35.8 us -> 47.4 us  [slot_forward(): pl.pallas_call(partial(forward_kernel, n_seq, heads, len(after)), grid=(1...]
    ppermute x43 -> x40, starting transfers between devices: 31.5 us -> 25.3 us  [xor_send(): return lax.ppermute(block, axis, [(i, i ^ bits) for i in range(n)])]
    unnamed x108 -> x116, local copies, waits for them, and re-layouts: 11.9 us -> 10.4 us
    ppermute x43 -> x40, waiting for transfers between devices: 88.3 us -> 89 us  [xor_send(): return lax.ppermute(block, axis, [(i, i ^ bits) for i in range(n)])]
  transfers between devices with their start and end apart: 57 -> 51, of which waited for: 17 -> 20; matrix products, arithmetic and copies ran while one was open for 19% -> 18% of each run, Pallas kernels for 19% -> 28%
where the time goes in v5:
time: 455 us; the launch traced here: 447 us
  Pallas kernels  177 us (39%)
  waiting for transfers between devices  93.9 us (21%)
  local copies, waits for them, and re-layouts  70.5 us (15%)
  starting transfers between devices  45.6 us (10%)
  other arithmetic  44.5 us (10%)
  between operations  15.9 us (3%)
    ppermute x40, waiting for transfers between devices, xor_send(): return lax.ppermute(block, axis, [(i, i ^ bits) for i in range(n)])  89 us
    pallas_call x3, Pallas kernels, slot_backward(): pl.pallas_call(partial(backward_kernel, n_seq, heads, len(after)), grid=(...  78 us
    pallas_call x1, Pallas kernels, feed_forward(): pl.pallas_call(partial(mlp_kernel, slots, groups), grid=(ff // chunk,), i...  51.3 us
    pallas_call x3, Pallas kernels, slot_forward(): pl.pallas_call(partial(forward_kernel, n_seq, heads, len(after)), grid=(1...  47.4 us
    ppermute x40, starting transfers between devices, xor_send(): return lax.ppermute(block, axis, [(i, i ^ bits) for i in range(n)])  25.3 us
    ppermute x9, starting transfers between devices, outer_send(): lax.ppermute(block, 'img', [(z * INNER + y, (z + shift) % outer * INNER +...  20.2 us
    dynamic_update_slice x8, local copies, waits for them, and re-layouts, place_outer(): lax.dynamic_update_slice_in_dim(placed, part[None], (z + outer - k) % out...  10.4 us
    unnamed x116, local copies, waits for them, and re-layouts  10.4 us
  transfers between devices with their start and end apart: 51, of which 20 were waited for; matrix products, arithmetic and copies ran while one was open for 18% of the time, Pallas kernels for 28%

profile of v5, /device:TPU:0, one launch (start us, length us, event | category | flops | bytes accessed | tf_op | source)
XLA Modules:
  0.0 447.2 jit_solution(5527942037381173488)
XLA Ops:
  25.8 3.5 reshape.292
  29.3 3.7 dynamic-slice_reduce_fusion
  49.7 15.3 %collective-permute-done.6 = bf16[4,112,576]{2,1,0:T(8,128)(2,1)S(1)} collective-permute-done((bf16[4,112,576]{2,1,0:T(8,128)(2,1)}, bf16[4,112,576]{2,1,0:T(8,128)(2,1)S(1)}, u32[]{:S(2)}, u32[]{:S(2)}) %collective-permute-start.6) | collective-permute-done | bytes 516128 | tf_op jit(solution)/shard_map/ppermute | solution.py:471
  72.4 3.4 collective-permute-start.20
  76.9 11.7 %slot_forward.3 = (bf16[1056,768]{1,0:T(8,128)(2,1)}, bf16[9,1152,128]{2,1,0:T(8,128)(2,1)}, bf16[264,192]{1,0:T(8,128)(2,1)}, bf16[264,192]{1,0:T(8,128)(2,1)},...) custom-call(bf16[3,264,768]{2,1,0:T(8,128)(2,1)} %refs_5_.3, bf16[3,264,768]{2,1,0:T(8,128)(2,1)} %copy-done.8, ...), custom_call_target="tpu_custom_call" | custom-call | flops 14000000000 | bytes 10000000 | tf_op jit(solution)/shard_map/slot_forward/pallas_call | solution.py:146
  90.5 24.0 %slot_forward.4 = (bf16[1056,768]{1,0:T(8,128)(2,1)}, bf16[9,1152,128]{2,1,0:T(8,128)(2,1)}, bf16[264,192]{1,0:T(8,128)(2,1)}, bf16[264,192]{1,0:T(8,128)(2,1)},...) custom-call(bf16[3,264,768]{2,1,0:T(8,128)(2,1)} %refs_5_.3, bf16[3,264,768]{2,1,0:T(8,128)(2,1)} %copy-done.8, ...), custom_call_target="tpu_custom_call" | custom-call | flops 14000000000 | bytes 10000000 | tf_op jit(solution)/shard_map/slot_forward/pallas_call | solution.py:146
  120.2 11.7 %slot_forward.5 = (bf16[1056,768]{1,0:T(8,128)(2,1)}, bf16[9,1152,128]{2,1,0:T(8,128)(2,1)}, bf16[264,192]{1,0:T(8,128)(2,1)}, bf16[264,192]{1,0:T(8,128)(2,1)},...) custom-call(bf16[3,264,768]{2,1,0:T(8,128)(2,1)} %refs_5_.3, bf16[3,264,768]{2,1,0:T(8,128)(2,1)} %copy-done.8, ...), custom_call_target="tpu_custom_call" | custom-call | flops 14000000000 | bytes 10000000 | tf_op jit(solution)/shard_map/slot_forward/pallas_call | solution.py:146
  140.7 3.8 collective-permute-done.14.refs_5_.refs_7_
  147.1 5.4 %collective-permute-done.21.refs_0_ = bf16[4,96,1920]{2,1,0:T(8,128)(2,1)S(1)} collective-permute-done((bf16[4,96,1920]{2,1,0:T(8,128)(2,1)S(1)}, bf16[4,96,1920]{2,1,0:T(8,128)(2,1)S(1)}, u32[]{:S(2)}, u32[]{:S(2)}) %collective-permute-start.21) | collective-permute-done | bytes 1474592 | tf_op jit(solution)/shard_map/ppermute | solution.py:471
  166.4 51.3 %feed_forward.1 = (bf16[3,264,768]{2,1,0:T(8,128)(2,1)}, f32[3,264,768]{2,1,0:T(8,128)}, bf16[264,192]{1,0:T(8,128)(2,1)}, bf16[264,192]{1,0:T(8,128)(2,1)}, bf1...) custom-call(bf16[264,192]{1,0:T(8,128)(2,1)} %get-tuple-element.67.r, ...), custom_call_target="tpu_custom_call" | custom-call | flops 54999998464 | bytes 10000000 | tf_op jit(solution)/shard_map/feed_forward/pallas_call | solution.py:407
  220.0 6.0 %collective-permute-done.29 = bf16[768,384]{1,0:T(8,128)(2,1)S(1)} collective-permute-done((bf16[768,384]{1,0:T(8,128)(2,1)S(1)}, bf16[768,384]{1,0:T(8,128)(2,1)S(1)}, u32[]{:S(2)}, u32[]{:S(2)}) %collective-permute-start.29) | collective-permute-done | bytes 589856 | tf_op jit(solution)/shard_map/ppermute | solution.py:471
  232.1 3.1 add_convert_fusion.1
  241.8 4.7 %collective-permute-done.26.refs_2_ = bf16[264,192]{1,0:T(8,128)(2,1)S(1)} collective-permute-done((bf16[264,192]{1,0:T(8,128)(2,1)S(1)}, bf16[264,192]{1,0:T(8,128)(2,1)S(1)}, u32[]{:S(2)}, u32[]{:S(2)}) %collective-permute-start.26) | collective-permute-done | bytes 101408 | tf_op jit(solution)/shard_map/ppermute | solution.py:471
  249.7 25.8 %slot_backward.3 = (f32[264,768]{1,0:T(8,128)}, f32[264,768]{1,0:T(8,128)}, bf16[2,264,768]{2,1,0:T(8,128)(2,1)}, f32[768,576]{1,0:T(8,128)}, f32[8,768]{1,0:T(8,128)}, /*index=5*/f32[8,576]{1,0:T(8,128)}) custom-call(bf16[264,192]{1,0:T(8,128)(2,1)} %get-tuple-element.81.refs_0_, bf16[264,192]{1,0:T(8,128)(2,1)} %copy-done.38, bf16[264,192]{1,0:T(8,128)(2,1)} %copy-done.39, ...), custom_call_target="tpu_custom_call" | custom-call | flops 1000000000 | bytes 10000000 | tf_op jit(solution)/shard_map/slot_backward/pallas_call | solution.py:244
  279.8 7.0 %collective-permute-done.34.refs_2_ = bf16[2,264,192]{2,1,0:T(8,128)(2,1)S(1)} collective-permute-done((bf16[2,264,192]{2,1,0:T(8,128)(2,1)S(1)}, bf16[2,264,192]{2,1,0:T(8,128)(2,1)S(1)}, u32[]{:S(2)}, u32[]{:S(2)}) %collective-permute-start.34) | collective-permute-done | bytes 202784 | tf_op jit(solution)/shard_map/ppermute | solution.py:471
  286.8 4.7 %collective-permute-done.35.refs_3_ = bf16[2,264,192]{2,1,0:T(8,128)(2,1)S(1)} collective-permute-done((bf16[2,264,192]{2,1,0:T(8,128)(2,1)S(1)}, bf16[2,264,192]{2,1,0:T(8,128)(2,1)S(1)}, u32[]{:S(2)}, u32[]{:S(2)}) %collective-permute-start.35) | collective-permute-done | bytes 202784 | tf_op jit(solution)/shard_map/ppermute | solution.py:471
  292.2 26.1 %slot_backward.4 = (f32[264,768]{1,0:T(8,128)}, f32[264,768]{1,0:T(8,128)}, bf16[2,264,768]{2,1,0:T(8,128)(2,1)}, f32[768,576]{1,0:T(8,128)}, f32[8,768]{1,0:T(8,128)}, /*index=5*/f32[8,576]{1,0:T(8,128)}) custom-call(bf16[2,264,192]{2,1,0:T(8,128)(2,1)} %get-tuple-element.95.refs_0_, bf16[2,264,192]{2,1,0:T(8,128)(2,1)} %copy-done.24, ...), custom_call_target="tpu_custom_call" | custom-call | flops 1000000000 | bytes 10000000 | tf_op jit(solution)/shard_map/slot_backward/pallas_call | solution.py:244
  320.0 26.1 %slot_backward.5 = (f32[264,768]{1,0:T(8,128)}, f32[264,768]{1,0:T(8,128)}, bf16[2,264,768]{2,1,0:T(8,128)(2,1)}, f32[768,576]{1,0:T(8,128)}, f32[8,768]{1,0:T(8,128)}, /*index=5*/f32[8,576]{1,0:T(8,128)}) custom-call(bf16[2,264,192]{2,1,0:T(8,128)(2,1)} %get-tuple-element.95.refs_0_, bf16[2,264,192]{2,1,0:T(8,128)(2,1)} %copy-done.24, ...), custom_call_target="tpu_custom_call" | custom-call | flops 1000000000 | bytes 10000000 | tf_op jit(solution)/shard_map/slot_backward/pallas_call | solution.py:244
  365.0 6.8 %collective-permute-done.40 = bf16[4,112,576]{2,1,0:T(8,128)(2,1)S(1)} collective-permute-done((bf16[4,112,576]{2,1,0:T(8,128)(2,1)S(1)}, bf16[4,112,576]{2,1,0:T(8,128)(2,1)S(1)}, u32[]{:S(2)}, u32[]{:S(2)}) %collective-permute-start.40) | collective-permute-done | bytes 516128 | tf_op jit(solution)/shard_map/ppermute | solution.py:471
  375.1 6.5 %collective-permute-start.41 = (bf16[112,576]{1,0:T(8,128)(2,1)S(1)}, bf16[112,576]{1,0:T(8,128)(2,1)S(1)}, u32[]{:S(2)}, u32[]{:S(2)}) collective-permute-start(bf16[112,576]{1,0:T(8,128)(2,1)S(1)} %get-tuple-element.148), channel_id=1, source_target_pairs={{0,8},{4,12},{8,16},{12,20},{16,24},{20,28},{24,0},{28,4},{1,9},{5... | collective-permute-start | bytes 387080 | tf_op jit(solution)/shard_map/ppermute | solution.py:479
  385.8 4.6 %collective-permute-done.42 = bf16[112,576]{1,0:T(8,128)(2,1)S(1)} collective-permute-done((bf16[112,576]{1,0:T(8,128)(2,1)S(1)}, bf16[112,576]{1,0:T(8,128)(2,1)S(1)}, u32[]{:S(2)}, u32[]{:S(2)}) %collective-permute-start.42) | collective-permute-done | bytes 129056 | tf_op jit(solution)/shard_map/ppermute | solution.py:479
  395.1 3.1 collective-permute-done.45
  403.7 5.9 %collective-permute-done.39 = bf16[264,768]{1,0:T(8,128)(2,1)} collective-permute-done((bf16[264,768]{1,0:T(8,128)(2,1)}, bf16[264,768]{1,0:T(8,128)(2,1)}, u32[]{:S(2)}, u32[]{:S(2)}) %collective-permute-start.39) | collective-permute-done | bytes 405536 | tf_op jit(solution)/shard_map/ppermute | solution.py:471
  416.1 13.3 %collective-permute-done.47 = bf16[96,3456]{1,0:T(8,128)(2,1)} collective-permute-done((bf16[96,3456]{1,0:T(8,128)(2,1)}, bf16[96,3456]{1,0:T(8,128)(2,1)}, u32[]{:S(2)}, u32[]{:S(2)}) %collective-permute-start.47) | collective-permute-done | bytes 663584 | tf_op jit(solution)/shard_map/ppermute | solution.py:471
  (368 shorter events, 153.6 us)
Async XLA Ops:
  7.2 150.1 %all-gather.3.cloned.1.call-start = ((), (), s32[]{:S(2)}) async-start(), calls=%async_computation.2 | async-start | bytes 2654208 | tf_op jit(solution)/shard_map/all_gather | solution.py:626
  15.6 26.0 %collective-permute-start.3 = (bf16[112,576]{1,0:T(8,128)(2,1)}, bf16[112,576]{1,0:T(8,128)(2,1)}, u32[]{:S(2)}, u32[]{:S(2)}) collective-permute-start(bf16[112,576]{1,0:T(8,128)(2,1)} %concatenate.80), channel_id=1, source_target_pairs={{0,8},{4,12},{8,16},{12,20},{16,24},{20,28},{24,0},{28,4},{1,9},{5... | collective-permute-start | bytes 387080 | tf_op jit(solution)/shard_map/ppermute | solution.py:479
  18.6 25.1 %collective-permute-start.4 = (bf16[112,576]{1,0:T(8,128)(2,1)}, bf16[112,576]{1,0:T(8,128)(2,1)}, u32[]{:S(2)}, u32[]{:S(2)}) collective-permute-start(bf16[112,576]{1,0:T(8,128)(2,1)} %concatenate.80), channel_id=1, source_target_pairs={{0,16},{4,20},{8,24},{12,28},{16,0},{20,4},{24,8},{28,12},{1,17},{... | collective-permute-start | bytes 387080 | tf_op jit(solution)/shard_map/ppermute | solution.py:479
  21.2 24.1 %collective-permute-start.5 = (bf16[112,576]{1,0:T(8,128)(2,1)}, bf16[112,576]{1,0:T(8,128)(2,1)}, u32[]{:S(2)}, u32[]{:S(2)}) collective-permute-start(bf16[112,576]{1,0:T(8,128)(2,1)} %concatenate.80), channel_id=1, source_target_pairs={{0,24},{4,28},{8,0},{12,4},{16,8},{20,12},{24,16},{28,20},{1,25},{... | collective-permute-start | bytes 387080 | tf_op jit(solution)/shard_map/ppermute | solution.py:479
  22.5 53.3 %collective-permute-start = (bf16[3,264,768]{2,1,0:T(8,128)(2,1)}, bf16[3,264,768]{2,1,0:T(8,128)(2,1)S(1)}, u32[]{:S(2)}, u32[]{:S(2)}) collective-permute-start(bf16[3,264,768]{2,1,0:T(8,128)(2,1)} %refs_5_.3), channel_id=1, source_target_pairs={{0,1},{1,0},{2,3},{3,2},{4,5},{5,4},{6,7},{7,6},{8,9},{9,8},{10,11... | collective-permute-start | bytes 3649544 | tf_op jit(solution)/shard_map/ppermute | solution.py:471
  24.3 25.3 %collective-permute-start.1 = (bf16[264,768]{1,0:T(8,128)(2,1)}, bf16[264,768]{1,0:T(8,128)(2,1)}, u32[]{:S(2)}, u32[]{:S(2)}) collective-permute-start(bf16[264,768]{1,0:T(8,128)(2,1)} %slice_bitcast_fusion.6), channel_id=1, source_target_pairs={{0,2},{1,3},{2,0},{3,1},{4,6},{5,7},{6,4},{7,5},{8,10},{9,11},{10,... | collective-permute-start | bytes 1216520 | tf_op jit(solution)/shard_map/ppermute | solution.py:471
  41.6 34.3 %collective-permute-start.7 = (bf16[2,264,768]{2,1,0:T(8,128)(2,1)}, bf16[2,264,768]{2,1,0:T(8,128)(2,1)}, u32[]{:S(2)}, u32[]{:S(2)}) collective-permute-start(bf16[2,264,768]{2,1,0:T(8,128)(2,1)} %slice.189), channel_id=1, source_target_pairs={{0,2},{1,3},{2,0},{3,1},{4,6},{5,7},{6,4},{7,5},{8,10},{9,11},{10,... | collective-permute-start | bytes 2433032 | tf_op jit(solution)/shard_map/ppermute | solution.py:471
  46.9 18.2 %collective-permute-start.6 = (bf16[4,112,576]{2,1,0:T(8,128)(2,1)}, bf16[4,112,576]{2,1,0:T(8,128)(2,1)S(1)}, u32[]{:S(2)}, u32[]{:S(2)}) collective-permute-start(bf16[4,112,576]{2,1,0:T(8,128)(2,1)} %bitcast_dynamic-update-slice_fusion.4), channel_id=1, source_target_pairs={{0,4},{4,0},{8,12},{12,8},{16,20},{20,16},{24,28},{28,24},{1,5},{5... | collective-permute-start | bytes 1548296 | tf_op jit(solution)/shard_map/ppermute | solution.py:471
  49.6 363.1 %reduce-scatter.2.cloned.1.call-start = ((), (), s32[]{:S(2)}) async-start(), calls=%async_computation.1 | async-start | bytes 5971968 | tf_op jit(solution)/shard_map/reduce_scatter | solution.py:543
  49.7 22.7 %collective-permute-start.2 = (bf16[264,768]{1,0:T(8,128)(2,1)}, bf16[264,768]{1,0:T(8,128)(2,1)}, u32[]{:S(2)}, u32[]{:S(2)}) collective-permute-start(bf16[264,768]{1,0:T(8,128)(2,1)} %collective-permute-done.1.refs_2_.refs_7_), channel_id=1, source_target_pairs={{0,1},{1,0},{2,3},{3,2},{4,5},{5,4},{6,7},{7,6},{8,9},{9,8},{10,11... | collective-permute-start | bytes 1216520 | tf_op jit(solution)/shard_map/ppermute | solution.py:471
  67.7 46.7 %collective-permute-start.18 = (bf16[96,1920]{1,0:T(8,128)(2,1)}, bf16[96,1920]{1,0:T(8,128)(2,1)}, u32[]{:S(2)}, u32[]{:S(2)}) collective-permute-start(bf16[96,1920]{1,0:T(8,128)(2,1)} %once_there.9), channel_id=1, source_target_pairs={{0,8},{4,12},{8,16},{12,20},{16,24},{20,28},{24,0},{28,4},{1,9},{5... | collective-permute-start | bytes 1105928 | tf_op jit(solution)/shard_map/ppermute | solution.py:479
  68.4 46.4 %collective-permute-start.19 = (bf16[96,1920]{1,0:T(8,128)(2,1)}, bf16[96,1920]{1,0:T(8,128)(2,1)}, u32[]{:S(2)}, u32[]{:S(2)}) collective-permute-start(bf16[96,1920]{1,0:T(8,128)(2,1)} %once_there.9), channel_id=1, source_target_pairs={{0,16},{4,20},{8,24},{12,28},{16,0},{20,4},{24,8},{28,12},{1,17},{... | collective-permute-start | bytes 1105928 | tf_op jit(solution)/shard_map/ppermute | solution.py:479
  72.4 42.4 %collective-permute-start.20 = (bf16[96,1920]{1,0:T(8,128)(2,1)S(1)}, bf16[96,1920]{1,0:T(8,128)(2,1)}, u32[]{:S(2)}, u32[]{:S(2)}) collective-permute-start(bf16[96,1920]{1,0:T(8,128)(2,1)S(1)} %copy-done.13), channel_id=1, source_target_pairs={{0,24},{4,28},{8,0},{12,4},{16,8},{20,12},{24,16},{28,20},{1,25},{... | collective-permute-start | bytes 1105928 | tf_op jit(solution)/shard_map/ppermute | solution.py:479
  75.8 14.3 %collective-permute-start.8 = (bf16[2,264,768]{2,1,0:T(8,128)(2,1)}, bf16[2,264,768]{2,1,0:T(8,128)(2,1)}, u32[]{:S(2)}, u32[]{:S(2)}) collective-permute-start(bf16[2,264,768]{2,1,0:T(8,128)(2,1)} %collective-permute-done.7.refs_2_.refs_6_.refs_7_), channel_id=1, source_target_pairs={{0,1},{1,0},{2,3},{3,2},{4,5},{5,4},{6,7},{7,6},{8,9},{9,8},{10,11... | collective-permute-start | bytes 2433032 | tf_op jit(solution)/shard_map/ppermute | solution.py:471
  88.6 31.0 %collective-permute-start.10 = (bf16[264,192]{1,0:T(8,128)(2,1)}, bf16[264,192]{1,0:T(8,128)(2,1)S(1)}, u32[]{:S(2)}, u32[]{:S(2)}) collective-permute-start(bf16[264,192]{1,0:T(8,128)(2,1)} %get-tuple-element.70), channel_id=1, source_target_pairs={{0,2},{1,3},{2,0},{3,1},{4,6},{5,7},{6,4},{7,5},{8,10},{9,11},{10,... | collective-permute-start | bytes 304136 | tf_op jit(solution)/shard_map/ppermute | solution.py:471
  90.2 29.4 %collective-permute-start.11 = (bf16[264,192]{1,0:T(8,128)(2,1)}, bf16[264,192]{1,0:T(8,128)(2,1)}, u32[]{:S(2)}, u32[]{:S(2)}) collective-permute-start(bf16[264,192]{1,0:T(8,128)(2,1)} %get-tuple-element.71), channel_id=1, source_target_pairs={{0,3},{1,2},{2,1},{3,0},{4,7},{5,6},{6,5},{7,4},{8,11},{9,10},{10,... | collective-permute-start | bytes 304136 | tf_op jit(solution)/shard_map/ppermute | solution.py:471
  118.0 34.5 %collective-permute-start.21 = (bf16[4,96,1920]{2,1,0:T(8,128)(2,1)S(1)}, bf16[4,96,1920]{2,1,0:T(8,128)(2,1)S(1)}, u32[]{:S(2)}, u32[]{:S(2)}) collective-permute-start(bf16[4,96,1920]{2,1,0:T(8,128)(2,1)S(1)} %bitcast_dynamic-update-slice_fusion), channel_id=1, source_target_pairs={{0,4},{4,0},{8,12},{12,8},{16,20},{20,16},{24,28},{28,24},{1,5},{5... | collective-permute-start | bytes 4423688 | tf_op jit(solution)/shard_map/ppermute | solution.py:471
  275.5 43.6 %collective-permute-start.31 = (bf16[2,264,768]{2,1,0:T(8,128)(2,1)}, bf16[2,264,768]{2,1,0:T(8,128)(2,1)S(1)}, u32[]{:S(2)}, u32[]{:S(2)}) collective-permute-start(bf16[2,264,768]{2,1,0:T(8,128)(2,1)} %get-tuple-element.93), channel_id=1, source_target_pairs={{0,1},{1,0},{2,3},{3,2},{4,5},{5,4},{6,7},{7,6},{8,9},{9,8},{10,11... | collective-permute-start | bytes 2433032 | tf_op jit(solution)/shard_map/ppermute | solution.py:471
  318.3 36.7 %collective-permute-start.36 = (bf16[2,264,768]{2,1,0:T(8,128)(2,1)}, bf16[2,264,768]{2,1,0:T(8,128)(2,1)S(1)}, u32[]{:S(2)}, u32[]{:S(2)}) collective-permute-start(bf16[2,264,768]{2,1,0:T(8,128)(2,1)} %get-tuple-element.103), channel_id=1, source_target_pairs={{0,1},{1,0},{2,3},{3,2},{4,5},{5,4},{6,7},{7,6},{8,9},{9,8},{10,11... | collective-permute-start | bytes 2433032 | tf_op jit(solution)/shard_map/ppermute | solution.py:471
  357.1 14.7 %collective-permute-start.40 = (bf16[4,112,576]{2,1,0:T(8,128)(2,1)S(1)}, bf16[4,112,576]{2,1,0:T(8,128)(2,1)S(1)}, u32[]{:S(2)}, u32[]{:S(2)}) collective-permute-start(bf16[4,112,576]{2,1,0:T(8,128)(2,1)S(1)} %dynamic-slice_bitcast_fusion), channel_id=1, source_target_pairs={{0,4},{4,0},{8,12},{12,8},{16,20},{20,16},{24,28},{28,24},{1,5},{5... | collective-permute-start | bytes 1548296 | tf_op jit(solution)/shard_map/ppermute | solution.py:471
  358.7 14.2 %collective-permute-start.38 = (bf16[2,264,768]{2,1,0:T(8,128)(2,1)}, bf16[2,264,768]{2,1,0:T(8,128)(2,1)S(1)}, u32[]{:S(2)}, u32[]{:S(2)}) collective-permute-start(bf16[2,264,768]{2,1,0:T(8,128)(2,1)} %get-tuple-element.109), channel_id=1, source_target_pairs={{0,1},{1,0},{2,3},{3,2},{4,5},{5,4},{6,7},{7,6},{8,9},{9,8},{10,11... | collective-permute-start | bytes 2433032 | tf_op jit(solution)/shard_map/ppermute | solution.py:471
  360.9 23.4 %collective-permute-start.37 = (bf16[264,768]{1,0:T(8,128)(2,1)}, bf16[264,768]{1,0:T(8,128)(2,1)S(1)}, u32[]{:S(2)}, u32[]{:S(2)}) collective-permute-start(bf16[264,768]{1,0:T(8,128)(2,1)} %fusion.13), channel_id=1, source_target_pairs={{0,2},{1,3},{2,0},{3,1},{4,6},{5,7},{6,4},{7,5},{8,10},{9,11},{10,... | collective-permute-start | bytes 1216520 | tf_op jit(solution)/shard_map/ppermute | solution.py:471
  394.3 15.3 %collective-permute-start.39 = (bf16[264,768]{1,0:T(8,128)(2,1)}, bf16[264,768]{1,0:T(8,128)(2,1)}, u32[]{:S(2)}, u32[]{:S(2)}) collective-permute-start(bf16[264,768]{1,0:T(8,128)(2,1)} %fusion.11), channel_id=1, source_target_pairs={{0,2},{1,3},{2,0},{3,1},{4,6},{5,7},{6,4},{7,5},{8,10},{9,11},{10,... | collective-permute-start | bytes 1216520 | tf_op jit(solution)/shard_map/ppermute | solution.py:471
  412.7 16.8 %collective-permute-start.47 = (bf16[96,3456]{1,0:T(8,128)(2,1)}, bf16[96,3456]{1,0:T(8,128)(2,1)}, u32[]{:S(2)}, u32[]{:S(2)}) collective-permute-start(bf16[96,3456]{1,0:T(8,128)(2,1)} %bitcast.142), channel_id=1, source_target_pairs={{0,2},{1,3},{2,0},{3,1},{4,6},{5,7},{6,4},{7,5},{8,10},{9,11},{10,... | collective-permute-start | bytes 1990664 | tf_op jit(solution)/shard_map/ppermute | solution.py:471
  (85 other events, 836.4 us)
Sparse Core Ops, SparseCore 0:
  49.7 64.3 all-gather.2
  238.5 108.7 reduce-scatter.1

commit v6 on v5

--- a/solution.py
+++ b/solution.py
@@ -258,7 +258,7 @@
             pltpu.VMEM((total, model), F32),
         ],
         compiler_params=pltpu.CompilerParams(vmem_limit_bytes=VMEM_BYTES),
-        cost_estimate=cost(1),
+        cost_estimate=cost(0),
         name="slot_backward",
     )(
         *[g[0] for g in grads], *after, *[t[0] for t in tokens], qkv, normed, weight, before,
@@ -708,8 +708,11 @@
     for slot in range(1, slot_count):
         slot_grads.append([(part, slot - 1) for part in grad_rest])
 
-    down_sum = grad_down_own.astype(F32) + xor_send(grad_down_other, "seq", 1).astype(F32)
-    up_sum = grad_up_own.astype(F32) + xor_send(grad_up_other, "seq", 1).astype(F32)
+    sent = tuple(grad_first[1:])
+    down_sum = once_there(xor_send(grad_down_other, "seq", 1), sent).astype(F32)
+    down_sum = grad_down_own.astype(F32) + down_sum
+    up_sum = once_there(xor_send(grad_up_other, "seq", 1), sent).astype(F32)
+    up_sum = grad_up_own.astype(F32) + up_sum
     grad_out_weight = jnp.concatenate(
         [lax.dynamic_index_in_dim(grad_out_groups, me ^ r, 0, keepdims=False) for r in range(n_seq)],
         axis=0,
@@ -730,7 +733,7 @@
     for slot in range(slot_count):
         after = (second_grads,) if slot == 0 else ()
         if slot > 1:
-            after = (arrivals[-2][0],)
+            after = (arrivals[-2][1],)
         own, across, pairs, grad_columns, slot_norm, slot_bias = slot_backward(
             slot_grads[slot],
             slot_tokens[slot],
@@ -772,7 +775,7 @@
     columns = jnp.concatenate([grad_columns.reshape(n_img, shard, group), extra], axis=1)
     columns = once_there(columns.astype(BF16), (arrivals[-2][0],))
     if few_devices():
-        own_columns = reduce_outer(once_there(reduce_inner(columns), (pairs,)))
+        own_columns = reduce_outer(once_there(reduce_inner(columns), (own_second, pairs)))
     else:
         own_columns = scatter_img(columns)
     own_columns = own_columns.astype(BF16)

time: 455 us -> 447 us (0.982)
  waiting for transfers between devices: 93.9 us -> 82.7 us
    ppermute x40, waiting for transfers between devices: 89 us -> 77.3 us  [xor_send(): return lax.ppermute(block, axis, [(i, i ^ bits) for i in range(n)])]
    unnamed x116 -> x106, local copies, waits for them, and re-layouts: 10.4 us -> 8.41 us
  transfers between devices with their start and end apart: 51 -> 51, of which waited for: 20 -> 19; matrix products, arithmetic and copies ran while one was open for 18% -> 19% of each run, Pallas kernels for 28% -> 28%
where the time goes in v6:
time: 447 us; the launch traced here: 440 us
  Pallas kernels  176 us (39%)
  waiting for transfers between devices  82.7 us (19%)
  local copies, waits for them, and re-layouts  71.1 us (16%)
  starting transfers between devices  49.3 us (11%)
  other arithmetic  44.7 us (10%)
  between operations  15.9 us (4%)
    pallas_call x3, Pallas kernels, slot_backward(): pl.pallas_call(partial(backward_kernel, n_seq, heads, len(after)), grid=(...  77.4 us
    ppermute x40, waiting for transfers between devices, xor_send(): return lax.ppermute(block, axis, [(i, i ^ bits) for i in range(n)])  77.3 us
    pallas_call x1, Pallas kernels, feed_forward(): pl.pallas_call(partial(mlp_kernel, slots, groups), grid=(ff // chunk,), i...  51.3 us
    pallas_call x3, Pallas kernels, slot_forward(): pl.pallas_call(partial(forward_kernel, n_seq, heads, len(after)), grid=(1...  47.4 us
    ppermute x40, starting transfers between devices, xor_send(): return lax.ppermute(block, axis, [(i, i ^ bits) for i in range(n)])  28.5 us
    ppermute x9, starting transfers between devices, outer_send(): lax.ppermute(block, 'img', [(z * INNER + y, (z + shift) % outer * INNER +...  20.7 us
    dynamic_update_slice x8, local copies, waits for them, and re-layouts, place_outer(): lax.dynamic_update_slice_in_dim(placed, part[None], (z + outer - k) % out...  10.4 us
  transfers between devices with their start and end apart: 51, of which 19 were waited for; matrix products, arithmetic and copies ran while one was open for 19% of the time, Pallas kernels for 28%

profile of v6, /device:TPU:0, one launch (start us, length us, event | category | flops | bytes accessed | tf_op | source)
XLA Modules:
  0.0 439.8 jit_solution(9561739056370305373)
XLA Ops:
  25.8 3.5 reshape.292
  29.3 3.7 dynamic-slice_reduce_fusion
  49.7 15.3 %collective-permute-done.6 = bf16[4,112,576]{2,1,0:T(8,128)(2,1)S(1)} collective-permute-done((bf16[4,112,576]{2,1,0:T(8,128)(2,1)}, bf16[4,112,576]{2,1,0:T(8,128)(2,1)S(1)}, u32[]{:S(2)}, u32[]{:S(2)}) %collective-permute-start.6) | collective-permute-done | bytes 516128 | tf_op jit(solution)/shard_map/ppermute | solution.py:471
  76.9 11.7 %slot_forward.3 = (bf16[1056,768]{1,0:T(8,128)(2,1)}, bf16[9,1152,128]{2,1,0:T(8,128)(2,1)}, bf16[264,192]{1,0:T(8,128)(2,1)}, bf16[264,192]{1,0:T(8,128)(2,1)},...) custom-call(bf16[3,264,768]{2,1,0:T(8,128)(2,1)} %refs_5_.3, bf16[3,264,768]{2,1,0:T(8,128)(2,1)} %copy-done.6, ...), custom_call_target="tpu_custom_call" | custom-call | flops 14000000000 | bytes 10000000 | tf_op jit(solution)/shard_map/slot_forward/pallas_call | solution.py:146
  90.5 24.0 %slot_forward.4 = (bf16[1056,768]{1,0:T(8,128)(2,1)}, bf16[9,1152,128]{2,1,0:T(8,128)(2,1)}, bf16[264,192]{1,0:T(8,128)(2,1)}, bf16[264,192]{1,0:T(8,128)(2,1)},...) custom-call(bf16[3,264,768]{2,1,0:T(8,128)(2,1)} %refs_5_.3, bf16[3,264,768]{2,1,0:T(8,128)(2,1)} %copy-done.6, ...), custom_call_target="tpu_custom_call" | custom-call | flops 14000000000 | bytes 10000000 | tf_op jit(solution)/shard_map/slot_forward/pallas_call | solution.py:146
  120.3 11.7 %slot_forward.5 = (bf16[1056,768]{1,0:T(8,128)(2,1)}, bf16[9,1152,128]{2,1,0:T(8,128)(2,1)}, bf16[264,192]{1,0:T(8,128)(2,1)}, bf16[264,192]{1,0:T(8,128)(2,1)},...) custom-call(bf16[3,264,768]{2,1,0:T(8,128)(2,1)} %refs_5_.3, bf16[3,264,768]{2,1,0:T(8,128)(2,1)} %copy-done.6, ...), custom_call_target="tpu_custom_call" | custom-call | flops 14000000000 | bytes 10000000 | tf_op jit(solution)/shard_map/slot_forward/pallas_call | solution.py:146
  140.7 3.8 collective-permute-done.14.refs_5_.refs_7_
  147.1 5.4 %collective-permute-done.21.refs_0_ = bf16[4,96,1920]{2,1,0:T(8,128)(2,1)S(1)} collective-permute-done((bf16[4,96,1920]{2,1,0:T(8,128)(2,1)S(1)}, bf16[4,96,1920]{2,1,0:T(8,128)(2,1)S(1)}, u32[]{:S(2)}, u32[]{:S(2)}) %collective-permute-start.21) | collective-permute-done | bytes 1474592 | tf_op jit(solution)/shard_map/ppermute | solution.py:471
  166.5 51.3 %feed_forward.1 = (bf16[3,264,768]{2,1,0:T(8,128)(2,1)}, f32[3,264,768]{2,1,0:T(8,128)}, bf16[264,192]{1,0:T(8,128)(2,1)}, bf16[264,192]{1,0:T(8,128)(2,1)}, bf1...) custom-call(bf16[264,192]{1,0:T(8,128)(2,1)} %get-tuple-element.67.r, ...), custom_call_target="tpu_custom_call" | custom-call | flops 54999998464 | bytes 10000000 | tf_op jit(solution)/shard_map/feed_forward/pallas_call | solution.py:407
  222.2 3.9 collective-permute-done.29
  227.4 4.2 collective-permute-done.27.refs_3_
  232.3 4.4 add_convert_fusion
  236.6 4.8 %concatenate.91 = bf16[8,96,1536]{2,1,0:T(8,128)(2,1)} reshape(bf16[1536,768]{1,0:T(8,128)(2,1)} %add_convert_fusion) | data formatting | bytes 4718592 | tf_op jit(solution)/shard_map/concatenate | solution.py:723
  250.4 25.7 %slot_backward.3 = (f32[264,768]{1,0:T(8,128)}, f32[264,768]{1,0:T(8,128)}, bf16[2,264,768]{2,1,0:T(8,128)(2,1)}, f32[768,576]{1,0:T(8,128)}, f32[8,768]{1,0:T(8,128)}, /*index=5*/f32[8,576]{1,0:T(8,128)}) custom-call(bf16[264,192]{1,0:T(8,128)(2,1)} %get-tuple-element.81.refs_0_, bf16[264,192]{1,0:T(8,128)(2,1)} %copy-done.19, bf16[264,192]{1,0:T(8,128)(2,1)} %copy-done.20, ...), custom_call_target="tpu_custom_call" | custom-call | bytes 10000000 | tf_op jit(solution)/shard_map/slot_backward/pallas_call | solution.py:244
  279.0 7.3 %collective-permute-done.34.refs_2_ = bf16[2,264,192]{2,1,0:T(8,128)(2,1)S(1)} collective-permute-done((bf16[2,264,192]{2,1,0:T(8,128)(2,1)S(1)}, bf16[2,264,192]{2,1,0:T(8,128)(2,1)S(1)}, u32[]{:S(2)}, u32[]{:S(2)}) %collective-permute-start.34) | collective-permute-done | bytes 202784 | tf_op jit(solution)/shard_map/ppermute | solution.py:471
  286.3 4.2 collective-permute-done.35.refs_3_
  291.2 26.1 %slot_backward.4 = (f32[264,768]{1,0:T(8,128)}, f32[264,768]{1,0:T(8,128)}, bf16[2,264,768]{2,1,0:T(8,128)(2,1)}, f32[768,576]{1,0:T(8,128)}, f32[8,768]{1,0:T(8,128)}, /*index=5*/f32[8,576]{1,0:T(8,128)}) custom-call(bf16[2,264,192]{2,1,0:T(8,128)(2,1)} %get-tuple-element.95.refs_0_, bf16[2,264,192]{2,1,0:T(8,128)(2,1)} %copy-done.22, ...), custom_call_target="tpu_custom_call" | custom-call | bytes 10000000 | tf_op jit(solution)/shard_map/slot_backward/pallas_call | solution.py:244
  323.5 8.7 %collective-permute-done.32.refs_4_ = bf16[264,768]{1,0:T(8,128)(2,1)S(1)} collective-permute-done((bf16[264,768]{1,0:T(8,128)(2,1)S(1)}, bf16[264,768]{1,0:T(8,128)(2,1)S(1)}, u32[]{:S(2)}, u32[]{:S(2)}) %collective-permute-start.32) | collective-permute-done | bytes 405536 | tf_op jit(solution)/shard_map/ppermute | solution.py:471
  333.0 25.7 %slot_backward.5 = (f32[264,768]{1,0:T(8,128)}, f32[264,768]{1,0:T(8,128)}, bf16[2,264,768]{2,1,0:T(8,128)(2,1)}, f32[768,576]{1,0:T(8,128)}, f32[8,768]{1,0:T(8,128)}, /*index=5*/f32[8,576]{1,0:T(8,128)}) custom-call(bf16[2,264,192]{2,1,0:T(8,128)(2,1)} %get-tuple-element.95.refs_0_, bf16[2,264,192]{2,1,0:T(8,128)(2,1)} %copy-done.22, ...), custom_call_target="tpu_custom_call" | custom-call | bytes 10000000 | tf_op jit(solution)/shard_map/slot_backward/pallas_call | solution.py:244
  369.9 10.7 %collective-permute-done.40 = bf16[4,112,576]{2,1,0:T(8,128)(2,1)S(1)} collective-permute-done((bf16[4,112,576]{2,1,0:T(8,128)(2,1)S(1)}, bf16[4,112,576]{2,1,0:T(8,128)(2,1)S(1)}, u32[]{:S(2)}, u32[]{:S(2)}) %collective-permute-start.40) | collective-permute-done | bytes 516128 | tf_op jit(solution)/shard_map/ppermute | solution.py:471
  389.7 7.2 %collective-permute-start.41 = (bf16[112,576]{1,0:T(8,128)(2,1)S(1)}, bf16[112,576]{1,0:T(8,128)(2,1)S(1)}, u32[]{:S(2)}, u32[]{:S(2)}) collective-permute-start(bf16[112,576]{1,0:T(8,128)(2,1)S(1)} %get-tuple-element.148), channel_id=1, source_target_pairs={{0,8},{4,12},{8,16},{12,20},{16,24},{20,28},{24,0},{28,4},{1,9},{5... | collective-permute-start | bytes 387080 | tf_op jit(solution)/shard_map/ppermute | solution.py:479
  401.0 4.8 %collective-permute-done.42 = bf16[112,576]{1,0:T(8,128)(2,1)S(1)} collective-permute-done((bf16[112,576]{1,0:T(8,128)(2,1)S(1)}, bf16[112,576]{1,0:T(8,128)(2,1)S(1)}, u32[]{:S(2)}, u32[]{:S(2)}) %collective-permute-start.42) | collective-permute-done | bytes 129056 | tf_op jit(solution)/shard_map/ppermute | solution.py:479
  408.9 4.7 %fusion.7 = f32[3,264,768]{2,1,0:T(8,128)} fusion(f32[3,264,768]{2,1,0:T(8,128)} %get-tuple-element.80, bf16[3,264,768]{2,1,0:T(8,128)(2,1)S(1)} %copy-done.5, f32[3,264,768]{2,1,0:T(8,128)} %bitcast.125, f32[3,264]{1,0:T(4,128)S(1)} %broadcast_multiply_fusion, f32[3,264]{1,0:T(4,128)S(1)} %div.30, f32[768]{0:T(1024)S(1)} %mul.76, ...), kind=kLoop, calls=%fused_computation.14 | loop fusion | flops 5474304 | bytes 8531328 | tf_op jit(solution)/shard_map/add | solution.py:789
  413.6 6.3 %collective-permute-done.45 = bf16[112,576]{1,0:T(8,128)(2,1)S(1)} collective-permute-done((bf16[112,576]{1,0:T(8,128)(2,1)S(1)}, bf16[112,576]{1,0:T(8,128)(2,1)S(1)}, u32[]{:S(2)}, u32[]{:S(2)}) %collective-permute-start.45) | collective-permute-done | bytes 129056 | tf_op jit(solution)/shard_map/ppermute | solution.py:471
  (361 shorter events, 145.1 us)
Async XLA Ops:
  7.2 150.2 %all-gather.3.cloned.1.call-start = ((), (), s32[]{:S(2)}) async-start(), calls=%async_computation.2 | async-start | bytes 2654208 | tf_op jit(solution)/shard_map/all_gather | solution.py:626
  15.6 26.0 %collective-permute-start.3 = (bf16[112,576]{1,0:T(8,128)(2,1)}, bf16[112,576]{1,0:T(8,128)(2,1)}, u32[]{:S(2)}, u32[]{:S(2)}) collective-permute-start(bf16[112,576]{1,0:T(8,128)(2,1)} %concatenate.80), channel_id=1, source_target_pairs={{0,8},{4,12},{8,16},{12,20},{16,24},{20,28},{24,0},{28,4},{1,9},{5... | collective-permute-start | bytes 387080 | tf_op jit(solution)/shard_map/ppermute | solution.py:479
  18.6 25.1 %collective-permute-start.4 = (bf16[112,576]{1,0:T(8,128)(2,1)}, bf16[112,576]{1,0:T(8,128)(2,1)}, u32[]{:S(2)}, u32[]{:S(2)}) collective-permute-start(bf16[112,576]{1,0:T(8,128)(2,1)} %concatenate.80), channel_id=1, source_target_pairs={{0,16},{4,20},{8,24},{12,28},{16,0},{20,4},{24,8},{28,12},{1,17},{... | collective-permute-start | bytes 387080 | tf_op jit(solution)/shard_map/ppermute | solution.py:479
  21.2 24.1 %collective-permute-start.5 = (bf16[112,576]{1,0:T(8,128)(2,1)}, bf16[112,576]{1,0:T(8,128)(2,1)}, u32[]{:S(2)}, u32[]{:S(2)}) collective-permute-start(bf16[112,576]{1,0:T(8,128)(2,1)} %concatenate.80), channel_id=1, source_target_pairs={{0,24},{4,28},{8,0},{12,4},{16,8},{20,12},{24,16},{28,20},{1,25},{... | collective-permute-start | bytes 387080 | tf_op jit(solution)/shard_map/ppermute | solution.py:479
  22.5 53.3 %collective-permute-start = (bf16[3,264,768]{2,1,0:T(8,128)(2,1)}, bf16[3,264,768]{2,1,0:T(8,128)(2,1)S(1)}, u32[]{:S(2)}, u32[]{:S(2)}) collective-permute-start(bf16[3,264,768]{2,1,0:T(8,128)(2,1)} %refs_5_.3), channel_id=1, source_target_pairs={{0,1},{1,0},{2,3},{3,2},{4,5},{5,4},{6,7},{7,6},{8,9},{9,8},{10,11... | collective-permute-start | bytes 3649544 | tf_op jit(solution)/shard_map/ppermute | solution.py:471
  24.3 25.3 %collective-permute-start.1 = (bf16[264,768]{1,0:T(8,128)(2,1)}, bf16[264,768]{1,0:T(8,128)(2,1)}, u32[]{:S(2)}, u32[]{:S(2)}) collective-permute-start(bf16[264,768]{1,0:T(8,128)(2,1)} %slice_bitcast_fusion.6), channel_id=1, source_target_pairs={{0,2},{1,3},{2,0},{3,1},{4,6},{5,7},{6,4},{7,5},{8,10},{9,11},{10,... | collective-permute-start | bytes 1216520 | tf_op jit(solution)/shard_map/ppermute | solution.py:471
  41.6 34.3 %collective-permute-start.7 = (bf16[2,264,768]{2,1,0:T(8,128)(2,1)}, bf16[2,264,768]{2,1,0:T(8,128)(2,1)}, u32[]{:S(2)}, u32[]{:S(2)}) collective-permute-start(bf16[2,264,768]{2,1,0:T(8,128)(2,1)} %slice.189), channel_id=1, source_target_pairs={{0,2},{1,3},{2,0},{3,1},{4,6},{5,7},{6,4},{7,5},{8,10},{9,11},{10,... | collective-permute-start | bytes 2433032 | tf_op jit(solution)/shard_map/ppermute | solution.py:471
  46.9 18.2 %collective-permute-start.6 = (bf16[4,112,576]{2,1,0:T(8,128)(2,1)}, bf16[4,112,576]{2,1,0:T(8,128)(2,1)S(1)}, u32[]{:S(2)}, u32[]{:S(2)}) collective-permute-start(bf16[4,112,576]{2,1,0:T(8,128)(2,1)} %bitcast_dynamic-update-slice_fusion.4), channel_id=1, source_target_pairs={{0,4},{4,0},{8,12},{12,8},{16,20},{20,16},{24,28},{28,24},{1,5},{5... | collective-permute-start | bytes 1548296 | tf_op jit(solution)/shard_map/ppermute | solution.py:471
  49.6 336.5 %reduce-scatter.2.cloned.1.call-start = ((), (), s32[]{:S(2)}) async-start(), calls=%async_computation.1 | async-start | bytes 5971968 | tf_op jit(solution)/shard_map/reduce_scatter | solution.py:543
  49.7 22.7 %collective-permute-start.2 = (bf16[264,768]{1,0:T(8,128)(2,1)}, bf16[264,768]{1,0:T(8,128)(2,1)}, u32[]{:S(2)}, u32[]{:S(2)}) collective-permute-start(bf16[264,768]{1,0:T(8,128)(2,1)} %collective-permute-done.1.refs_2_.refs_7_), channel_id=1, source_target_pairs={{0,1},{1,0},{2,3},{3,2},{4,5},{5,4},{6,7},{7,6},{8,9},{9,8},{10,11... | collective-permute-start | bytes 1216520 | tf_op jit(solution)/shard_map/ppermute | solution.py:471
  67.7 46.7 %collective-permute-start.18 = (bf16[96,1920]{1,0:T(8,128)(2,1)}, bf16[96,1920]{1,0:T(8,128)(2,1)}, u32[]{:S(2)}, u32[]{:S(2)}) collective-permute-start(bf16[96,1920]{1,0:T(8,128)(2,1)} %once_there.11), channel_id=1, source_target_pairs={{0,8},{4,12},{8,16},{12,20},{16,24},{20,28},{24,0},{28,4},{1,9},{5... | collective-permute-start | bytes 1105928 | tf_op jit(solution)/shard_map/ppermute | solution.py:479
  68.4 46.4 %collective-permute-start.19 = (bf16[96,1920]{1,0:T(8,128)(2,1)}, bf16[96,1920]{1,0:T(8,128)(2,1)}, u32[]{:S(2)}, u32[]{:S(2)}) collective-permute-start(bf16[96,1920]{1,0:T(8,128)(2,1)} %once_there.11), channel_id=1, source_target_pairs={{0,16},{4,20},{8,24},{12,28},{16,0},{20,4},{24,8},{28,12},{1,17},{... | collective-permute-start | bytes 1105928 | tf_op jit(solution)/shard_map/ppermute | solution.py:479
  72.4 42.4 %collective-permute-start.20 = (bf16[96,1920]{1,0:T(8,128)(2,1)S(1)}, bf16[96,1920]{1,0:T(8,128)(2,1)}, u32[]{:S(2)}, u32[]{:S(2)}) collective-permute-start(bf16[96,1920]{1,0:T(8,128)(2,1)S(1)} %copy-done.12), channel_id=1, source_target_pairs={{0,24},{4,28},{8,0},{12,4},{16,8},{20,12},{24,16},{28,20},{1,25},{... | collective-permute-start | bytes 1105928 | tf_op jit(solution)/shard_map/ppermute | solution.py:479
  75.8 14.3 %collective-permute-start.8 = (bf16[2,264,768]{2,1,0:T(8,128)(2,1)}, bf16[2,264,768]{2,1,0:T(8,128)(2,1)}, u32[]{:S(2)}, u32[]{:S(2)}) collective-permute-start(bf16[2,264,768]{2,1,0:T(8,128)(2,1)} %collective-permute-done.7.refs_2_.refs_6_.refs_7_), channel_id=1, source_target_pairs={{0,1},{1,0},{2,3},{3,2},{4,5},{5,4},{6,7},{7,6},{8,9},{9,8},{10,11... | collective-permute-start | bytes 2433032 | tf_op jit(solution)/shard_map/ppermute | solution.py:471
  88.6 31.0 %collective-permute-start.10 = (bf16[264,192]{1,0:T(8,128)(2,1)}, bf16[264,192]{1,0:T(8,128)(2,1)S(1)}, u32[]{:S(2)}, u32[]{:S(2)}) collective-permute-start(bf16[264,192]{1,0:T(8,128)(2,1)} %get-tuple-element.70), channel_id=1, source_target_pairs={{0,2},{1,3},{2,0},{3,1},{4,6},{5,7},{6,4},{7,5},{8,10},{9,11},{10,... | collective-permute-start | bytes 304136 | tf_op jit(solution)/shard_map/ppermute | solution.py:471
  90.2 29.4 %collective-permute-start.11 = (bf16[264,192]{1,0:T(8,128)(2,1)}, bf16[264,192]{1,0:T(8,128)(2,1)}, u32[]{:S(2)}, u32[]{:S(2)}) collective-permute-start(bf16[264,192]{1,0:T(8,128)(2,1)} %get-tuple-element.71), channel_id=1, source_target_pairs={{0,3},{1,2},{2,1},{3,0},{4,7},{5,6},{6,5},{7,4},{8,11},{9,10},{10,... | collective-permute-start | bytes 304136 | tf_op jit(solution)/shard_map/ppermute | solution.py:471
  118.0 34.5 %collective-permute-start.21 = (bf16[4,96,1920]{2,1,0:T(8,128)(2,1)S(1)}, bf16[4,96,1920]{2,1,0:T(8,128)(2,1)S(1)}, u32[]{:S(2)}, u32[]{:S(2)}) collective-permute-start(bf16[4,96,1920]{2,1,0:T(8,128)(2,1)S(1)} %bitcast_dynamic-update-slice_fusion), channel_id=1, source_target_pairs={{0,4},{4,0},{8,12},{12,8},{16,20},{20,16},{24,28},{28,24},{1,5},{5... | collective-permute-start | bytes 4423688 | tf_op jit(solution)/shard_map/ppermute | solution.py:471
  217.7 13.9 %collective-permute-start.30 = (bf16[1536,768]{1,0:T(8,128)(2,1)}, bf16[1536,768]{1,0:T(8,128)(2,1)}, u32[]{:S(2)}, u32[]{:S(2)}) collective-permute-start(bf16[1536,768]{1,0:T(8,128)(2,1)} %get-tuple-element.89), channel_id=1, source_target_pairs={{0,1},{1,0},{2,3},{3,2},{4,5},{5,4},{6,7},{7,6},{8,9},{9,8},{10,11... | collective-permute-start | bytes 7077896 | tf_op jit(solution)/shard_map/ppermute | solution.py:471
  217.9 23.5 %collective-permute-start.28 = (bf16[768,1536]{1,0:T(8,128)(2,1)}, bf16[768,1536]{1,0:T(8,128)(2,1)S(1)}, u32[]{:S(2)}, u32[]{:S(2)}) collective-permute-start(bf16[768,1536]{1,0:T(8,128)(2,1)} %get-tuple-element.86), channel_id=1, source_target_pairs={{0,1},{1,0},{2,3},{3,2},{4,5},{5,4},{6,7},{7,6},{8,9},{9,8},{10,11... | collective-permute-start | bytes 7077896 | tf_op jit(solution)/shard_map/ppermute | solution.py:471
  276.0 42.7 %collective-permute-start.31 = (bf16[2,264,768]{2,1,0:T(8,128)(2,1)}, bf16[2,264,768]{2,1,0:T(8,128)(2,1)S(1)}, u32[]{:S(2)}, u32[]{:S(2)}) collective-permute-start(bf16[2,264,768]{2,1,0:T(8,128)(2,1)} %get-tuple-element.93), channel_id=1, source_target_pairs={{0,1},{1,0},{2,3},{3,2},{4,5},{5,4},{6,7},{7,6},{8,9},{9,8},{10,11... | collective-permute-start | bytes 2433032 | tf_op jit(solution)/shard_map/ppermute | solution.py:471
  322.9 45.7 %collective-permute-start.37 = (bf16[264,768]{1,0:T(8,128)(2,1)}, bf16[264,768]{1,0:T(8,128)(2,1)}, u32[]{:S(2)}, u32[]{:S(2)}) collective-permute-start(bf16[264,768]{1,0:T(8,128)(2,1)} %fusion.13), channel_id=1, source_target_pairs={{0,2},{1,3},{2,0},{3,1},{4,6},{5,7},{6,4},{7,5},{8,10},{9,11},{10,... | collective-permute-start | bytes 1216520 | tf_op jit(solution)/shard_map/ppermute | solution.py:471
  365.2 15.4 %collective-permute-start.40 = (bf16[4,112,576]{2,1,0:T(8,128)(2,1)S(1)}, bf16[4,112,576]{2,1,0:T(8,128)(2,1)S(1)}, u32[]{:S(2)}, u32[]{:S(2)}) collective-permute-start(bf16[4,112,576]{2,1,0:T(8,128)(2,1)S(1)} %dynamic-slice_bitcast_fusion), channel_id=1, source_target_pairs={{0,4},{4,0},{8,12},{12,8},{16,20},{20,16},{24,28},{28,24},{1,5},{5... | collective-permute-start | bytes 1548296 | tf_op jit(solution)/shard_map/ppermute | solution.py:471
  367.1 14.7 %collective-permute-start.39 = (bf16[264,768]{1,0:T(8,128)(2,1)S(1)}, bf16[264,768]{1,0:T(8,128)(2,1)S(1)}, u32[]{:S(2)}, u32[]{:S(2)}) collective-permute-start(bf16[264,768]{1,0:T(8,128)(2,1)S(1)} %fusion.11), channel_id=1, source_target_pairs={{0,2},{1,3},{2,0},{3,1},{4,6},{5,7},{6,4},{7,5},{8,10},{9,11},{10,... | collective-permute-start | bytes 1216520 | tf_op jit(solution)/shard_map/ppermute | solution.py:471
  399.3 23.6 %collective-permute-start.47 = (bf16[96,3456]{1,0:T(8,128)(2,1)S(1)}, bf16[96,3456]{1,0:T(8,128)(2,1)S(1)}, u32[]{:S(2)}, u32[]{:S(2)}) collective-permute-start(bf16[96,3456]{1,0:T(8,128)(2,1)S(1)} %bitcast.141), channel_id=1, source_target_pairs={{0,2},{1,3},{2,0},{3,1},{4,6},{5,7},{6,4},{7,5},{8,10},{9,11},{10,... | collective-permute-start | bytes 1990664 | tf_op jit(solution)/shard_map/ppermute | solution.py:471
  (80 other events, 766.3 us)
Sparse Core Ops, SparseCore 0:
  49.7 64.3 all-gather.2
  249.1 108.6 reduce-scatter.1

commit v7 on v6

--- a/solution.py
+++ b/solution.py
@@ -156,7 +156,7 @@
             pltpu.VMEM((total, width), F32),
             pltpu.VMEM((total, heads * HEAD_DIM), F32),
         ],
-        compiler_params=pltpu.CompilerParams(vmem_limit_bytes=VMEM_BYTES),
+        compiler_params=pltpu.CompilerParams(vmem_limit_bytes=36 * 1024 * 1024),
         cost_estimate=cost(14),
         name="slot_forward",
     )(
@@ -720,10 +720,13 @@
     out_sum = half_of(grad_out_weight, 1, pair_me).astype(F32) + xor_send(
         half_of(grad_out_weight, 1, 1 - pair_me), "seq", 1
     ).astype(F32)
+    down_sum = down_sum.astype(BF16).reshape(n_img, -1, shard, model_width)
+    down_blocks = down_sum.shape[1]
     second_grads = jnp.concatenate(
-        [up_sum.astype(BF16), out_sum.astype(BF16), down_sum.astype(BF16).reshape(model_width, -1)],
-        axis=1,
-    ).reshape(n_img, shard, -1)
+        [part.astype(BF16).reshape(n_img, shard, -1) for part in (up_sum, out_sum)]
+        + [down_sum[:, p] for p in range(down_blocks)],
+        axis=2,
+    )
     own_second = scatter_img(second_grads)
 
     grad_columns = jnp.zeros((model_width, group), F32)
@@ -746,8 +749,11 @@
         norm_sums += slot_norm
         bias_sums += slot_bias[0]
         pairs = xor_send(pairs, "seq", 1)
-        across = xor_send((across + pairs[1].astype(F32)).astype(BF16), "seq", 2)
-        own_sums.append(own + pairs[0].astype(F32) + across.astype(F32))
+        across = (across + pairs[1].astype(F32)).astype(BF16)
+        own_sums.append(own + pairs[0].astype(F32))
+        if slot < slot_count - 1:
+            across = xor_send(across, "seq", 2)
+            own_sums[-1] = own_sums[-1] + across.astype(F32)
         arrivals.append((pairs, across))
     bias_sums = bias_sums.reshape(heads_here, 3, HEAD_DIM)
     grad_pairs = jnp.concatenate([bias_sums[:, :1], bias_sums[:, 2:]], axis=1).reshape(-1)
@@ -773,12 +779,15 @@
         extra.reshape(n_img, extra_rows, group), ((0, 0), (0, 16 - extra_rows), (0, 0))
     )
     columns = jnp.concatenate([grad_columns.reshape(n_img, shard, group), extra], axis=1)
-    columns = once_there(columns.astype(BF16), (arrivals[-2][0],))
+    columns = once_there(columns.astype(BF16), (own_second, arrivals[-2][0]))
     if few_devices():
-        own_columns = reduce_outer(once_there(reduce_inner(columns), (own_second, pairs)))
+        own_columns = reduce_outer(reduce_inner(columns))
     else:
         own_columns = scatter_img(columns)
     own_columns = own_columns.astype(BF16)
+
+    across = xor_send(once_there(arrivals[-1][1], (columns,)), "seq", 2)
+    own_sums[-1] = own_sums[-1] + once_there(across, (own_columns,)).astype(F32)
 
     grad_norm_first = jnp.concatenate(own_sums, axis=0)
     unit, factor = normalize(tokens.reshape(row_count, model_width).astype(F32))
@@ -804,8 +813,10 @@
     up_there = up_there.reshape(shard, n_img, 1, ff_half)
     share_up = in_pair_order(up_low, up_there, 2).reshape(shard, ff).astype(F32)
     share_out = in_pair_order(out_low, out_there, 1).astype(F32)
-    down_low = down_low.reshape(ff_half, model_width)
-    down_there = down_there.reshape(ff_half, model_width)
+    down_low, down_there = (
+        jnp.concatenate(jnp.split(part, down_blocks, axis=1), axis=0)
+        for part in (down_low, down_there)
+    )
     share_down = in_pair_order(down_low, down_there, 0).astype(F32)
 
     shares, at = [], 0

time: 447 us -> 425 us (0.951)
  waiting for transfers between devices: 82.7 us -> 73.9 us
  local copies, waits for them, and re-layouts: 71.1 us -> 65 us
  starting transfers between devices: 49.3 us -> 44.3 us
    unnamed x106 -> x168, local copies, waits for them, and re-layouts: 8.41 us -> 18.8 us
    ppermute x40, waiting for transfers between devices: 77.3 us -> 68.1 us  [xor_send(): return lax.ppermute(block, axis, [(i, i ^ bits) for i in range(n)])]
    concatenate x1 -> x0, local copies, waits for them, and re-layouts: 4.75 us -> none  [local(): jnp.concatenate([up_sum.astype(BF16), out_sum.astype(BF16), down_sum.asty...]
  transfers between devices with their start and end apart: 51 -> 51, of which waited for: 19 -> 16; matrix products, arithmetic and copies ran while one was open for 19% -> 17% of each run, Pallas kernels for 28% -> 29%
where the time goes in v7:
time: 425 us; the launch traced here: 418 us
  Pallas kernels  173 us (41%)
  waiting for transfers between devices  73.9 us (17%)
  local copies, waits for them, and re-layouts  65 us (15%)
  other arithmetic  45.6 us (11%)
  starting transfers between devices  44.3 us (10%)
  between operations  16.3 us (4%)
    pallas_call x3, Pallas kernels, slot_backward(): pl.pallas_call(partial(backward_kernel, n_seq, heads, len(after)), grid=(...  77.5 us
    ppermute x40, waiting for transfers between devices, xor_send(): return lax.ppermute(block, axis, [(i, i ^ bits) for i in range(n)])  68.1 us
    pallas_call x1, Pallas kernels, feed_forward(): pl.pallas_call(partial(mlp_kernel, slots, groups), grid=(ff // chunk,), i...  51.3 us
    pallas_call x3, Pallas kernels, slot_forward(): pl.pallas_call(partial(forward_kernel, n_seq, heads, len(after)), grid=(1...  44.2 us
    ppermute x40, starting transfers between devices, xor_send(): return lax.ppermute(block, axis, [(i, i ^ bits) for i in range(n)])  27.8 us
    unnamed x168, local copies, waits for them, and re-layouts  18.8 us
    ppermute x9, starting transfers between devices, outer_send(): lax.ppermute(block, 'img', [(z * INNER + y, (z + shift) % outer * INNER +...  16.4 us
  transfers between devices with their start and end apart: 51, of which 16 were waited for; matrix products, arithmetic and copies ran while one was open for 17% of the time, Pallas kernels for 29%

profile of v7, /device:TPU:0, one launch (start us, length us, event | category | flops | bytes accessed | tf_op | source)
XLA Modules:
  0.0 418.1 jit_solution(9006592338088599174)
XLA Ops:
  13.8 3.1 collective-permute-start.3
  35.0 15.1 %collective-permute-done.6 = bf16[4,112,576]{2,1,0:T(8,128)(2,1)} collective-permute-done((bf16[4,112,576]{2,1,0:T(8,128)(2,1)S(1)}, bf16[4,112,576]{2,1,0:T(8,128)(2,1)}, u32[]{:S(2)}, u32[]{:S(2)}) %collective-permute-start.6) | collective-permute-done | bytes 516128 | tf_op jit(solution)/shard_map/ppermute | solution.py:471
  57.8 3.3 collective-permute-start.20
  61.2 11.1 %slot_forward.3 = (bf16[1056,768]{1,0:T(8,128)(2,1)S(1)}, bf16[9,1152,128]{2,1,0:T(8,128)(2,1)S(1)}, bf16[264,192]{1,0:T(8,128)(2,1)S(1)}, bf16[264,192]{1,0:T(8...) custom-call(bf16[3,264,768]{2,1,0:T(8,128)(2,1)S(1)} %copy-done.2, ...), custom_call_target="tpu_custom_call" | custom-call | flops 14000000000 | bytes 10000000 | tf_op jit(solution)/shard_map/slot_forward/pallas_call | solution.py:146
  76.8 22.7 %slot_forward.4 = (bf16[1056,768]{1,0:T(8,128)(2,1)S(1)}, bf16[9,1152,128]{2,1,0:T(8,128)(2,1)S(1)}, bf16[264,192]{1,0:T(8,128)(2,1)S(1)}, bf16[264,192]{1,0:T(8...) custom-call(bf16[3,264,768]{2,1,0:T(8,128)(2,1)S(1)} %copy-done.2, ...), custom_call_target="tpu_custom_call" | custom-call | flops 14000000000 | bytes 10000000 | tf_op jit(solution)/shard_map/slot_forward/pallas_call | solution.py:146
  113.4 10.4 %slot_forward.5 = (bf16[1056,768]{1,0:T(8,128)(2,1)S(1)}, bf16[9,1152,128]{2,1,0:T(8,128)(2,1)S(1)}, bf16[264,192]{1,0:T(8,128)(2,1)S(1)}, bf16[264,192]{1,0:T(8...) custom-call(bf16[3,264,768]{2,1,0:T(8,128)(2,1)S(1)} %copy-done.2, ...), custom_call_target="tpu_custom_call" | custom-call | flops 14000000000 | bytes 10000000 | tf_op jit(solution)/shard_map/slot_forward/pallas_call | solution.py:146
  135.8 3.7 collective-permute-done.14.refs_5_.refs_7_
  141.6 3.7 collective-permute-done.21.refs_0_
  158.3 51.3 %feed_forward.1 = (bf16[3,264,768]{2,1,0:T(8,128)(2,1)}, f32[3,264,768]{2,1,0:T(8,128)}, bf16[264,192]{1,0:T(8,128)(2,1)}, bf16[264,192]{1,0:T(8,128)(2,1)}, bf1...) custom-call(bf16[264,192]{1,0:T(8,128)(2,1)} %copy-done.31, ...), custom_call_target="tpu_custom_call" | custom-call | flops 54999998464 | bytes 10000000 | tf_op jit(solution)/shard_map/feed_forward/pallas_call | solution.py:407
  214.0 3.8 collective-permute-done.29
  219.2 4.1 collective-permute-done.27.refs_3_
  224.0 3.0 add_convert_fusion
  229.9 3.1 add_convert_fusion.1
  233.1 2.9 pad_maximum_fusion.refs_4_
  237.5 25.7 %slot_backward.3 = (f32[264,768]{1,0:T(8,128)}, f32[264,768]{1,0:T(8,128)}, bf16[2,264,768]{2,1,0:T(8,128)(2,1)}, f32[768,576]{1,0:T(8,128)}, f32[8,768]{1,0:T(8,128)}, /*index=5*/f32[8,576]{1,0:T(8,128)}) custom-call(bf16[264,192]{1,0:T(8,128)(2,1)} %get-tuple-element.81.refs_0_, bf16[264,192]{1,0:T(8,128)(2,1)} %copy-done.49, bf16[264,192]{1,0:T(8,128)(2,1)} %copy-done.50, ...), custom_call_target="tpu_custom_call" | custom-call | bytes 10000000 | tf_op jit(solution)/shard_map/slot_backward/pallas_call | solution.py:244
  266.1 7.3 %collective-permute-done.34.refs_2_ = bf16[2,264,192]{2,1,0:T(8,128)(2,1)S(1)} collective-permute-done((bf16[2,264,192]{2,1,0:T(8,128)(2,1)S(1)}, bf16[2,264,192]{2,1,0:T(8,128)(2,1)S(1)}, u32[]{:S(2)}, u32[]{:S(2)}) %collective-permute-start.34) | collective-permute-done | bytes 202784 | tf_op jit(solution)/shard_map/ppermute | solution.py:471
  273.4 4.2 %collective-permute-done.35.refs_3_ = bf16[2,264,192]{2,1,0:T(8,128)(2,1)S(1)} collective-permute-done((bf16[2,264,192]{2,1,0:T(8,128)(2,1)S(1)}, bf16[2,264,192]{2,1,0:T(8,128)(2,1)S(1)}, u32[]{:S(2)}, u32[]{:S(2)}) %collective-permute-start.35) | collective-permute-done | bytes 202784 | tf_op jit(solution)/shard_map/ppermute | solution.py:471
  278.3 26.1 %slot_backward.4 = (f32[264,768]{1,0:T(8,128)}, f32[264,768]{1,0:T(8,128)}, bf16[2,264,768]{2,1,0:T(8,128)(2,1)}, f32[768,576]{1,0:T(8,128)}, f32[8,768]{1,0:T(8,128)}, /*index=5*/f32[8,576]{1,0:T(8,128)}) custom-call(bf16[2,264,192]{2,1,0:T(8,128)(2,1)} %get-tuple-element.95.refs_0_, bf16[2,264,192]{2,1,0:T(8,128)(2,1)} %copy-done.52, ...), custom_call_target="tpu_custom_call" | custom-call | bytes 10000000 | tf_op jit(solution)/shard_map/slot_backward/pallas_call | solution.py:244
  310.6 8.7 %collective-permute-done.32.refs_4_ = bf16[264,768]{1,0:T(8,128)(2,1)S(1)} collective-permute-done((bf16[264,768]{1,0:T(8,128)(2,1)S(1)}, bf16[264,768]{1,0:T(8,128)(2,1)S(1)}, u32[]{:S(2)}, u32[]{:S(2)}) %collective-permute-start.32) | collective-permute-done | bytes 405536 | tf_op jit(solution)/shard_map/ppermute | solution.py:471
  320.1 25.7 %slot_backward.5 = (f32[264,768]{1,0:T(8,128)}, f32[264,768]{1,0:T(8,128)}, bf16[2,264,768]{2,1,0:T(8,128)(2,1)}, f32[768,576]{1,0:T(8,128)}, f32[8,768]{1,0:T(8,128)}, /*index=5*/f32[8,576]{1,0:T(8,128)}) custom-call(bf16[2,264,192]{2,1,0:T(8,128)(2,1)} %get-tuple-element.95.refs_0_, bf16[2,264,192]{2,1,0:T(8,128)(2,1)} %copy-done.52, ...), custom_call_target="tpu_custom_call" | custom-call | bytes 10000000 | tf_op jit(solution)/shard_map/slot_backward/pallas_call | solution.py:244
  361.5 9.7 %collective-permute-done.40 = bf16[4,112,576]{2,1,0:T(8,128)(2,1)} collective-permute-done((bf16[4,112,576]{2,1,0:T(8,128)(2,1)}, bf16[4,112,576]{2,1,0:T(8,128)(2,1)}, u32[]{:S(2)}, u32[]{:S(2)}) %collective-permute-start.40) | collective-permute-done | bytes 516128 | tf_op jit(solution)/shard_map/ppermute | solution.py:471
  374.6 3.1 collective-permute-start.43
  381.0 4.9 %collective-permute-done.42 = bf16[112,576]{1,0:T(8,128)(2,1)S(1)} collective-permute-done((bf16[112,576]{1,0:T(8,128)(2,1)S(1)}, bf16[112,576]{1,0:T(8,128)(2,1)S(1)}, u32[]{:S(2)}, u32[]{:S(2)}) %collective-permute-start.42) | collective-permute-done | bytes 129056 | tf_op jit(solution)/shard_map/ppermute | solution.py:479
  394.4 3.3 fusion.7
  (424 shorter events, 142.1 us)
Async XLA Ops:
  7.2 142.0 %all-gather.3.cloned.1.call-start = ((), (), s32[]{:S(2)}) async-start(), calls=%async_computation.2 | async-start | bytes 2654208 | tf_op jit(solution)/shard_map/all_gather | solution.py:626
  13.8 17.4 %collective-permute-start.3 = (bf16[112,576]{1,0:T(8,128)(2,1)S(1)}, bf16[112,576]{1,0:T(8,128)(2,1)S(1)}, u32[]{:S(2)}, u32[]{:S(2)}) collective-permute-start(bf16[112,576]{1,0:T(8,128)(2,1)S(1)} %concatenate.77), channel_id=1, source_target_pairs={{0,8},{4,12},{8,16},{12,20},{16,24},{20,28},{24,0},{28,4},{1,9},{5... | collective-permute-start | bytes 387080 | tf_op jit(solution)/shard_map/ppermute | solution.py:479
  16.9 14.9 %collective-permute-start.4 = (bf16[112,576]{1,0:T(8,128)(2,1)S(1)}, bf16[112,576]{1,0:T(8,128)(2,1)S(1)}, u32[]{:S(2)}, u32[]{:S(2)}) collective-permute-start(bf16[112,576]{1,0:T(8,128)(2,1)S(1)} %concatenate.77), channel_id=1, source_target_pairs={{0,16},{4,20},{8,24},{12,28},{16,0},{20,4},{24,8},{28,12},{1,17},{... | collective-permute-start | bytes 387080 | tf_op jit(solution)/shard_map/ppermute | solution.py:479
  20.8 40.3 %collective-permute-start = (bf16[3,264,768]{2,1,0:T(8,128)(2,1)}, bf16[3,264,768]{2,1,0:T(8,128)(2,1)}, u32[]{:S(2)}, u32[]{:S(2)}) collective-permute-start(bf16[3,264,768]{2,1,0:T(8,128)(2,1)} %refs_5_.3), channel_id=1, source_target_pairs={{0,1},{1,0},{2,3},{3,2},{4,5},{5,4},{6,7},{7,6},{8,9},{9,8},{10,11... | collective-permute-start | bytes 3649544 | tf_op jit(solution)/shard_map/ppermute | solution.py:471
  31.2 29.9 %collective-permute-start.7 = (bf16[2,264,768]{2,1,0:T(8,128)(2,1)}, bf16[2,264,768]{2,1,0:T(8,128)(2,1)}, u32[]{:S(2)}, u32[]{:S(2)}) collective-permute-start(bf16[2,264,768]{2,1,0:T(8,128)(2,1)} %slice.199), channel_id=1, source_target_pairs={{0,2},{1,3},{2,0},{3,1},{4,6},{5,7},{6,4},{7,5},{8,10},{9,11},{10,... | collective-permute-start | bytes 2433032 | tf_op jit(solution)/shard_map/ppermute | solution.py:471
  31.9 18.2 %collective-permute-start.6 = (bf16[4,112,576]{2,1,0:T(8,128)(2,1)S(1)}, bf16[4,112,576]{2,1,0:T(8,128)(2,1)}, u32[]{:S(2)}, u32[]{:S(2)}) collective-permute-start(bf16[4,112,576]{2,1,0:T(8,128)(2,1)S(1)} %bitcast_dynamic-update-slice_fusion.4), channel_id=1, source_target_pairs={{0,4},{4,0},{8,12},{12,8},{16,20},{20,16},{24,28},{28,24},{1,5},{5... | collective-permute-start | bytes 1548296 | tf_op jit(solution)/shard_map/ppermute | solution.py:471
  33.9 317.2 %reduce-scatter.2.cloned.1.call-start = ((), (), s32[]{:S(2)}) async-start(), calls=%async_computation.1 | async-start | bytes 5971968 | tf_op jit(solution)/shard_map/reduce_scatter | solution.py:543
  35.0 22.8 %collective-permute-start.2 = (bf16[264,768]{1,0:T(8,128)(2,1)}, bf16[264,768]{1,0:T(8,128)(2,1)S(1)}, u32[]{:S(2)}, u32[]{:S(2)}) collective-permute-start(bf16[264,768]{1,0:T(8,128)(2,1)} %collective-permute-done.1.refs_2_.refs_7_), channel_id=1, source_target_pairs={{0,1},{1,0},{2,3},{3,2},{4,5},{5,4},{6,7},{7,6},{8,9},{9,8},{10,11... | collective-permute-start | bytes 1216520 | tf_op jit(solution)/shard_map/ppermute | solution.py:471
  52.8 52.1 %collective-permute-start.18 = (bf16[96,1920]{1,0:T(8,128)(2,1)}, bf16[96,1920]{1,0:T(8,128)(2,1)}, u32[]{:S(2)}, u32[]{:S(2)}) collective-permute-start(bf16[96,1920]{1,0:T(8,128)(2,1)} %once_there.12), channel_id=1, source_target_pairs={{0,8},{4,12},{8,16},{12,20},{16,24},{20,28},{24,0},{28,4},{1,9},{5... | collective-permute-start | bytes 1105928 | tf_op jit(solution)/shard_map/ppermute | solution.py:479
  53.6 51.5 %collective-permute-start.19 = (bf16[96,1920]{1,0:T(8,128)(2,1)}, bf16[96,1920]{1,0:T(8,128)(2,1)}, u32[]{:S(2)}, u32[]{:S(2)}) collective-permute-start(bf16[96,1920]{1,0:T(8,128)(2,1)} %once_there.12), channel_id=1, source_target_pairs={{0,16},{4,20},{8,24},{12,28},{16,0},{20,4},{24,8},{28,12},{1,17},{... | collective-permute-start | bytes 1105928 | tf_op jit(solution)/shard_map/ppermute | solution.py:479
  57.8 47.4 %collective-permute-start.20 = (bf16[96,1920]{1,0:T(8,128)(2,1)}, bf16[96,1920]{1,0:T(8,128)(2,1)}, u32[]{:S(2)}, u32[]{:S(2)}) collective-permute-start(bf16[96,1920]{1,0:T(8,128)(2,1)} %once_there.12), channel_id=1, source_target_pairs={{0,24},{4,28},{8,0},{12,4},{16,8},{20,12},{24,16},{28,20},{1,25},{... | collective-permute-start | bytes 1105928 | tf_op jit(solution)/shard_map/ppermute | solution.py:479
  61.1 15.3 %collective-permute-start.8 = (bf16[2,264,768]{2,1,0:T(8,128)(2,1)}, bf16[2,264,768]{2,1,0:T(8,128)(2,1)S(1)}, u32[]{:S(2)}, u32[]{:S(2)}) collective-permute-start(bf16[2,264,768]{2,1,0:T(8,128)(2,1)} %collective-permute-done.7.refs_2_.refs_6_.refs_7_), channel_id=1, source_target_pairs={{0,1},{1,0},{2,3},{3,2},{4,5},{5,4},{6,7},{7,6},{8,9},{9,8},{10,11... | collective-permute-start | bytes 2433032 | tf_op jit(solution)/shard_map/ppermute | solution.py:471
  75.0 37.1 %collective-permute-start.10 = (bf16[264,192]{1,0:T(8,128)(2,1)}, bf16[264,192]{1,0:T(8,128)(2,1)S(1)}, u32[]{:S(2)}, u32[]{:S(2)}) collective-permute-start(bf16[264,192]{1,0:T(8,128)(2,1)} %get-tuple-element.70), channel_id=1, source_target_pairs={{0,2},{1,3},{2,0},{3,1},{4,6},{5,7},{6,4},{7,5},{8,10},{9,11},{10,... | collective-permute-start | bytes 304136 | tf_op jit(solution)/shard_map/ppermute | solution.py:471
  76.5 35.6 %collective-permute-start.11 = (bf16[264,192]{1,0:T(8,128)(2,1)}, bf16[264,192]{1,0:T(8,128)(2,1)S(1)}, u32[]{:S(2)}, u32[]{:S(2)}) collective-permute-start(bf16[264,192]{1,0:T(8,128)(2,1)} %get-tuple-element.71), channel_id=1, source_target_pairs={{0,3},{1,2},{2,1},{3,0},{4,7},{5,6},{6,5},{7,4},{8,11},{9,10},{10,... | collective-permute-start | bytes 304136 | tf_op jit(solution)/shard_map/ppermute | solution.py:471
  110.6 34.7 %collective-permute-start.21 = (bf16[4,96,1920]{2,1,0:T(8,128)(2,1)}, bf16[4,96,1920]{2,1,0:T(8,128)(2,1)}, u32[]{:S(2)}, u32[]{:S(2)}) collective-permute-start(bf16[4,96,1920]{2,1,0:T(8,128)(2,1)} %bitcast_dynamic-update-slice_fusion), channel_id=1, source_target_pairs={{0,4},{4,0},{8,12},{12,8},{16,20},{20,16},{24,28},{28,24},{1,5},{5... | collective-permute-start | bytes 4423688 | tf_op jit(solution)/shard_map/ppermute | solution.py:471
  209.5 13.8 %collective-permute-start.30 = (bf16[1536,768]{1,0:T(8,128)(2,1)}, bf16[1536,768]{1,0:T(8,128)(2,1)}, u32[]{:S(2)}, u32[]{:S(2)}) collective-permute-start(bf16[1536,768]{1,0:T(8,128)(2,1)} %get-tuple-element.89), channel_id=1, source_target_pairs={{0,1},{1,0},{2,3},{3,2},{4,5},{5,4},{6,7},{7,6},{8,9},{9,8},{10,11... | collective-permute-start | bytes 7077896 | tf_op jit(solution)/shard_map/ppermute | solution.py:471
  209.7 18.8 %collective-permute-start.28 = (bf16[768,1536]{1,0:T(8,128)(2,1)}, bf16[768,1536]{1,0:T(8,128)(2,1)S(1)}, u32[]{:S(2)}, u32[]{:S(2)}) collective-permute-start(bf16[768,1536]{1,0:T(8,128)(2,1)} %get-tuple-element.86), channel_id=1, source_target_pairs={{0,1},{1,0},{2,3},{3,2},{4,5},{5,4},{6,7},{7,6},{8,9},{9,8},{10,11... | collective-permute-start | bytes 7077896 | tf_op jit(solution)/shard_map/ppermute | solution.py:471
  263.1 42.6 %collective-permute-start.31 = (bf16[2,264,768]{2,1,0:T(8,128)(2,1)}, bf16[2,264,768]{2,1,0:T(8,128)(2,1)S(1)}, u32[]{:S(2)}, u32[]{:S(2)}) collective-permute-start(bf16[2,264,768]{2,1,0:T(8,128)(2,1)} %get-tuple-element.93), channel_id=1, source_target_pairs={{0,1},{1,0},{2,3},{3,2},{4,5},{5,4},{6,7},{7,6},{8,9},{9,8},{10,11... | collective-permute-start | bytes 2433032 | tf_op jit(solution)/shard_map/ppermute | solution.py:471
  310.1 67.6 %collective-permute-start.37 = (bf16[264,768]{1,0:T(8,128)(2,1)}, bf16[264,768]{1,0:T(8,128)(2,1)}, u32[]{:S(2)}, u32[]{:S(2)}) collective-permute-start(bf16[264,768]{1,0:T(8,128)(2,1)} %fusion.13), channel_id=1, source_target_pairs={{0,2},{1,3},{2,0},{3,1},{4,6},{5,7},{6,4},{7,5},{8,10},{9,11},{10,... | collective-permute-start | bytes 1216520 | tf_op jit(solution)/shard_map/ppermute | solution.py:471
  355.4 15.7 %collective-permute-start.40 = (bf16[4,112,576]{2,1,0:T(8,128)(2,1)}, bf16[4,112,576]{2,1,0:T(8,128)(2,1)}, u32[]{:S(2)}, u32[]{:S(2)}) collective-permute-start(bf16[4,112,576]{2,1,0:T(8,128)(2,1)} %dynamic-slice_bitcast_fusion), channel_id=1, source_target_pairs={{0,4},{4,0},{8,12},{12,8},{16,20},{20,16},{24,28},{28,24},{1,5},{5... | collective-permute-start | bytes 1548296 | tf_op jit(solution)/shard_map/ppermute | solution.py:471
  360.0 27.9 %collective-permute-start.39 = (bf16[264,768]{1,0:T(8,128)(2,1)}, bf16[264,768]{1,0:T(8,128)(2,1)S(1)}, u32[]{:S(2)}, u32[]{:S(2)}) collective-permute-start(bf16[264,768]{1,0:T(8,128)(2,1)} %once_there.22), channel_id=1, source_target_pairs={{0,2},{1,3},{2,0},{3,1},{4,6},{5,7},{6,4},{7,5},{8,10},{9,11},{10,... | collective-permute-start | bytes 1216520 | tf_op jit(solution)/shard_map/ppermute | solution.py:471
  378.9 18.7 %collective-permute-start.47 = (bf16[96,3456]{1,0:T(8,128)(2,1)}, bf16[96,3456]{1,0:T(8,128)(2,1)}, u32[]{:S(2)}, u32[]{:S(2)}) collective-permute-start(bf16[96,3456]{1,0:T(8,128)(2,1)} %bitcast.43), channel_id=1, source_target_pairs={{0,2},{1,3},{2,0},{3,1},{4,6},{5,7},{6,4},{7,5},{8,10},{9,11},{10,... | collective-permute-start | bytes 1990664 | tf_op jit(solution)/shard_map/ppermute | solution.py:471
  386.0 14.0 %collective-permute-start.44 = (bf16[112,576]{1,0:T(8,128)(2,1)S(1)}, bf16[112,576]{1,0:T(8,128)(2,1)}, u32[]{:S(2)}, u32[]{:S(2)}) collective-permute-start(bf16[112,576]{1,0:T(8,128)(2,1)S(1)} %fusion.21.refs_1_), channel_id=1, source_target_pairs={{0,1},{1,0},{2,3},{3,2},{4,5},{5,4},{6,7},{7,6},{8,9},{9,8},{10,11... | collective-permute-start | bytes 387080 | tf_op jit(solution)/shard_map/ppermute | solution.py:471
  386.0 13.9 %collective-permute-start.45 = (bf16[112,576]{1,0:T(8,128)(2,1)S(1)}, bf16[112,576]{1,0:T(8,128)(2,1)}, u32[]{:S(2)}, u32[]{:S(2)}) collective-permute-start(bf16[112,576]{1,0:T(8,128)(2,1)S(1)} %fusion.21.refs_1_), channel_id=1, source_target_pairs={{0,2},{1,3},{2,0},{3,1},{4,6},{5,7},{6,4},{7,5},{8,10},{9,11},{10,... | collective-permute-start | bytes 387080 | tf_op jit(solution)/shard_map/ppermute | solution.py:471
  (111 other events, 986.9 us)
Sparse Core Ops, SparseCore 0:
  34.1 70.7 all-gather.2
  236.1 103.8 reduce-scatter.1
